TPU v7x, 32 devices: a whole 2x2x4 slice. The times are simulated.
32 devices in a mesh: rows: 2 (over core), imgs: 16 (over z, y, x).
Axes of the slice: x: 2, y: 2, z: 4, core: 2. Of those that a mesh axis runs over, the one named last changes fastest.
Arguments:
- inputs: bfloat16 [256, 22, 18, 320], P('imgs', 'rows')
- cotangent: bfloat16 [256, 22, 18, 320], P('imgs', 'rows')
- scales: float32 [4, 320], replicated, may hold values from 0.25 to 1.75
- shifts: float32 [8, 320], replicated, may hold values from -3 to 3
- hidden_shift: float32 [2, 1280], replicated, may hold values from -3 to 3
- w_inward: bfloat16 [320, 320], replicated, may hold values from -0.3125 to 0.3125
- w_gating: bfloat16 [320, 320], replicated, may hold values from -0.3125 to 0.3125
- w_outward: bfloat16 [320, 320], replicated, may hold values from -0.3125 to 0.3125
- w_expand: bfloat16 [320, 1280], replicated, may hold values from -0.3125 to 0.3125
- w_reduce: bfloat16 [1280, 320], replicated, may hold values from -0.15625 to 0.15625
- kernel_local: float32 [25, 320], replicated, may hold values from -1.25 to 1.25
- kernel_dilated: float32 [49, 320], replicated, may hold values from -0.875 to 0.875
- kernel_hidden: float32 [9, 1280], replicated, may hold values from -2 to 2
- image_size: int32 [256], replicated, may hold values from 14 to 18, as said below
- band_split: int32 [256], replicated, may hold values from 5 to 11, as said below
- slot_image: int32 [256], P('imgs'), may hold values from 0 to 255, each once
Outputs:
- result: float32 [256, 22, 18, 320], P('imgs', 'rows')
- input_grad: float32 [256, 22, 18, 320], P('imgs', 'rows')
- scales_grad: float32 [4, 320], replicated
- shifts_grad: float32 [8, 320], replicated
- hidden_shift_grad: float32 [2, 1280], replicated
- w_inward_grad: float32 [320, 320], replicated
- w_gating_grad: float32 [320, 320], replicated
- w_outward_grad: float32 [320, 320], replicated
- w_expand_grad: float32 [320, 1280], replicated
- w_reduce_grad: float32 [1280, 320], replicated
- kernel_local_grad: float32 [25, 320], replicated
- kernel_dilated_grad: float32 [49, 320], replicated
- kernel_hidden_grad: float32 [9, 1280], replicated
Inputs may be any that keep to these rules, and one draw needn't show every extreme that they name: `image_size`: side of each square image in pixels: 14, 16 or 18. `band_split`: an image of side n has from n / 2 - 2 to n / 2 + 2 of its rows in the first band. `slot_image`: each image stands in exactly one slot.
All inputs are finite; a program needn't handle non-finite values.
Results may differ from a plain program's by a relative error of at most 0.003.
Values may be sent and summed in bfloat16 or wider, within the bound.
A program may use at most 320 MiB of HBM per device.

v0:
```python
import jax
import jax.numpy as jnp
from jax import lax
from jax.sharding import PartitionSpec as P

epsilon = 1e-05


def padded_2(x, sides, width):
    for axis, dim in sides:
        size, length = (lax.axis_size(axis), x.shape[dim])
        up = [(i, (i + 1) % size) for i in range(size - 1)]
        down = [(j, i) for i, j in up]
        last = lax.slice_in_dim(x, length - width, length, axis=dim)
        initial = lax.slice_in_dim(x, 0, width, axis=dim)
        before = lax.ppermute(last, axis, up)
        after = lax.ppermute(initial, axis, down)
        x = jnp.concatenate([before, x, after], axis=dim)
    return x


def smooth(values):
    return jax.nn.gelu(values, approximate=False)


def matmul(values, weight):
    return jnp.einsum("irwk,kn->irwn", values, weight, preferred_element_type=jnp.float32)


def weight_grad(values, gradient):
    return jnp.einsum("irwk,irwn->kn", values, gradient, preferred_element_type=jnp.float32)


def back_matmul(gradient, weight):
    return jnp.einsum("irwn,kn->irwk", gradient, weight, preferred_element_type=jnp.float32)


def pixel_sum(values):
    return jnp.sum(values.astype(jnp.float32), axis=(0, 1, 2))


def keep_inside(values, inside):
    return jnp.where(inside > 0, values, jnp.zeros_like(values))


def column_padded(extended, margin):
    return jnp.pad(extended.astype(jnp.float32), ((0, 0), (0, 0), (margin, margin), (0, 0)))


def depthwise(extended, kernel, extent, dilation, out_rows):
    margin = extent // 2 * dilation
    columns = extended.shape[2]
    padded = column_padded(extended, margin)
    summed = jnp.zeros((extended.shape[0], out_rows, columns, extended.shape[3]), jnp.float32)
    for row_tap in range(extent):
        for col_tap in range(extent):
            window = padded[
                :,
                row_tap * dilation : row_tap * dilation + out_rows,
                col_tap * dilation : col_tap * dilation + columns,
                :,
            ]
            summed = summed + kernel[row_tap * extent + col_tap] * window
    return summed


def kernel_grad(extended, gradient, extent, dilation):
    margin = extent // 2 * dilation
    out_rows = gradient.shape[1]
    columns = gradient.shape[2]
    padded = column_padded(extended, margin)
    gradient_f = gradient.astype(jnp.float32)
    tap_sums = []
    for row_tap in range(extent):
        for col_tap in range(extent):
            window = padded[
                :,
                row_tap * dilation : row_tap * dilation + out_rows,
                col_tap * dilation : col_tap * dilation + columns,
                :,
            ]
            tap_sums.append(jnp.sum(gradient_f * window, axis=(0, 1, 2)))
    return jnp.stack(tap_sums)


def slot_masks(image_size, band_split, slot_image, first_row, count_rows, band_rows, columns):
    everyone = jnp.arange(image_size.shape[0], dtype=jnp.int32)
    chosen = (slot_image[:, None] == everyone[None, :]).astype(jnp.int32)
    extent = jnp.sum(chosen * image_size[None, :], axis=1)
    top_row = band_rows - jnp.sum(chosen * band_split[None, :], axis=1)
    row_index = first_row + jnp.arange(count_rows, dtype=jnp.int32)
    col_index = jnp.arange(columns, dtype=jnp.int32)
    row_inside = (row_index[None, :] >= top_row[:, None]) & (
        row_index[None, :] < (top_row + extent)[:, None]
    )
    col_inside = col_index[None, :] < extent[:, None]
    return (row_inside[:, :, None] & col_inside[:, None, :]).astype(jnp.float32)[:, :, :, None]


def on_device(
    inputs,
    cotangent,
    scales,
    shifts,
    hidden_shift,
    w_inward,
    w_gating,
    w_outward,
    w_expand,
    w_reduce,
    kernel_local,
    kernel_dilated,
    kernel_hidden,
    image_size,
    band_split,
    slot_image,
):
    band_rows = inputs.shape[1]
    columns = inputs.shape[2]
    start_row = lax.axis_index("rows") * band_rows
    counted = jnp.sum(image_size * image_size).astype(jnp.float32)
    inside = slot_masks(
        image_size, band_split, slot_image, start_row, band_rows, band_rows, columns
    )
    masked_in = inside * inputs.astype(jnp.float32)
    first_sums = lax.psum(
        (pixel_sum(masked_in), pixel_sum(masked_in * masked_in)), ("rows", "imgs")
    )
    mean_one = first_sums[0] / counted
    rstd_one = lax.rsqrt(first_sums[1] / counted - mean_one * mean_one + epsilon)
    scale_one = rstd_one * scales[0]
    normed_one = ((masked_in - mean_one) * scale_one + shifts[0]).astype(jnp.bfloat16)
    pre_gelu = matmul(normed_one, w_inward) + shifts[1]
    gelu_out = smooth(pre_gelu).astype(jnp.bfloat16)
    gelu_masked = keep_inside(gelu_out, inside)
    near_margin = padded_2(gelu_masked, (("rows", 1),), 2)
    conv_one = (depthwise(near_margin, kernel_local, 5, 1, band_rows) + shifts[2]).astype(
        jnp.bfloat16
    )
    dilated_margin = padded_2(keep_inside(conv_one, inside), (("rows", 1),), 9)
    conv_two = (depthwise(dilated_margin, kernel_dilated, 7, 3, band_rows) + shifts[3]).astype(
        jnp.bfloat16
    )
    gate_pre = matmul(conv_two, w_gating) + shifts[4]
    gelu_f = gelu_out.astype(jnp.float32)
    gated = (gelu_f * gate_pre).astype(jnp.bfloat16)
    branch = matmul(gated, w_outward) + shifts[5]
    normed_f = normed_one.astype(jnp.float32)
    middle = masked_in + scales[1] * (branch + normed_f)
    middle_masked = inside * middle
    second_sums = lax.psum(
        (pixel_sum(middle_masked), pixel_sum(middle_masked * middle_masked)), ("rows", "imgs")
    )
    mean_two = second_sums[0] / counted
    rstd_two = lax.rsqrt(second_sums[1] / counted - mean_two * mean_two + epsilon)
    scale_two = rstd_two * scales[2]
    normed_two = ((middle - mean_two) * scale_two + shifts[6]).astype(jnp.bfloat16)
    expanded = (matmul(normed_two, w_expand) + hidden_shift[0]).astype(jnp.bfloat16)
    hidden_margin = padded_2(keep_inside(expanded, inside), (("rows", 1),), 1)
    hidden_conv = depthwise(hidden_margin, kernel_hidden, 3, 1, band_rows) + hidden_shift[1]
    hidden_act = smooth(hidden_conv).astype(jnp.bfloat16)
    reduced = matmul(hidden_act, w_reduce) + shifts[7]
    result = inside * (middle + scales[3] * reduced)
    grad_out = inside * cotangent.astype(jnp.float32)
    grad_reduced = (scales[3] * grad_out).astype(jnp.bfloat16)
    gain_four = pixel_sum(grad_out * reduced)
    bias_reduce = pixel_sum(grad_reduced)
    grad_w_reduce = weight_grad(hidden_act, grad_reduced)
    grad_act = back_matmul(grad_reduced, w_reduce)
    slope_hidden = jax.vjp(smooth, hidden_conv)[1]
    grad_conv = slope_hidden(grad_act)[0].astype(jnp.bfloat16)
    bias_conv = pixel_sum(grad_conv)
    grad_k_hidden = kernel_grad(hidden_margin, grad_conv, 3, 1)
    conv_margin = padded_2(grad_conv, (("rows", 1),), 1)
    grad_expanded = (inside * depthwise(conv_margin, kernel_hidden[::-1], 3, 1, band_rows)).astype(
        jnp.bfloat16
    )
    bias_expand = pixel_sum(grad_expanded)
    grad_w_expand = weight_grad(normed_two, grad_expanded)
    grad_normed_two = back_matmul(grad_expanded, w_expand)
    hat_two = (middle - mean_two) * rstd_two
    back_two = lax.psum(
        (pixel_sum(grad_normed_two), pixel_sum(grad_normed_two * hat_two)), ("rows", "imgs")
    )
    grad_middle = grad_out + scale_two * (
        grad_normed_two - inside * (back_two[0] / counted + hat_two * back_two[1] / counted)
    )
    grad_branch = (scales[1] * grad_middle).astype(jnp.bfloat16)
    gain_two = pixel_sum(grad_middle * (branch + normed_f))
    bias_branch = pixel_sum(grad_branch)
    grad_w_outward = weight_grad(gated, grad_branch)
    grad_gated = back_matmul(grad_branch, w_outward)
    grad_gate = (grad_gated * gelu_f).astype(jnp.bfloat16)
    bias_gate = pixel_sum(grad_gate)
    grad_w_gating = weight_grad(conv_two, grad_gate)
    grad_conv_two = back_matmul(grad_gate, w_gating).astype(jnp.bfloat16)
    bias_dilated = pixel_sum(grad_conv_two)
    grad_k_dilated = kernel_grad(dilated_margin, grad_conv_two, 7, 3)
    dilated_grad_margin = padded_2(grad_conv_two, (("rows", 1),), 9)
    grad_conv_one = (
        inside * depthwise(dilated_grad_margin, kernel_dilated[::-1], 7, 3, band_rows)
    ).astype(jnp.bfloat16)
    bias_local = pixel_sum(grad_conv_one)
    grad_k_local = kernel_grad(near_margin, grad_conv_one, 5, 1)
    local_grad_margin = padded_2(grad_conv_one, (("rows", 1),), 2)
    grad_gelu = grad_gated * gate_pre + inside * depthwise(
        local_grad_margin, kernel_local[::-1], 5, 1, band_rows
    )
    slope_first = jax.vjp(smooth, pre_gelu)[1]
    grad_pre = slope_first(grad_gelu)[0].astype(jnp.bfloat16)
    bias_inward = pixel_sum(grad_pre)
    grad_w_inward = weight_grad(normed_one, grad_pre)
    grad_normed_one = back_matmul(grad_pre, w_inward) + scales[1] * grad_middle
    hat_one = (masked_in - mean_one) * rstd_one
    back_one = lax.psum(
        (pixel_sum(grad_normed_one), pixel_sum(grad_normed_one * hat_one)), ("rows", "imgs")
    )
    input_grad = inside * (
        grad_middle
        + scale_one * (grad_normed_one - (back_one[0] / counted + hat_one * back_one[1] / counted))
    )
    summed_all = lax.psum(
        (
            gain_four,
            bias_reduce,
            bias_expand,
            bias_conv,
            grad_w_expand,
            grad_w_reduce,
            grad_k_hidden,
            gain_two,
            bias_inward,
            bias_local,
            bias_dilated,
            bias_gate,
            bias_branch,
            grad_w_inward,
            grad_w_gating,
            grad_w_outward,
            grad_k_local,
            grad_k_dilated,
        ),
        ("rows", "imgs"),
    )
    hidden_done = summed_all[:7]
    mixer_done = summed_all[7:]
    scales_grad = jnp.stack([back_one[1], mixer_done[0], back_two[1], hidden_done[0]])
    shifts_grad = jnp.stack(
        [
            back_one[0],
            mixer_done[1],
            mixer_done[2],
            mixer_done[3],
            mixer_done[4],
            mixer_done[5],
            back_two[0],
            hidden_done[1],
        ]
    )
    hidden_shift_grad = jnp.stack([hidden_done[2], hidden_done[3]])
    return (
        result,
        input_grad,
        scales_grad,
        shifts_grad,
        hidden_shift_grad,
        mixer_done[6],
        mixer_done[7],
        mixer_done[8],
        hidden_done[4],
        hidden_done[5],
        mixer_done[9],
        mixer_done[10],
        hidden_done[6],
    )


def solution(mesh):
    in_specs = (
        P("imgs", "rows", None, None),
        P("imgs", "rows", None, None),
        P(),
        P(),
        P(),
        P(),
        P(),
        P(),
        P(),
        P(),
        P(),
        P(),
        P(),
        P(),
        P(),
        P("imgs"),
    )
    out_specs = (
        P("imgs", "rows", None, None),
        P("imgs", "rows", None, None),
        P(),
        P(),
        P(),
        P(),
        P(),
        P(),
        P(),
        P(),
        P(),
        P(),
        P(),
    )
    return jax.shard_map(
        on_device, mesh=mesh, in_specs=in_specs, out_specs=out_specs, check_vma=False
    )
```

profile of v0, /device:TPU:0, one launch (start us, length us, event | category | flops | bytes accessed | tf_op | source)
XLA Modules:
  0.0 1524.6 jit_solution(15453987486436206448)
XLA Ops:
  12.1 2.9 fusion.232
  15.0 42.0 %all-reduce.9 = (f32[320]{0:T(512)S(1)}, f32[320]{0:T(512)S(1)}) all-reduce(f32[320]{0:T(512)S(1)} %get-tuple-element.148, f32[320]{0:T(512)S(1)} %get-tuple-element.147), channel_id=1, replica_groups=mesh['rows'=2,'imgs'=16] {'rows','imgs'}, use_global_device_ids=true, to_apply=%region_6.0 | all-reduce | flops 640 | bytes 5120 | tf_op jit(solution)/shard_map/psum | solution.py:126
  57.7 19.4 %broadcast_select_fusion.1 = (bf16[16,11,18,320]{3,2,1,0:T(8,128)(2,1)S(1)}, bf16[16,11,18,320]{3,2,1,0:T(8,128)(2,1)}, f32[16,11,18,320]{3,2,1,0:T(8,128)}) fusion(pred[16,11,18]{2,1,0:T(8,128)(4,1)S(1)} %get-tuple-element.309, f32[320]{0:T(512)S(1)} %get-tuple-element.239, bf16[320,320]{1,0:T(8,128)(2,1)} %param.21, ...), kind=kOutput, calls=%fused_computation.485 | convolution fusion | flops 722810880 | bytes 10363360 | tf_op jit(solution)/shard_map/irwk,kn->irwn/dot_general | solution.py:27
  78.7 3.1 collective-permute-start
  83.3 4.0 maximum_convert_fusion.4
  87.5 67.1 %broadcast_select_fusion = bf16[16,11,18,320]{3,2,1,0:T(8,128)(2,1)} fusion(pred[16,11,18]{2,1,0:T(8,128)(4,1)S(1)} %get-tuple-element.309, f32[320]{0:T(512)S(1)} %get-tuple-element.238, f32[320]{0:T(512)S(1)} %get-tuple-element.232, f32[320]{0:T(512)S(1)} %get-tuple-element.233, f32[16,15,18,320]{3,2,1,0:T(8,128)} %maximum_convert_fusion.4, ...), kind=kLoop, calls=%fused_computation.484 | loop fusion | flops 52715520 | bytes 43351648 | tf_op jit(solution)/shard_map/jit(_where)/select_n | solution.py:43
  154.7 3.1 fusion.264
  159.9 3.4 collective-permute-start.2
  167.4 6.5 maximum_convert_fusion.2
  174.3 145.7 %add_convert_fusion.4 = bf16[16,11,18,320]{3,2,1,0:T(8,128)(2,1)} fusion(f32[16,29,18,320]{3,2,1,0:T(8,128)} %maximum_convert_fusion.2, f32[320]{0:T(512)S(1)} %get-tuple-element.237, f32[320]{0:T(512)S(1)} %get-tuple-element.198, f32[320]{0:T(512)S(1)} %get-tuple-element.199, f32[320]{0:T(512)S(1)} %get-tuple-element.152, f32[320]{0:T(512)S(1)} %get-tuple-element.153, ...), kind=kLoop, calls=%fused_computation.456 | loop fusion | flops 100362240 | bytes 64620544 | tf_op jit(solution)/shard_map/convert_element_type | solution.py:141
  320.0 8.4 fusion.28
  328.4 8.8 multiply_reduce_fusion.6
  337.2 49.8 %all-reduce.8 = (f32[320]{0:T(512)S(1)}, f32[320]{0:T(512)S(1)}) all-reduce(f32[320]{0:T(512)S(1)} %get-tuple-element.137, f32[320]{0:T(512)S(1)} %get-tuple-element.136), channel_id=1, replica_groups=mesh['rows'=2,'imgs'=16] {'rows','imgs'}, use_global_device_ids=true, to_apply=%region_10.11 | all-reduce | flops 640 | bytes 5120 | tf_op jit(solution)/shard_map/psum | solution.py:151
  387.6 8.5 fusion.27
  397.8 3.1 collective-permute-start.4
  403.0 9.4 maximum_convert_fusion
  412.4 91.2 %multiply_convert_fusion = (bf16[16,11,18,1280]{3,2,1,0:T(8,128)(2,1)}, f32[16,11,18,1280]{3,2,1,0:T(8,128)}, f32[16,11,18,1280]{3,2,1,0:T(8,128)}) fusion(f32[1280]{0:T(1024)S(1)} %get-tuple-element.242, f32[1280]{0:T(1024)S(1)} %get-tuple-element.207, f32[16,13,18,1280]{3,2,1,0:T(8,128)} %maximum_convert_fusion, f32[1280]{0:T(1024)S(1)} %get-tuple-element.208, ...), kind=kLoop, calls=%fused_computation.200 | loop fusion | flops 336568320 | bytes 131041280 | tf_op jit(solution)/shard_map/convert_element_type | solution.py:161
  503.6 79.0 %fusion.9 = (f32[1280]{0:T(1024)S(1)}, f32[1280]{0:T(1024)S(1)}, f32[1280]{0:T(1024)S(1)}, f32[1280]{0:T(1024)S(1)}, f32[1280]{0:T(1024)S(1)}, /*index=5*/f32[12...) fusion(f32[16,13,18,1280]{3,2,1,0:T(8,128)} %maximum_convert_fu, ...), kind=kOutput, calls=%fused_computation.180 | convolution fusion | flops 2737139200 | bytes 144715392 | tf_op jit(solution)/shard_map/irwn,kn->irwk/dot_general | solution.py:35
  588.2 4.8 collective-permute-start.6
  594.3 9.7 convolution_bitcast_fusion.1
  606.7 9.8 maximum_convert_fusion.1
  616.5 67.0 %convert_reduce_fusion.3 = (f32[1280]{0:T(1024)S(1)}, bf16[16,11,18,1280]{3,2,1,0:T(8,128)(2,1)}) fusion(f32[1280]{0:T(1024)S(1)} %get-tuple-element.200, f32[16,13,18,1280]{3,2,1,0:T(8,128)} %maximum_convert_fusion.1, f32[1280]{0:T(1024)S(1)} %get-tuple-element.206, f32[1280]{0:T(1024)S(1)} %get-tuple-element.205, f32[1280]{0:T(1024)S(1)} %get-tuple-element.204, ...), kind=kLoop, calls=%fused_computation.194 | loop fusion | flops 85154560 | bytes 98613632 | tf_op jit(solution)/shard_map/reduce_sum | solution.py:39
  683.5 11.1 convolution_bitcast_fusion
  694.6 10.1 fusion.253
  704.7 40.1 %all-reduce.7 = (f32[320]{0:T(512)S(1)}, f32[320]{0:T(512)S(1)}) all-reduce(f32[320]{0:T(512)S(1)} %get-tuple-element.141, f32[320]{0:T(512)S(1)} %get-tuple-element.140), channel_id=1, replica_groups=mesh['rows'=2,'imgs'=16] {'rows','imgs'}, use_global_device_ids=true, to_apply=%region_14.15 | all-reduce | flops 640 | bytes 5120 | tf_op jit(solution)/shard_map/psum | solution.py:182
  744.8 8.4 convert_reduce_fusion.5
  753.2 5.2 convert_reduce_fusion.6
  758.5 43.1 %fusion.104 = (f32[320]{0:T(512)S(1)}, f32[320]{0:T(512)S(1)}, f32[320]{0:T(512)S(1)}, f32[320]{0:T(512)S(1)}, f32[320]{0:T(512)S(1)}, /*index=5*/f32[320]{0:T(5...) fusion(f32[16,29,18,320]{3,2,1,0:T(8,128)} %maximum_convert_fus, ...), kind=kOutput, calls=%fused_computation.300 | convolution fusion | flops 688336960 | bytes 34365184 | tf_op jit(solution)/shard_map/irwn,kn->irwk/dot_general | solution.py:35
  801.6 30.8 %fusion.102 = (f32[320]{0:T(512)S(1)}, f32[320]{0:T(512)S(1)}, f32[320]{0:T(512)S(1)}, f32[320]{0:T(512)S(1)}, f32[320]{0:T(512)S(1)}, /*index=5*/f32[320]{0:T(5...) fusion(bf16[16,11,18,320]{3,2,1,0:T(8,128)(2,1)} %get-tuple-ele, ...), kind=kLoop, calls=%fused_computation.298 | loop fusion | flops 27367360 | bytes 33341696 | tf_op jit(solution)/shard_map/reduce_sum | solution.py:82
  832.4 49.6 %fusion.103 = (f32[320]{0:T(512)S(1)}, f32[320]{0:T(512)S(1)}, f32[320]{0:T(512)S(1)}, f32[320]{0:T(512)S(1)}, f32[320]{0:T(512)S(1)}, /*index=5*/f32[320]{0:T(5...) fusion(bf16[16,11,18,320]{3,2,1,0:T(8,128)(2,1)} %get-tuple-ele, ...), kind=kLoop, calls=%fused_computation.299 | loop fusion | flops 37503360 | bytes 39836160 | tf_op jit(solution)/shard_map/reduce_sum | solution.py:82
  882.0 3.1 fusion.263
  888.4 5.7 collective-permute-start.8
  899.3 4.4 stack.401
  903.7 5.3 convolution_bitcast_fusion.3
  913.7 6.8 maximum_convert_fusion.3
  920.8 165.4 %fusion.53 = (f32[320]{0:T(512)S(1)}, f32[320]{0:T(512)S(1)}, f32[320]{0:T(512)S(1)}, f32[320]{0:T(512)S(1)}, f32[320]{0:T(512)S(1)}, /*index=5*/bf16[16,11,18,320]{3,2,1,0:T(8,128)(2,1)}) fusion(f32[16,15,18,320]{3,2,1,0:T(8,128)} %maximum_convert_fusion.4, f32[320]{0:T(512)S(1)} %copy-done.90, f32[320]{0:T(512)S(1)} %copy-done.52, f32[320]{0:T(512)S(1)} %copy-done.30, ...), kind=kLoop, calls=%fused_computation.249 | loop fusion | flops 111512000 | bytes 79974528 | tf_op jit(solution)/shard_map/reduce_sum | solution.py:82
  1086.3 27.9 %fusion.55 = (f32[320]{0:T(512)S(1)}, f32[320]{0:T(512)S(1)}, f32[320]{0:T(512)S(1)}, f32[320]{0:T(512)S(1)}, f32[320]{0:T(512)S(1)}, /*index=5*/f32[320]{0:T(51...) fusion(bf16[16,11,18,320]{3,2,1,0:T(8,128)(2,1)} %get-tuple-element.276,, ...), kind=kLoop, calls=%fused_computation.251 | loop fusion | flops 22299200 | bytes 25081600 | tf_op jit(solution)/shard_map/reduce_sum | solution.py:82
  1117.9 3.1 collective-permute-start.10
  1121.0 13.9 fusion.54
  1141.8 41.9 %convert_reduce_fusion.7 = (f32[320]{0:T(512)S(1)}, bf16[16,11,18,320]{3,2,1,0:T(8,128)(2,1)}) fusion(f32[320]{0:T(512)S(1)} %copy-done.107, f32[320]{0:T(512)S(1)} %copy-done.145, f32[16,15,18,320]{3,2,1,0:T(8,128)S(1)} %maximum_convert_fusion.5, f32[320]{0:T(512)S(1)} %copy-done.151, f32[320]{0:T(512)S(1)} %copy-done.149, f32[320]{0:T(512)S(1)} %copy-done.147, ...), kind=kLoop, calls=%fused_computation.432 | loop fusion | flops 129760960 | bytes 55667200 | tf_op jit(solution)/shard_map/reduce_sum | solution.py:39
  1184.3 7.1 multiply_add_fusion.2
  1191.4 21.2 %fusion.252 = (f32[320]{0:T(512)}, f32[320]{0:T(512)}, f32[320]{0:T(512)S(1)}, f32[320]{0:T(512)S(1)}, f32[320]{0:T(512)S(1)}, /*index=5*/f32[16,11,18,320]{3,2,1,0:T(8,128)}) fusion(f32[16,11,18,320]{3,2,1,0:T(8,128)} %multiply_add_fusion.2, f32[320]{0:T(512)S(1)} %copy-done.157, f32[320]{0:T(512)} %get-tuple-element.312, ...), kind=kOutput, calls=%fused_computation.626 | convolution fusion | flops 2622595584 | bytes 33287552 | tf_op jit(solution)/shard_map/irwk,kn->irwn/dot_general | solution.py:27
  1214.3 5.7 convolution_bitcast_fusion.4
  1220.1 6.0 copy.87
  1226.1 125.4 %all-reduce.14.cloned.1.call-done = (f32[320]{0:T(512)}, f32[320]{0:T(512)}, f32[1,320]{1,0:T(1,128)}, f32[1,320]{1,0:T(1,128)}, f32[1,320]{1,0:T(1,128)}, /*ind...) async-done(((f32[320]{0:T(512)}, f32[320]{0:T(512)}, ...) | async-done | bytes 163856 | tf_op jit(solution)/shard_map/psum | solution.py:215
  1353.5 6.4 add_multiply_fusion
  1360.1 3.1 copy.88
  1365.1 141.0 %all-reduce.16.cloned.1.call-done = (f32[320,320]{1,0:T(8,128)}, f32[320,320]{1,0:T(8,128)}, f32[320,320]{1,0:T(8,128)}, f32[320,1280]{1,0:T(8,128)}, f32[1280,320]{0,1:T(8,128)}) async-done(((f32[320,320]{1,0:T(8,128)}, f32[320,320]{1,0:T(8,128)}, f32[320,320]{1,0:T(8,128)}, f32[320,1280]{1,0:T(8,128)}, f32[1280,320]{0,1:T(8,128)}), (f32[320,320]{1,0:T(8,128)}, f32[320,320]{1,0:T(8,128)}, ...) | async-done | bytes 4505616 | tf_op jit(solution)/shard_map/psum | solution.py:222
  (560 shorter events, 67.7 us)
Async XLA Ops:
  7.2 496.4 %copy-start = (bf16[1280,320]{0,1:T(8,128)(2,1)S(1)}, bf16[1280,320]{0,1:T(8,128)(2,1)}, u32[]{:S(2)}) copy-start(bf16[1280,320]{0,1:T(8,128)(2,1)} %param.25) | copy-start | bytes 2457604
  7.2 1344.3 %all-reduce.14.cloned.1.call-start = ((), (), s32[]{:S(2)}) async-start(), calls=%async_computation | async-start | bytes 487424 | tf_op jit(solution)/shard_map/psum | solution.py:215
  11.9 65.2 %copy-start.161 = (f32[320]{0:T(512)}, f32[320]{0:T(512)S(1)}, u32[]{:S(2)}) copy-start(f32[320]{0:T(512)S(1)} %get-tuple-element.239) | copy-start | bytes 3844
  57.7 24.2 %copy-start.27 = (f32[25,320]{1,0:T(8,128)S(1)}, f32[25,320]{1,0:T(8,128)}, u32[]{:S(2)}) copy-start(f32[25,320]{1,0:T(8,128)} %param.26) | copy-start | bytes 96004
  77.3 4.9 collective-permute-start.1
  78.7 4.5 collective-permute-start
  158.1 6.5 collective-permute-start.3
  159.9 6.9 collective-permute-start.2
  163.5 10.4 copy-start.29
  163.5 10.4 copy-start.31
  163.5 10.4 copy-start.33
  163.5 10.4 copy-start.35
  163.5 10.4 copy-start.37
  163.5 10.4 copy-start.39
  163.5 10.4 copy-start.41
  163.5 10.4 copy-start.43
  174.3 145.7 %copy-start.16 = (bf16[320,320]{1,0:T(8,128)(2,1)S(1)}, bf16[320,320]{1,0:T(8,128)(2,1)}, u32[]{:S(2)}) copy-start(bf16[320,320]{1,0:T(8,128)(2,1)} %param.22) | copy-start | bytes 614404
  328.4 59.1 %copy-start.178 = (bf16[320,1280]{1,0:T(8,128)(2,1)S(1)}, bf16[320,1280]{1,0:T(8,128)(2,1)}, u32[]{:S(2)}) copy-start(bf16[320,1280]{1,0:T(8,128)(2,1)} %param.24) | copy-start | bytes 2457604
  396.4 4.7 collective-permute-start.5
  397.8 4.9 collective-permute-start.4
  412.4 91.2 %copy-start.12 = (bf16[16,11,18,320]{3,0,2,1:T(8,128)(2,1)S(1)}, bf16[16,11,18,320]{3,0,2,1:T(8,128)(2,1)}, u32[]{:S(2)}) copy-start(bf16[16,11,18,320]{3,0,2,1:T(8,128)(2,1)} %param.17) | copy-start | bytes 6082564
  412.4 91.2 %copy-start.168 = (f32[320]{0:T(512)S(1)}, f32[320]{0:T(512)}, u32[]{:S(2)}) copy-start(f32[320]{0:T(512)} %get-tuple-element.326) | copy-start | bytes 3844
  586.9 17.1 %collective-permute-start.7 = (bf16[16,1,18,1280]{3,0,2,1:T(8,128)(2,1)}, bf16[16,1,18,1280]{3,0,2,1:T(8,128)(2,1)}, u32[]{:S(2)}, u32[]{:S(2)}) collective-permute-start(bf16[16,1,18,1280]{3,0,2,1:T(8,128)(2,1)} %copy.76), channel_id=1, source_target_pairs={{16,0},{17,1},{18,2},{19,3},{20,4},{21,5},{22,6},{23,7},{24,8},{25... | collective-permute-start | bytes 2211848 | tf_op jit(solution)/shard_map/ppermute | solution.py:17
  588.2 17.1 %collective-permute-start.6 = (bf16[16,1,18,1280]{3,0,2,1:T(8,128)(2,1)}, bf16[16,1,18,1280]{3,0,2,1:T(8,128)(2,1)}, u32[]{:S(2)}, u32[]{:S(2)}) collective-permute-start(bf16[16,1,18,1280]{3,0,2,1:T(8,128)(2,1)} %copy.75), channel_id=1, source_target_pairs={{0,16},{1,17},{2,18},{3,19},{4,20},{5,21},{6,22},{7,23},{8,24},{9,... | collective-permute-start | bytes 2211848 | tf_op jit(solution)/shard_map/ppermute | solution.py:16
  594.3 12.4 slice-start.5
  594.3 12.4 slice-start.6
  594.3 12.4 slice-start.7
  616.5 67.0 %copy-start.24 = (f32[320]{0:T(512)S(1)}, f32[320]{0:T(512)}, u32[]{:S(2)}) copy-start(f32[320]{0:T(512)} %copy-done.23) | copy-start | bytes 3844
  616.5 67.0 %copy-start.26 = (f32[320]{0:T(512)S(1)}, f32[320]{0:T(512)}, u32[]{:S(2)}) copy-start(f32[320]{0:T(512)} %copy-done.25) | copy-start | bytes 3844
  683.5 11.1 copy-start.2
  683.5 11.1 copy-start.158
  683.5 11.1 copy-start.179
  758.5 43.1 %copy-start.8 = (bf16[16,11,18,320]{3,2,1,0:T(8,128)(2,1)}, bf16[16,11,18,320]{3,2,1,0:T(8,128)(2,1)S(1)}, u32[]{:S(2)}) copy-start(bf16[16,11,18,320]{3,2,1,0:T(8,128)(2,1)S(1)} %get-tuple-element.283) | copy-start | bytes 6082564
  887.0 22.0 %collective-permute-start.9 = (bf16[16,9,18,320]{3,0,2,1:T(8,128)(2,1)}, bf16[16,9,18,320]{3,0,2,1:T(8,128)(2,1)}, u32[]{:S(2)}, u32[]{:S(2)}) collective-permute-start(bf16[16,9,18,320]{3,0,2,1:T(8,128)(2,1)} %copy.80), channel_id=1, source_target_pairs={{16,0},{17,1},{18,2},{19,3},{20,4},{21,5},{22,6},{23,7},{24,8},{25... | collective-permute-start | bytes 4976648 | tf_op jit(solution)/shard_map/ppermute | solution.py:17
  888.4 22.8 %collective-permute-start.8 = (bf16[16,9,18,320]{3,0,2,1:T(8,128)(2,1)S(1)}, bf16[16,9,18,320]{3,0,2,1:T(8,128)(2,1)}, u32[]{:S(2)}, u32[]{:S(2)}) collective-permute-start(bf16[16,9,18,320]{3,0,2,1:T(8,128)(2,1)S(1)} %copy.79), channel_id=1, source_target_pairs={{0,16},{1,17},{2,18},{3,19},{4,20},{5,21},{6,22},{7,23},{8,24},{9,... | collective-permute-start | bytes 4976648 | tf_op jit(solution)/shard_map/ppermute | solution.py:16
  1086.3 34.7 %slice-start = ((s8[8847360]{0:T(1024)(128)(4,1)}), s8[4194304]{0:T(1024)(128)(4,1)S(1)}, s32[]{:S(2)}) async-start(s8[8847360]{0:T(1024)(128)(4,1)} %bitcast.86), calls=%async_computation.2 | async-start | bytes 8388608
  1086.3 34.7 %slice-start.1 = ((s8[8847360]{0:T(1024)(128)(4,1)}), s8[4194304]{0:T(1024)(128)(4,1)S(1)}, s32[]{:S(2)}) async-start(s8[8847360]{0:T(1024)(128)(4,1)} %bitcast.86), calls=%async_computation.3 | async-start | bytes 8388608
  1086.3 34.7 %slice-start.2 = ((s8[8847360]{0:T(1024)(128)(4,1)}), s8[458752]{0:T(1024)(128)(4,1)S(1)}, s32[]{:S(2)}) async-start(s8[8847360]{0:T(1024)(128)(4,1)} %bitcast.86), calls=%async_computation.4 | async-start | bytes 917504
  1116.6 21.7 %collective-permute-start.11 = (bf16[16,2,18,320]{3,0,2,1:T(8,128)(2,1)S(1)}, bf16[16,2,18,320]{3,0,2,1:T(8,128)(2,1)S(1)}, u32[]{:S(2)}, u32[]{:S(2)}) collective-permute-start(bf16[16,2,18,320]{3,0,2,1:T(8,128)(2,1)S(1)} %copy.84), channel_id=1, source_target_pairs={{16,0},{17,1},{18,2},{19,3},{20,4},{21,5},{22,6},{23,7},{24,8},{25... | collective-permute-start | bytes 1105928 | tf_op jit(solution)/shard_map/ppermute | solution.py:17
  1117.9 20.5 %collective-permute-start.10 = (bf16[16,2,18,320]{3,0,2,1:T(8,128)(2,1)}, bf16[16,2,18,320]{3,0,2,1:T(8,128)(2,1)S(1)}, u32[]{:S(2)}, u32[]{:S(2)}) collective-permute-start(bf16[16,2,18,320]{3,0,2,1:T(8,128)(2,1)} %copy.83), channel_id=1, source_target_pairs={{0,16},{1,17},{2,18},{3,19},{4,20},{5,21},{6,22},{7,23},{8,24},{9,... | collective-permute-start | bytes 1105928 | tf_op jit(solution)/shard_map/ppermute | solution.py:16
  1138.7 45.5 %slice-start.3 = ((s8[6488064]{0:T(1024)(128)(4,1)}), s8[4194304]{0:T(1024)(128)(4,1)S(1)}, s32[]{:S(2)}) async-start(s8[6488064]{0:T(1024)(128)(4,1)} %bitcast.88), calls=%async_computation.5 | async-start | bytes 8388608
  1141.7 42.5 %slice-start.4 = ((s8[6488064]{0:T(1024)(128)(4,1)}), s8[2293760]{0:T(1024)(128)(4,1)S(1)}, s32[]{:S(2)}) async-start(s8[6488064]{0:T(1024)(128)(4,1)} %bitcast.88), calls=%async_computation.6 | async-start | bytes 4587520
  1141.7 42.5 %copy-start.18 = (bf16[320,320]{1,0:T(8,128)(2,1)S(1)}, bf16[320,320]{1,0:T(8,128)(2,1)}, u32[]{:S(2)}) copy-start(bf16[320,320]{1,0:T(8,128)(2,1)} %param.21) | copy-start | bytes 614404
  1191.3 23.0 %copy-start.11 = (bf16[16,11,18,320]{3,0,2,1:T(8,128)(2,1)S(1)}, bf16[16,11,18,320]{3,0,2,1:T(8,128)(2,1)}, u32[]{:S(2)}) copy-start(bf16[16,11,18,320]{3,0,2,1:T(8,128)(2,1)} %param.16) | copy-start | bytes 6082564
  1214.3 291.8 %all-reduce.16.cloned.1.call-start = ((), (), s32[]{:S(2)}) async-start(), calls=%async_computation.1 | async-start | bytes 9502720 | tf_op jit(solution)/shard_map/psum | solution.py:222
  1363.2 152.4 %copy-start.22 = (f32[25,320]{1,0:T(8,128)S(1)}, f32[25,320]{1,0:T(8,128)}, u32[]{:S(2)}) copy-start(f32[25,320]{1,0:T(8,128)} %get-tuple-element.337) | copy-start | bytes 96004
  1363.2 153.0 %copy-start.19 = (f32[49,320]{1,0:T(8,128)S(1)}, f32[49,320]{1,0:T(8,128)}, u32[]{:S(2)}) copy-start(f32[49,320]{1,0:T(8,128)} %get-tuple-element.338) | copy-start | bytes 188164
  1363.2 153.7 %copy-start.20 = (f32[9,1280]{1,0:T(8,128)S(1)}, f32[9,1280]{1,0:T(8,128)}, u32[]{:S(2)}) copy-start(f32[9,1280]{1,0:T(8,128)} %get-tuple-element.339) | copy-start | bytes 138244
  (154 other events, 1007.1 us)
Sparse Core Ops, SparseCore 0:
  1214.4 137.0 all-reduce.13
  1359.1 146.9 all-reduce.15
where the time goes:
time: 1530 us; the launch traced here: 1520 us
  other arithmetic  763 us (50%)
  waiting for transfers between devices  270 us (18%)
  matrix products  245 us (16%)
  blocking collectives  132 us (9%)
  local copies, waits for them, and re-layouts  64.4 us (4%)
  starting transfers between devices  31.4 us (2%)
  between operations  18.5 us (1%)
    reduce_sum x5, other arithmetic, kernel_grad(): tap_sums.append(jnp.sum(gradient_f * window, axis=(0, 1, 2)))  288 us
    convert_element_type x1, other arithmetic, on_device(): (depthwise(dilated_margin, kernel_dilated, 7, 3, band_rows) + shifts[3])....  146 us
    dot_general x5, matrix products, back_matmul(): jnp.einsum('irwn,kn->irwk', gradient, weight, preferred_element_type=jnp....  144 us
    psum x1, waiting for transfers between devices, on_device(): lax.psum((gain_four, bias_reduce, bias_expand, bias_conv, grad_w_expand,...  141 us
    psum x1, waiting for transfers between devices, on_device(): lax.psum((pixel_sum(grad_normed_one), pixel_sum(grad_normed_one * hat_one...  125 us
    reduce_sum x4, other arithmetic, pixel_sum(): return jnp.sum(values.astype(jnp.float32), axis=(0, 1, 2))  120 us
    convert_element_type x1, other arithmetic, on_device(): hidden_act = smooth(hidden_conv).astype(jnp.bfloat16)  91.2 us
    select_n x1, other arithmetic, keep_inside(): return jnp.where(inside > 0, values, jnp.zeros_like(values))  67.1 us
  transfers between devices with their start and end apart: 14, of which 5 were waited for; matrix products, arithmetic and copies ran while one was open for 5% of the time, Pallas kernels for 0%

commit v1 on v0

v1 whole, which is shorter than its diff:
```python
import functools

import jax
import jax.numpy as jnp
from jax import lax
from jax.experimental import pallas as pl
from jax.experimental.pallas import tpu as pltpu
from jax.sharding import PartitionSpec as P

MESH = pl.DeviceIdType.MESH
epsilon = 1e-05
bf16 = jnp.bfloat16
f32 = jnp.float32
SUB = 8
LANE = 128
MIB = 1 << 20
ANY = pl.BlockSpec(memory_space=pl.ANY)
VMEM = pl.BlockSpec(memory_space=pltpu.VMEM)


def low(values):
    return values.astype(bf16).astype(f32)


def normal_parts(v):
    bell = jnp.exp(-0.5 * (v * v))
    base = 1.0 + (0.3275911 * 0.7071067811865476) * jnp.abs(v)
    t = pl.reciprocal(base, approx=True)
    t = t * (2.0 - base * t)
    poly = 0.5 * 1.061405429
    for coef in (-1.453152027, 1.421413741, -0.284496736, 0.254829592):
        poly = poly * t + 0.5 * coef
    tail = poly * t * bell
    return jnp.where(v >= 0, 1.0 - tail, tail), bell * 0.3989422804014327


def dot(a, b):
    return jnp.dot(a, b, preferred_element_type=f32)


def dot_nt(a, b):
    return lax.dot_general(a, b, (((1,), (1,)), ((), ())), preferred_element_type=f32)


def dot_tn(a, b):
    return lax.dot_general(a, b, (((0,), (0,)), ((), ())), preferred_element_type=f32)


def groups_of(channels):
    return [(g, min(LANE, channels - g * LANE)) for g in range(pl.cdiv(channels, LANE))]


def spread_taps(k_ref, kb, flip=False):
    count, channels = k_ref.shape
    for tap in range(count):
        from_tap = count - 1 - tap if flip else tap
        row = jnp.broadcast_to(k_ref[from_tap : from_tap + 1, :], (SUB, channels))
        for g, width in groups_of(channels):
            kb[tap, g, :, :width] = row[:, g * LANE : g * LANE + width]


def add_row(acc, load, taps, dilation):
    columns, half = len(acc), len(taps) // 2
    for c in range(columns):
        value = load(c)
        for j, tap in enumerate(taps):
            at = c - (j - half) * dilation
            if 0 <= at < columns:
                acc[at] = acc[at] + tap * value
    return acc


def tap_sums(acc, load_fixed, load_moved, dilation):
    columns, half = load_fixed[1], len(acc) // 2
    fixed = [load_fixed[0](c) for c in range(columns)]
    for c in range(columns):
        value = load_moved(c)
        for j in range(len(acc)):
            at = c - (j - half) * dilation
            if 0 <= at < columns:
                acc[j] = acc[j] + fixed[at] * value
    return acc


def row_range(r, rows, half, dilation):
    low_i = jnp.maximum(half - r // dilation, 0)
    high_i = jnp.minimum(half + (rows - 1 - r) // dilation, 2 * half)
    return low_i, high_i + 1


def zeros_list(count):
    return [jnp.zeros((SUB, LANE), f32) for _ in range(count)]


def b8(ref, i):
    return jnp.broadcast_to(ref[i : i + 1, :], (SUB, ref.shape[1]))


def make_col_mask(meta, cm):
    size = meta[2]
    for c in range(cm.shape[0]):
        cm[c] = (size > c).astype(f32)


def row_mask(meta, cm, r):
    at = (r * 1).astype(f32)
    inside = (at >= meta[1]) & (at < meta[1] + meta[2])
    return cm[...] * inside.astype(f32)[None]


def pixels3(values):
    return values.reshape(values.shape[0] // SUB, SUB, values.shape[1])


def pixels2(values):
    return values.reshape(values.shape[0] * SUB, values.shape[2])


def fold(values):
    return jnp.sum(values, axis=0)


def statistics(sums, count, i):
    mean = b8(sums, i) / count
    return mean, lax.rsqrt(b8(sums, i + 1) / count - mean * mean + epsilon)


def mixer_kernel(
    xw, cw, meta, count, sums1, scales, shifts, w_in, w_gate, w_out, kl, kd,
    xa_o, ca_o, gl_o, sl_o, c1_o, c2_o, gp_o, bn_o, sums_o,
    cm, klb, kdb, xa, ca, gl, sl, c1, c2, gp, bn, gf, c1f, sem,
):
    rows, px, channels = xa.shape
    columns = px // SUB
    groups = groups_of(channels)
    offsets = xw.shape[0] - rows + 1
    make_col_mask(meta, cm)
    spread_taps(kl, klb)
    spread_taps(kd, kdb)
    for edge in (0, 1, rows + 2, rows + 3):
        gf[:, edge] = jnp.zeros(gf.shape[:1] + gf.shape[2:], f32)
    total = count[0:1, 0:1]
    mean, rstd = statistics(sums1, total, 0)
    scale = rstd * b8(scales, 0)
    starts = [meta[0] == float(t) for t in range(offsets)]

    def aligned(ref, r):
        value = pixels3(ref[r].astype(f32))
        for t in range(1, offsets):
            value = jnp.where(starts[t][None], pixels3(ref[r + t].astype(f32)), value)
        return value

    def first(r, _):
        mask = row_mask(meta, cm, r)
        x = mask * aligned(xw, r)
        xa[r] = pixels2(x).astype(bf16)
        ca[r] = pixels2(mask * aligned(cw, r)).astype(bf16)
        normed = pixels2((x - mean) * scale + b8(shifts, 0)).astype(bf16)
        pre = pixels3(dot(normed, w_in[...])) + b8(shifts, 1)
        phi_sum, bell = normal_parts(pre)
        gelu = mask * low(pre * phi_sum)
        sl[r] = pixels2(phi_sum + pre * bell)
        gl[r] = pixels2(gelu).astype(bf16)
        for g, width in groups:
            gf[g, r + 2, :, :, :width] = gelu[:, :, g * LANE : g * LANE + width]
        return 0

    lax.fori_loop(0, rows, first, 0)
    early = [(xa, xa_o), (ca, ca_o), (gl, gl_o), (sl, sl_o)]
    copies = [pltpu.make_async_copy(a, b, sem.at[k]) for k, (a, b) in enumerate(early)]
    for copy in copies:
        copy.start()

    def local(r, _):
        mask = row_mask(meta, cm, r)
        for g, width in groups:
            acc = zeros_list(columns)
            for i in range(5):
                taps = [klb[5 * i + j, g] for j in range(5)]
                acc = add_row(acc, lambda c: gf[g, r + i, c], taps, 1)
            bias = b8(shifts, 2)[:, g * LANE : g * LANE + width]
            value = jnp.stack(acc)[:, :, :width] + bias
            value = mask[:, :, :width] * low(value)
            c1f[g, r, :, :, :width] = value
            c1[r, :, g * LANE : g * LANE + width] = pixels2(value).astype(bf16)
        return 0

    lax.fori_loop(0, rows, local, 0)
    copies.append(pltpu.make_async_copy(c1, c1_o, sem.at[4]))
    copies[-1].start()

    def dilated(r, _):
        low_i, high_i = row_range(r, rows, 3, 3)
        for g, width in groups:

            def tap_row(i, acc):
                taps = [kdb[7 * i + j, g] for j in range(7)]
                at = r + (i - 3) * 3
                return add_row(list(acc), lambda c: c1f[g, at, c], taps, 3)

            acc = lax.fori_loop(low_i, high_i, tap_row, zeros_list(columns))
            bias = b8(shifts, 3)[:, g * LANE : g * LANE + width]
            value = jnp.stack(acc)[:, :, :width] + bias
            c2[r, :, g * LANE : g * LANE + width] = pixels2(value).astype(bf16)
        return 0

    lax.fori_loop(0, rows, dilated, 0)
    copies.append(pltpu.make_async_copy(c2, c2_o, sem.at[5]))
    copies[-1].start()

    def last(r, sums):
        mask = row_mask(meta, cm, r)
        gate = dot(c2[r], w_gate[...]) + jnp.broadcast_to(shifts[4:5, :], (px, channels))
        gp[r] = gate
        gated = (gl[r].astype(f32) * gate).astype(bf16)
        branch = dot(gated, w_out[...])
        x = pixels3(xa[r].astype(f32))
        normed = low((x - mean) * scale + b8(shifts, 0))
        both = pixels3(branch) + b8(shifts, 5) + normed
        bn[r] = pixels2(both)
        middle = mask * (x + b8(scales, 1) * both)
        return sums[0] + fold(middle), sums[1] + fold(middle * middle)

    zero = jnp.zeros((SUB, channels), f32)
    sums = lax.fori_loop(0, rows, last, (zero, zero))
    copies.append(pltpu.make_async_copy(gp, gp_o, sem.at[6]))
    copies[-1].start()
    copies.append(pltpu.make_async_copy(bn, bn_o, sem.at[7]))
    copies[-1].start()
    sums_o[0] = sums[0]
    sums_o[1] = sums[1]
    for copy in copies:
        copy.wait()


def mixer_forward(xw, cw, meta, count, sums1, scales, shifts, w_in, w_gate, w_out, kl, kd):
    band, px, channels = xw.shape
    columns = px // SUB
    rows = columns
    n = len(groups_of(channels))
    small = (rows, px, channels)
    kinds = (bf16, bf16, bf16, f32, bf16, bf16, f32, f32)
    return pl.pallas_call(
        mixer_kernel,
        name="mixer_forward",
        out_shape=[jax.ShapeDtypeStruct(small, k) for k in kinds]
        + [jax.ShapeDtypeStruct((2, SUB, channels), f32)],
        in_specs=[VMEM] * 12,
        out_specs=[ANY] * 8 + [VMEM],
        scratch_shapes=[
            pltpu.VMEM((columns, SUB, channels), f32),
            pltpu.VMEM((25, n, SUB, LANE), f32),
            pltpu.VMEM((49, n, SUB, LANE), f32),
        ]
        + [pltpu.VMEM(small, k) for k in kinds]
        + [
            pltpu.VMEM((n, rows + 4, columns, SUB, LANE), f32),
            pltpu.VMEM((n, rows, columns, SUB, LANE), f32),
            pltpu.SemaphoreType.DMA((8,)),
        ],
        compiler_params=pltpu.CompilerParams(vmem_limit_bytes=56 * MIB),
    )(xw, cw, meta, count, sums1, scales, shifts, w_in, w_gate, w_out, kl, kd)


def hidden_kernel(
    xa, ca, bn, meta, count, sums2, scales, shifts, hshift, w_e, w_rt, kh,
    res_o, gn_o, gwe_o, gwr_o, gk_o, gh_o, sums_o,
    cm, khb, kfb, n2, gr, ha, ge, em, gc, kacc, wet, wr, sem,
):
    rows, px, channels = xa.shape
    columns = px // SUB
    hidden = w_e.shape[1]
    wide = em.shape[0] * LANE
    parts = em.shape[0]
    make_col_mask(meta, cm)
    spread_taps(kh, khb)
    spread_taps(kh, kfb, flip=True)
    for edge in (0, rows + 1):
        em[:, edge] = jnp.zeros(em.shape[:1] + em.shape[2:], f32)
        gc[:, edge] = jnp.zeros(gc.shape[:1] + gc.shape[2:], f32)
    wet[...] = w_e[...].astype(f32).T.astype(bf16)
    wr[...] = w_rt[...].astype(f32).T.astype(bf16)
    total = count[0:1, 0:1]
    mean, rstd = statistics(sums2, total, 0)
    scale = rstd * b8(scales, 2)

    def middle_of(r):
        return pixels3(xa[r].astype(f32)) + b8(scales, 1) * pixels3(bn[r])

    def prepare(r, acc):
        normed = (middle_of(r) - mean) * scale + b8(shifts, 6)
        n2[r] = pixels2(normed).astype(bf16)
        grad = (b8(scales, 3) * pixels3(ca[r].astype(f32))).astype(bf16)
        gr[r] = pixels2(grad)
        return acc + fold(grad.astype(f32))

    zero = jnp.zeros((SUB, channels), f32)
    sums_o[2] = lax.fori_loop(0, rows, prepare, zero)

    def chunk(f, _):
        base = pl.multiple_of(f * wide, wide)
        lanes = pl.ds(base, wide)
        group = f * parts

        def expand(r, _):
            mask = row_mask(meta, cm, r)[:, :, :LANE]
            value = dot(n2[r], w_e[:, lanes])
            value = low(value + jnp.broadcast_to(hshift[0:1, lanes], value.shape))
            for g in range(parts):
                em[g, r + 1] = mask * pixels3(value[:, g * LANE : (g + 1) * LANE])
            return 0

        lax.fori_loop(0, rows, expand, 0)

        def forward(r, acc):
            grad = dot(gr[r], w_rt[:, lanes])
            out = []
            for g in range(parts):
                conv = zeros_list(columns)
                for i in range(3):
                    taps = [khb[3 * i + j, group + g] for j in range(3)]
                    conv = add_row(conv, lambda c: em[g, r + i, c], taps, 1)
                here = pl.ds(pl.multiple_of(base + g * LANE, LANE), LANE)
                v = jnp.stack(conv) + jnp.broadcast_to(hshift[1:2, here], (SUB, LANE))
                phi_sum, bell = normal_parts(v)
                ha[r, :, here] = pixels2(v * phi_sum).astype(bf16)
                part = pixels3(grad[:, g * LANE : (g + 1) * LANE])
                back = low(part * (phi_sum + v * bell))
                gc[g, r + 1] = back
                out.append(acc[g] + fold(back))
            return tuple(out)

        bias = lax.fori_loop(0, rows, forward, tuple(zeros_list(parts)))
        for g in range(parts):
            here = pl.ds(pl.multiple_of(base + g * LANE, LANE), LANE)
            gh_o[1:2, here] = jnp.sum(bias[g], axis=0, keepdims=True)
            for tap in range(9):
                kacc[g, tap] = jnp.zeros((SUB, LANE), f32)

        def backward(r, acc):
            mask = row_mask(meta, cm, r)[:, :, :LANE]
            out = []
            for g in range(parts):
                conv = zeros_list(columns)
                for i in range(3):
                    taps = [kfb[3 * i + j, group + g] for j in range(3)]
                    sums = [kacc[g, 3 * i + j] for j in range(3)]
                    fixed = [em[g, r + 1, c] for c in range(columns)]
                    for c in range(columns):
                        value = gc[g, r + i, c]
                        for j in range(3):
                            at = c - (j - 1)
                            if 0 <= at < columns:
                                conv[at] = conv[at] + taps[j] * value
                                sums[j] = sums[j] + fixed[at] * value
                    for j in range(3):
                        kacc[g, 3 * i + j] = sums[j]
                here = pl.ds(pl.multiple_of(base + g * LANE, LANE), LANE)
                value = low(mask * jnp.stack(conv))
                ge[r, :, here] = pixels2(value).astype(bf16)
                out.append(acc[g] + fold(value))
            return tuple(out)

        bias = lax.fori_loop(0, rows, backward, tuple(zeros_list(parts)))
        for g in range(parts):
            here = pl.ds(pl.multiple_of(base + g * LANE, LANE), LANE)
            gh_o[0:1, here] = jnp.sum(bias[g], axis=0, keepdims=True)
            for tap in range(9):
                gk_o[8 - tap : 9 - tap, here] = jnp.sum(kacc[g, tap], axis=0, keepdims=True)
        return 0

    lax.fori_loop(0, hidden // wide, chunk, 0)

    whole = rows * px
    gwe_o[...] = dot_tn(n2[...].reshape(whole, channels), ge[...].reshape(whole, hidden))
    gwr_o[...] = dot_tn(gr[...].reshape(whole, channels), ha[...].reshape(whole, hidden))

    def finish(r, sums):
        mask = row_mask(meta, cm, r)
        reduced = pixels3(dot(ha[r], wr[...])) + b8(shifts, 7)
        middle = middle_of(r)
        res_o[r] = pixels2(mask * (middle + b8(scales, 3) * reduced))
        gn = pixels3(dot(ge[r], wet[...]))
        gn_o[r] = pixels2(gn)
        hat = (middle - mean) * rstd
        out = pixels3(ca[r].astype(f32))
        return sums[0] + fold(gn), sums[1] + fold(gn * hat), sums[2] + fold(out * reduced)

    sums = lax.fori_loop(0, rows, finish, (zero, zero, zero))
    sums_o[0] = sums[0]
    sums_o[1] = sums[1]
    sums_o[3] = sums[2]


def hidden_block(xa, ca, bn, meta, count, sums2, scales, shifts, hshift, w_e, w_rt, kh):
    rows, px, channels = xa.shape
    columns = px // SUB
    hidden = w_e.shape[1]
    groups = hidden // LANE
    parts = 2
    shape = jax.ShapeDtypeStruct
    return pl.pallas_call(
        hidden_kernel,
        name="hidden_block",
        out_shape=[
            shape((rows, px, channels), f32),
            shape((rows, px, channels), f32),
            shape((channels, hidden), f32),
            shape((channels, hidden), f32),
            shape((9, hidden), f32),
            shape((2, hidden), f32),
            shape((4, SUB, channels), f32),
        ],
        in_specs=[VMEM] * 12,
        out_specs=[VMEM] * 7,
        scratch_shapes=[
            pltpu.VMEM((columns, SUB, channels), f32),
            pltpu.VMEM((9, groups, SUB, LANE), f32),
            pltpu.VMEM((9, groups, SUB, LANE), f32),
            pltpu.VMEM((rows, px, channels), bf16),
            pltpu.VMEM((rows, px, channels), bf16),
            pltpu.VMEM((rows, px, hidden), bf16),
            pltpu.VMEM((rows, px, hidden), bf16),
            pltpu.VMEM((parts, rows + 2, columns, SUB, LANE), f32),
            pltpu.VMEM((parts, rows + 2, columns, SUB, LANE), f32),
            pltpu.VMEM((parts, 9, SUB, LANE), f32),
            pltpu.VMEM((hidden, channels), bf16),
            pltpu.VMEM((hidden, channels), bf16),
            pltpu.SemaphoreType.DMA((1,)),
        ],
        compiler_params=pltpu.CompilerParams(vmem_limit_bytes=60 * MIB),
    )(xa, ca, bn, meta, count, sums2, scales, shifts, hshift, w_e, w_rt, kh)


def back_kernel(
    gn, bn, xa, ca, gl, sl, c1, c2, gp, meta, count, sums1, sums2, sums3, scales, shifts,
    w_in, w_gate, w_out, kl, kd,
    mix_o, gwi_o, gwg_o, gwo_o, gkl_o, gkd_o, sums_o,
    cm, klb, kdb, gb, gg, gt, gm, tt, g2, g1, src, sem,
):
    rows, px, channels = xa.shape
    columns = px // SUB
    groups = groups_of(channels)
    make_col_mask(meta, cm)
    spread_taps(kl, klb, flip=True)
    spread_taps(kd, kdb, flip=True)
    for edge in (0, 1, rows + 2, rows + 3):
        g1[:, edge] = jnp.zeros(g1.shape[:1] + g1.shape[2:], f32)
    total = count[0:1, 0:1]
    mean1, rstd1 = statistics(sums1, total, 0)
    scale1 = rstd1 * b8(scales, 0)
    mean2, rstd2 = statistics(sums2, total, 0)
    scale2 = rstd2 * b8(scales, 2)
    back0 = b8(sums3, 0) / total
    back1 = b8(sums3, 1) / total
    zero = jnp.zeros((SUB, channels), f32)

    def first(r, sums):
        mask = row_mask(meta, cm, r)
        both = pixels3(bn[r])
        middle = pixels3(xa[r].astype(f32)) + b8(scales, 1) * both
        hat = (middle - mean2) * rstd2
        grad = pixels3(ca[r].astype(f32)) + scale2 * (
            pixels3(gn[r]) - mask * (back0 + hat * back1)
        )
        gm[r] = pixels2(grad)
        branch = (b8(scales, 1) * grad).astype(bf16)
        gb[r] = pixels2(branch)
        gated_grad = dot_nt(pixels2(branch), w_out[...])
        gelu = gl[r].astype(f32)
        gate_grad = (gated_grad * gelu).astype(bf16)
        gg[r] = gate_grad
        gt[r] = (gelu * gp[r]).astype(bf16)
        tt[r] = gated_grad * gp[r]
        conv = low(dot_nt(gate_grad, w_gate[...]))
        for g, width in groups:
            g2[g, r, :, :, :width] = pixels3(conv[:, g * LANE : g * LANE + width])
            src[g, r, :, :, :width] = pixels3(c1[r, :, g * LANE : g * LANE + width].astype(f32))
        return (
            sums[0] + fold(grad * both),
            sums[1] + fold(branch.astype(f32)),
            sums[2] + fold(pixels3(gate_grad.astype(f32))),
            sums[3] + fold(pixels3(conv)),
        )

    sums = lax.fori_loop(0, rows, first, (zero,) * 4)
    for k in range(4):
        sums_o[2 + k] = sums[k]
    whole = rows * px
    flat = lambda ref: ref[...].reshape(whole, channels)
    gwo_o[...] = dot_tn(flat(gt), flat(gb))
    gwg_o[...] = dot_tn(flat(c2), flat(gg))

    for g, width in groups:
        for i in range(7):
            first_row = max(0, 3 * (3 - i))
            last_row = min(rows, rows - 3 * (i - 3))

            def taps_row(r, acc, g=g, i=i):
                at = r + (i - 3) * 3
                return tap_sums(
                    list(acc), (lambda c: g2[g, r, c], columns), lambda c: src[g, at, c], 3
                )

            acc = lax.fori_loop(first_row, last_row, taps_row, zeros_list(7))
            for j in range(7):
                row = jnp.sum(acc[j], axis=0, keepdims=True)
                gkd_o[7 * i + j : 7 * i + j + 1, g * LANE : g * LANE + width] = row[:, :width]

    def dilated(r, sums):
        mask = row_mask(meta, cm, r)
        low_i, high_i = row_range(r, rows, 3, 3)
        out = []
        for g, width in groups:

            def tap_row(i, acc):
                taps = [kdb[7 * i + j, g] for j in range(7)]
                at = r + (i - 3) * 3
                return add_row(list(acc), lambda c: g2[g, at, c], taps, 3)

            acc = lax.fori_loop(low_i, high_i, tap_row, zeros_list(columns))
            value = low(mask[:, :, :width] * jnp.stack(acc)[:, :, :width])
            g1[g, r + 2, :, :, :width] = value
            out.append(sums[g] + fold(value))
        return tuple(out)

    start = tuple(jnp.zeros((SUB, width), f32) for g, width in groups)
    sums = lax.fori_loop(0, rows, dilated, start)
    for g, width in groups:
        sums_o[6, :, g * LANE : g * LANE + width] = sums[g]

    def refill(r, _):
        for g, width in groups:
            src[g, r, :, :, :width] = pixels3(gl[r, :, g * LANE : g * LANE + width].astype(f32))
        return 0

    lax.fori_loop(0, rows, refill, 0)

    for g, width in groups:
        for i in range(5):

            def taps_row(r, acc, g=g, i=i):
                return tap_sums(
                    list(acc), (lambda c: src[g, r, c], columns), lambda c: g1[g, r + i, c], 1
                )

            acc = lax.fori_loop(0, rows, taps_row, zeros_list(5))
            for j in range(5):
                tap = 24 - (5 * i + j)
                row = jnp.sum(acc[j], axis=0, keepdims=True)
                gkl_o[tap : tap + 1, g * LANE : g * LANE + width] = row[:, :width]

    def local(r, sums):
        mask = row_mask(meta, cm, r)
        parts = []
        for g, width in groups:
            acc = zeros_list(columns)
            for i in range(5):
                taps = [klb[5 * i + j, g] for j in range(5)]
                acc = add_row(acc, lambda c: g1[g, r + i, c], taps, 1)
            value = mask[:, :, :width] * jnp.stack(acc)[:, :, :width]
            at = slice(g * LANE, g * LANE + width)
            grad = (tt[r, :, at] + pixels2(value)) * sl[r, :, at]
            gg[r, :, at] = grad.astype(bf16)
            parts.append(sums[g] + fold(pixels3(low(grad))))
        return tuple(parts)

    sums = lax.fori_loop(0, rows, local, start)
    for g, width in groups:
        sums_o[7, :, g * LANE : g * LANE + width] = sums[g]

    def last(r, sums):
        x = pixels3(xa[r].astype(f32))
        grad = pixels3(gm[r])
        gn1 = pixels3(dot_nt(gg[r], w_in[...])) + b8(scales, 1) * grad
        mix_o[r] = pixels2(grad + scale1 * gn1)
        hat = (x - mean1) * rstd1
        normed = (x - mean1) * scale1 + b8(shifts, 0)
        gb[r] = pixels2(normed).astype(bf16)
        return sums[0] + fold(gn1), sums[1] + fold(gn1 * hat)

    sums = lax.fori_loop(0, rows, last, (zero, zero))
    sums_o[0] = sums[0]
    sums_o[1] = sums[1]
    gwi_o[...] = dot_tn(flat(gb), flat(gg))


def mixer_back(gn, bn, xa, ca, gl, sl, c1, c2, gp, meta, count, sums1, sums2, sums3, scales,
               shifts, w_in, w_gate, w_out, kl, kd):
    rows, px, channels = xa.shape
    columns = px // SUB
    n = len(groups_of(channels))
    small = (rows, px, channels)
    shape = jax.ShapeDtypeStruct
    square = shape((channels, channels), f32)
    return pl.pallas_call(
        back_kernel,
        name="mixer_back",
        out_shape=[
            shape(small, f32), square, square, square,
            shape((25, channels), f32), shape((49, channels), f32), shape((8, SUB, channels), f32),
        ],
        in_specs=[VMEM] * 21,
        out_specs=[VMEM] * 7,
        scratch_shapes=[
            pltpu.VMEM((columns, SUB, channels), f32),
            pltpu.VMEM((25, n, SUB, LANE), f32),
            pltpu.VMEM((49, n, SUB, LANE), f32),
            pltpu.VMEM(small, bf16),
            pltpu.VMEM(small, bf16),
            pltpu.VMEM(small, bf16),
            pltpu.VMEM(small, f32),
            pltpu.VMEM(small, f32),
            pltpu.VMEM((n, rows, columns, SUB, LANE), f32),
            pltpu.VMEM((n, rows + 4, columns, SUB, LANE), f32),
            pltpu.VMEM((n, rows, columns, SUB, LANE), f32),
            pltpu.SemaphoreType.DMA((1,)),
        ],
        compiler_params=pltpu.CompilerParams(vmem_limit_bytes=62 * MIB),
    )(gn, bn, xa, ca, gl, sl, c1, c2, gp, meta, count, sums1, sums2, sums3, scales, shifts,
      w_in, w_gate, w_out, kl, kd)


def input_kernel(mix, xa, meta, count, sums1, sums4, scales, out, cm, al):
    rows, px, channels = xa.shape
    make_col_mask(meta, cm)
    total = count[0:1, 0:1]
    mean1, rstd1 = statistics(sums1, total, 0)
    scale1 = rstd1 * b8(scales, 0)
    back0 = b8(sums4, 0) / total
    back1 = b8(sums4, 1) / total

    def one(r, _):
        mask = row_mask(meta, cm, r)
        hat = (pixels3(xa[r].astype(f32)) - mean1) * rstd1
        grad = mask * (pixels3(mix[r]) - scale1 * (back0 + hat * back1))
        al[r] = pixels2(grad)
        return 0

    lax.fori_loop(0, rows, one, 0)
    unalign(al, meta, out)


def unalign(al, meta, out):
    rows, px, channels = al.shape
    offsets = out.shape[0] - rows + 1
    for at in range(out.shape[0]):
        value = jnp.zeros((px // SUB, SUB, channels), f32)
        for t in range(offsets):
            if 0 <= at - t < rows:
                chosen = (meta[0] == float(t))[None]
                value = jnp.where(chosen, pixels3(al[at - t]), value)
        out[at] = pixels2(value)


def input_grad_kernel(mix, xa, meta, count, sums1, sums4, scales, band):
    rows, px, channels = xa.shape
    return pl.pallas_call(
        input_kernel,
        name="input_grad",
        out_shape=jax.ShapeDtypeStruct((band, px, channels), f32),
        in_specs=[VMEM] * 7,
        out_specs=VMEM,
        scratch_shapes=[
            pltpu.VMEM((px // SUB, SUB, channels), f32),
            pltpu.VMEM((rows, px, channels), f32),
        ],
        compiler_params=pltpu.CompilerParams(vmem_limit_bytes=56 * MIB),
    )(mix, xa, meta, count, sums1, sums4, scales)


def unalign_kernel(res, meta, out):
    unalign(res, meta, out)


def unaligned(res, meta, band):
    rows, px, channels = res.shape
    return pl.pallas_call(
        unalign_kernel,
        name="unalign",
        out_shape=jax.ShapeDtypeStruct((band, px, channels), f32),
        in_specs=[VMEM] * 2,
        out_specs=VMEM,
        compiler_params=pltpu.CompilerParams(vmem_limit_bytes=56 * MIB),
    )(res, meta)


def reduce_kernel(stages, v_ref, out_ref, mine, *rest):
    slots, sems = rest[: len(stages)], rest[len(stages) :]
    core = lax.axis_index("rows")
    chip = lax.axis_index("imgs")
    barrier = pltpu.get_barrier_semaphore()
    peers = []
    for axis, stride, size in stages:
        place = lax.rem((core if axis == "rows" else chip) // stride, size)
        stage = []
        for step in range(1, size):
            other = lax.rem(place + step, size)
            index = (core if axis == "rows" else chip) + (other - place) * stride
            stage.append((step, (index, chip) if axis == "rows" else (core, index)))
        peers.append(stage)
    for stage in peers:
        for step, device in stage:
            pl.semaphore_signal(barrier, inc=1, device_id=device, device_id_type=MESH)
    pl.semaphore_wait(barrier, sum(len(stage) for stage in peers))
    mine[...] = jnp.sum(v_ref[...], axis=1)
    for k, stage in enumerate(peers):
        slot, (send, recv) = slots[k], sems[2 * k : 2 * k + 2]
        copies = []
        for step, device in stage:
            copies.append(
                pltpu.make_async_remote_copy(
                    src_ref=mine,
                    dst_ref=slot.at[step - 1],
                    send_sem=send.at[step - 1],
                    recv_sem=recv.at[step - 1],
                    device_id=device,
                    device_id_type=MESH,
                )
            )
            copies[-1].start()
        for copy in copies:
            copy.wait()
        total = mine[...]
        for step, device in stage:
            total = total + slot[step - 1]
        mine[...] = total
    out_ref[...] = mine[...]


def reduce_all(v, sizes, collective_id):
    k, _, channels = v.shape
    stages = [("rows", 1, sizes["rows"])]
    left, stride = sizes["imgs"], 1
    while left > 1:
        size = 4 if left % 4 == 0 else (2 if left % 2 == 0 else left)
        stages.append(("imgs", stride, size))
        left, stride = left // size, stride * size
    stages = [s for s in stages if s[2] > 1]
    table = (k, channels)
    sems = []
    for _, _, size in stages:
        sems += [pltpu.SemaphoreType.DMA((size - 1,))] * 2
    return pl.pallas_call(
        functools.partial(reduce_kernel, stages),
        name="reduce_all",
        out_shape=jax.ShapeDtypeStruct(table, f32),
        in_specs=[VMEM],
        out_specs=VMEM,
        scratch_shapes=[pltpu.VMEM(table, f32)]
        + [pltpu.VMEM((size - 1,) + table, f32) for _, _, size in stages]
        + sems,
        compiler_params=pltpu.CompilerParams(collective_id=collective_id, has_side_effects=True),
    )(v)


def halves(values, core, half, axis):
    mine = lax.dynamic_slice_in_dim(values, core * half, half, axis=axis)
    other = lax.dynamic_slice_in_dim(values, (1 - core) * half, half, axis=axis)
    return mine, lax.ppermute(other, "rows", [(0, 1), (1, 0)])


def first_sums_kernel(x, meta, out, cm):
    rows, columns, images, channels = x.shape
    size, top = meta[2], meta[0]
    for c in range(columns):
        cm[c] = (size > c).astype(f32)

    def one(r, sums):
        at = (r * 1).astype(f32)
        inside = ((at >= top) & (at < top + size)).astype(f32)
        value = cm[...] * inside[None] * x[r].astype(f32)
        return sums[0] + fold(value), sums[1] + fold(value * value)

    zero = jnp.zeros((images, channels), f32)
    sums = lax.fori_loop(0, rows, one, (zero, zero))
    for k in range(2):
        out[k] = sums[k][:SUB] + sums[k][SUB:]


def first_sums(x, meta):
    rows, columns, images, channels = x.shape
    return pl.pallas_call(
        first_sums_kernel,
        name="first_sums",
        out_shape=jax.ShapeDtypeStruct((2, SUB, channels), f32),
        in_specs=[VMEM] * 2,
        out_specs=VMEM,
        scratch_shapes=[pltpu.VMEM((columns, images, channels), f32)],
        compiler_params=pltpu.CompilerParams(vmem_limit_bytes=32 * MIB),
    )(x, meta)


def on_device(sizes, inputs, cotangent, scales, shifts, hidden_shift, w_inward, w_gating,
              w_outward, w_expand, w_reduce, kernel_local, kernel_dilated, kernel_hidden,
              image_size, band_split, slot_image):
    images, band, columns, channels = inputs.shape
    half = images // 2
    px = columns * half
    core = lax.axis_index("rows")
    counted = jnp.sum(image_size * image_size).astype(f32)
    count = jnp.full((SUB, LANE), counted)
    everyone = jnp.arange(image_size.shape[0], dtype=jnp.int32)
    chosen = (slot_image[:, None] == everyone[None, :]).astype(jnp.int32)
    extent = jnp.sum(chosen * image_size[None, :], axis=1)
    top = band - jnp.sum(chosen * band_split[None, :], axis=1)
    start = jnp.clip(top, 0, 2 * band - columns)
    own_meta = jnp.stack([top - core * band, top, extent]).astype(f32)
    own_meta = jnp.broadcast_to(own_meta[:, :, None], (3, images, channels))
    meta = jnp.stack([start, top - start, extent]).astype(f32)
    meta = lax.dynamic_slice_in_dim(meta, core * half, half, axis=1)
    meta = jnp.broadcast_to(meta[:, :, None], (3, half, channels))

    x = jnp.transpose(inputs, (1, 2, 0, 3))
    y = jnp.transpose(cotangent, (1, 2, 0, 3))
    sums1 = reduce_all(first_sums(x, own_meta), sizes, 1)

    def gather_rows(v):
        mine, theirs = halves(v, core, half, 2)
        upper = jnp.where(core == 0, mine, theirs)
        lower = jnp.where(core == 0, theirs, mine)
        return jnp.concatenate([upper, lower], axis=0).reshape(2 * band, px, channels)

    xw, cw = gather_rows(x), gather_rows(y)
    xa, ca, gl, sl, c1, c2, gp, bn, part2 = mixer_forward(
        xw, cw, meta, count, sums1, scales, shifts, w_inward, w_gating, w_outward,
        kernel_local, kernel_dilated,
    )
    sums2 = reduce_all(part2, sizes, 2)
    res, gn, gwe, gwr, gk, gh, part3 = hidden_block(
        xa, ca, bn, meta, count, sums2, scales, shifts, hidden_shift, w_expand, w_reduce.T,
        kernel_hidden,
    )
    sums3 = reduce_all(part3, sizes, 3)
    mix, gwi, gwg, gwo, gkl, gkd, part4 = mixer_back(
        gn, bn, xa, ca, gl, sl, c1, c2, gp, meta, count, sums1, sums2, sums3, scales, shifts,
        w_inward, w_gating, w_outward, kernel_local, kernel_dilated,
    )
    sums4 = reduce_all(part4, sizes, 4)

    def scatter_rows(v):
        v = v.reshape(2 * band, columns, half, channels)
        mine = lax.dynamic_slice_in_dim(v, core * band, band, axis=0)
        other = lax.dynamic_slice_in_dim(v, (1 - core) * band, band, axis=0)
        theirs = lax.ppermute(other, "rows", [(0, 1), (1, 0)])
        lower = jnp.where(core == 0, mine, theirs)
        upper = jnp.where(core == 0, theirs, mine)
        both = jnp.concatenate([lower, upper], axis=2)
        return jnp.transpose(both, (2, 0, 1, 3))

    result = scatter_rows(unaligned(res, meta, 2 * band))
    input_grad = scatter_rows(
        input_grad_kernel(mix, xa, meta, count, sums1, sums4, scales, 2 * band)
    )
    gwe, gwr, gk, gh, gwi, gwg, gwo, gkl, gkd = lax.psum(
        (gwe, gwr, gk, gh, gwi, gwg, gwo, gkl, gkd), ("rows", "imgs")
    )
    scales_grad = jnp.stack([sums4[1], sums4[2], sums3[1], sums3[3]])
    shifts_grad = jnp.stack(
        [sums4[0], sums4[7], sums4[6], sums4[5], sums4[4], sums4[3], sums3[0], sums3[2]]
    )
    return (
        result, input_grad, scales_grad, shifts_grad, gh, gwi, gwg, gwo, gwe, gwr.T,
        gkl, gkd, gk,
    )


def solution(mesh):
    wide = P("imgs", "rows", None, None)
    sizes = dict(mesh.shape)
    return jax.shard_map(
        functools.partial(on_device, sizes),
        mesh=mesh,
        in_specs=(wide, wide) + (P(),) * 13 + (P("imgs"),),
        out_specs=(wide, wide) + (P(),) * 11,
        check_vma=False,
    )
```

time: 1530 us -> 581 us (0.38)
  other arithmetic: 763 us -> 19.1 us
  Pallas kernels: 0 us -> 254 us
  matrix products: 245 us -> 0 us
  blocking collectives: 132 us -> 0 us
  local copies, waits for them, and re-layouts: 64.4 us -> 23.5 us
  starting transfers between devices: 31.4 us -> 1.1 us
    reduce_sum x11 -> x2, other arithmetic: 410 us -> 0.82 us  [the longest x1 0.63 us: on_device(): counted = jnp.sum(image_size * image_size).astype(f32)]
    convert_element_type x8 -> x1, other arithmetic: 276 us -> 0.01 us  [on_device(): own_meta = jnp.stack([top - core * band, top, extent]).astype(f32)]
    pallas_call x0 -> x10, Pallas kernels: none -> 254 us  [the longest x1 90.2 us: hidden_block(): pl.pallas_call(hidden_kernel, name='hidden_block', out_shape=[shape((rows...]
    dot_general x15 -> x0, matrix products: 245 us -> none  [the longest x5 144 us: back_matmul(): jnp.einsum('irwn,kn->irwk', gradient, weight, preferred_element_type=jnp....]
    psum x3 -> x0, blocking collectives: 132 us -> none  [the longest x1 49.8 us: on_device(): lax.psum((pixel_sum(middle_masked), pixel_sum(middle_masked * middle_mask...]
    select_n x1 -> x3, other arithmetic: 67.1 us -> 8.19 us  [the longest x1 4.68 us: scatter_rows(): lower = jnp.where(core == 0, mine, theirs)]
    ppermute x12 -> x4, starting transfers between devices: 31.3 us -> 1.02 us  [the longest x2 0.51 us: scatter_rows(): theirs = lax.ppermute(other, 'rows', [(0, 1), (1, 0)])]
    slice x26 -> x3, local copies, waits for them, and re-layouts: 18 us -> 0.02 us  [the longest x1 0.01 us: on_device(): sums4[3]]
  transfers between devices with their start and end apart: 14 -> 6, of which waited for: 5 -> 3; matrix products, arithmetic and copies ran while one was open for 5% -> 3% of each run, Pallas kernels for 0% -> 3%
where the time goes in v1:
time: 581 us; the launch traced here: 580 us
  waiting for transfers between devices  268 us (46%)
  Pallas kernels  254 us (44%)
  local copies, waits for them, and re-layouts  23.5 us (4%)
  other arithmetic  19.1 us (3%)
  between operations  14.9 us (3%)
    psum x2, waiting for transfers between devices, on_device(): lax.psum((gwe, gwr, gk, gh, gwi, gwg, gwo, gkl, gkd), ('rows', 'imgs'))  262 us
    pallas_call x1, Pallas kernels, hidden_block(): pl.pallas_call(hidden_kernel, name='hidden_block', out_shape=[shape((rows...  90.2 us
    pallas_call x1, Pallas kernels, mixer_back(): pl.pallas_call(back_kernel, name='mixer_back', out_shape=[shape(small, f3...  60.7 us
    pallas_call x4, Pallas kernels, reduce_all(): pl.pallas_call(functools.partial(reduce_kernel, stages), name='reduce_all...  47.5 us
    pallas_call x1, Pallas kernels, mixer_forward(): pl.pallas_call(mixer_kernel, name='mixer_forward', out_shape=[jax.ShapeDt...  41 us
    unnamed x39, local copies, waits for them, and re-layouts  14.7 us
  transfers between devices with their start and end apart: 6, of which 3 were waited for; matrix products, arithmetic and copies ran while one was open for 3% of the time, Pallas kernels for 3%

profile of v1, /device:TPU:0, one launch (start us, length us, event | category | flops | bytes accessed | tf_op | source)
XLA Modules:
  0.0 580.3 jit_solution(16475598552509448640)
XLA Ops:
  7.3 2.6 dynamic-slice_bitcast_fusion.1
  9.9 0.5 collective-permute-start
  10.3 2.4 dynamic-slice_bitcast_fusion
  12.7 0.1 collective-permute-start.1
  12.8 0.2 select_reduce_fusion.1
  13.0 0.6 multiply_reduce_fusion
  14.3 0.1 broadcast_in_dim.8.meta
  14.4 1.5 first_sums.1.v_ref
  16.0 0.6 copy-done.1
  16.6 13.6 %reduce_all.4.sums1 = f32[2,320]{1,0:T(2,128)} custom-call(f32[2,8,320]{2,1,0:T(8,128)} %copy-done.1), custom_call_target="tpu_custom_call" | custom-call | tf_op jit(solution)/shard_map/reduce_all/pallas_call | solution.py:744
  30.2 0.1 constant_dynamic-slice_fusion.2
  30.2 1.7 bitcast_select_fusion.3
  32.0 1.9 maximum_bitcast_fusion.2.xw
  33.9 0.5 copy-done.4
  34.4 1.8 bitcast_select_fusion.1
  36.1 1.9 maximum_bitcast_fusion.3.cw
  38.1 0.6 broadcast_in_dim.7.count
  38.7 0.7 broadcast_in_dim.6.meta
  39.3 41.0 %mixer_forward.1 = (bf16[18,144,320]{2,1,0:T(8,128)(2,1)}, bf16[18,144,320]{2,1,0:T(8,128)(2,1)}, bf16[18,144,320]{2,1,0:T(8,128)(2,1)}, f32[18,144,320]{2,1,0:T...) custom-call(bf16[22,144,320]{2,1,0:T(8,128)(2,1)} %maximum_bitcast_f, ...), custom_call_target="tpu_custom_call" | custom-call | tf_op jit(solution)/shard_map/mixer_forward/pallas_call | solution.py:243
  80.3 11.7 %reduce_all.5.sums2 = f32[2,320]{1,0:T(2,128)} custom-call(f32[2,8,320]{2,1,0:T(8,128)} %get-tuple-element.39.v_ref), custom_call_target="tpu_custom_call" | custom-call | tf_op jit(solution)/shard_map/reduce_all/pallas_call | solution.py:744
  92.0 90.2 %hidden_block.1 = (f32[18,144,320]{2,1,0:T(8,128)}, f32[18,144,320]{2,1,0:T(8,128)}, f32[320,1280]{1,0:T(8,128)}, f32[320,1280]{1,0:T(8,128)}, f32[9,1280]{1,0:T...) custom-call(bf16[18,144,320]{2,1,0:T(8,128)(2,1)} %get-tuple-element.36.xa, ...), custom_call_target="tpu_custom_call" | custom-call | tf_op jit(solution)/shard_map/hidden_block/pallas_call | solution.py:402
  182.2 10.2 %reduce_all.6.sums3 = f32[4,320]{1,0:T(4,128)} custom-call(f32[4,8,320]{2,1,0:T(8,128)} %get-tuple-element.47.v_ref), custom_call_target="tpu_custom_call" | custom-call | tf_op jit(solution)/shard_map/reduce_all/pallas_call | solution.py:744
  192.4 60.7 %mixer_back.1 = (f32[18,144,320]{2,1,0:T(8,128)}, f32[320,320]{1,0:T(8,128)}, f32[320,320]{1,0:T(8,128)}, f32[320,320]{1,0:T(8,128)}, f32[25,320]{1,0:T(8,128)},...) custom-call(f32[18,144,320]{2,1,0:T(8,128)} %get-tuple-element.41.gn, f32[18,144,320]{2,1,0:T(8,128)} %get-tuple-element.38.bn, ...), custom_call_target="tpu_custom_call" | custom-call | tf_op jit(solution)/shard_map/mixer_back/pallas_call | solution.py:596
  253.2 12.0 %reduce_all.7.sums4 = f32[8,320]{1,0:T(8,128)} custom-call(f32[8,8,320]{2,1,0:T(8,128)} %get-tuple-element.49.v_ref), custom_call_target="tpu_custom_call" | custom-call | tf_op jit(solution)/shard_map/reduce_all/pallas_call | solution.py:744
  265.2 5.2 unalign.1
  270.5 7.4 %input_grad.1 = f32[22,144,320]{2,1,0:T(8,128)} custom-call(f32[18,144,320]{2,1,0:T(8,128)} %get-tuple-element.48.mix, bf16[18,144,320]{2,1,0:T(8,128)(2,1)} %get-tuple-element.36.xa, f32[3,8,320]{2,1,0:T(8,128)} %broadcast_in_dim.6.meta, f32[8,128]{1,0:T(8,128)} %broadcast_in_dim.7.count, f32[2,320]{1,0:T(2,128)} %reduce_all.4.sums1, ...), custom_call_target="tpu_custom_call" | custom-call | tf_op jit(solution)/shard_map/input_grad/pallas_call | solution.py:658
  277.9 0.2 constant_dynamic-slice_fusion.1
  278.1 2.2 copy-done.3
  280.3 1.6 constant_dynamic-slice_fusion
  281.9 0.5 collective-permute-start.2
  282.5 0.7 all-reduce.7.cloned.1.call-update
  283.3 0.6 stack.25
  283.9 0.6 pad_maximum_fusion
  284.5 5.8 %collective-permute-done.3 = f32[11,18,8,320]{3,2,1,0:T(8,128)} collective-permute-done((f32[11,18,8,320]{3,2,1,0:T(8,128)}, f32[11,18,8,320]{3,2,1,0:T(8,128)}, u32[]{:S(2)}, u32[]{:S(2)}) %collective-permute-start.3) | collective-permute-done | bytes 2027552 | tf_op jit(solution)/shard_map/ppermute | solution.py:845
  290.3 4.7 dynamic-slice_select_fusion.1
  295.0 2.8 maximum_bitcast_fusion.1
  297.8 2.8 maximum_bitcast_fusion
  300.7 106.0 %all-reduce.5.cloned.1.call-done = (f32[2,1280]{1,0:T(2,128)}, f32[25,320]{1,0:T(8,128)}, f32[49,320]{1,0:T(8,128)}, f32[9,1280]{1,0:T(8,128)}) async-done(((f32[2,1280]{1,0:T(2,128)}, f32[25,320]{1,0:T(8,128)}, f32[49,320]{1,0:T(8,128)}, f32[9,1280]{1,0:T(8,128)}), (f32[2,1280]{1,0:T(2,128)}, f32[25,320]{1,0:T(8,128)}, f32[49,320]{1,0:T(8,128)}, f32[9,1280]{1,0:T(8,128)})) %all-reduce.5.cloned.1.call-update) | async-done | bytes 151056 | tf_op jit(solution)/shard_map/psum | solution.py:855
  406.7 155.5 %all-reduce.7.cloned.1.call-done = (f32[320,320]{1,0:T(8,128)}, f32[320,320]{1,0:T(8,128)}, f32[320,320]{1,0:T(8,128)}, f32[320,1280]{1,0:T(8,128)}, f32[1280,320]{0,1:T(8,128)}) async-done(((f32[320,320]{1,0:T(8,128)}, f32[320,320]{1,0:T(8,128)}, f32[320,320]{1,0:T(8,128)}, f32[320,1280]{1,0:T(8,128)}, f32[1280,320]{0,1:T(8,128)}), (f32[320,320]{1,0:T(8,128)}, f32[320,320]{1,0:T(8,128)}, ...) | async-done | bytes 4505616 | tf_op jit(solution)/shard_map/psum | solution.py:855
  562.2 1.4 copy.38
  563.6 1.8 copy.39
  565.5 2.0 copy.40
  567.4 1.8 copy.41
  569.3 1.2 copy.42
  570.4 1.2 copy.43
  571.6 0.6 copy.44
  572.2 0.6 copy.45
  572.9 0.6 copy.46
  (40 shorter events, 0.2 us)
Async XLA Ops:
  7.2 399.5 %all-reduce.5.cloned.1.call-start = ((), (), s32[]{:S(2)}) async-start(), calls=%async_computation | async-start | bytes 454656 | tf_op jit(solution)/shard_map/psum | solution.py:855
  7.2 5.6 copy-start.12
  7.2 5.6 copy-start.13
  7.3 5.6 copy-start.14
  7.3 7.1 %copy-start = (bf16[16,11,18,320]{3,0,2,1:T(8,128)(2,1)S(1)}, bf16[16,11,18,320]{3,0,2,1:T(8,128)(2,1)}, u32[]{:S(2)}) copy-start(bf16[16,11,18,320]{3,0,2,1:T(8,128)(2,1)} %param.16) | copy-start | bytes 6082564
  9.9 20.4 %collective-permute-start = (bf16[11,18,8,320]{3,2,1,0:T(8,128)(2,1)}, bf16[11,18,8,320]{3,2,1,0:T(8,128)(2,1)}, u32[]{:S(2)}, u32[]{:S(2)}) collective-permute-start(bf16[11,18,8,320]{3,2,1,0:T(8,128)(2,1)} %dynamic-slice_bitcast_fusion.1), channel_id=1, source_target_pairs={{0,16},{16,0},{1,17},{17,1},{2,18},{18,2},{3,19},{19,3},{4,20},{20... | collective-permute-start | bytes 3041288 | tf_op jit(solution)/shard_map/ppermute | solution.py:760
  12.7 21.2 %collective-permute-start.1 = (bf16[11,18,8,320]{3,2,1,0:T(8,128)(2,1)}, bf16[11,18,8,320]{3,2,1,0:T(8,128)(2,1)}, u32[]{:S(2)}, u32[]{:S(2)}) collective-permute-start(bf16[11,18,8,320]{3,2,1,0:T(8,128)(2,1)} %dynamic-slice_bitcast_fusion), channel_id=1, source_target_pairs={{0,16},{16,0},{1,17},{17,1},{2,18},{18,2},{3,19},{19,3},{4,20},{20... | collective-permute-start | bytes 3041288 | tf_op jit(solution)/shard_map/ppermute | solution.py:760
  15.9 0.6 copy-start.1
  32.0 2.4 copy-start.4
  270.5 7.4 %copy-start.2 = (f32[22,144,320]{2,1,0:T(8,128)S(1)}, f32[22,144,320]{2,1,0:T(8,128)}, u32[]{:S(2)}) copy-start(f32[22,144,320]{2,1,0:T(8,128)} %unalign.1) | copy-start | bytes 12165124
  277.9 2.4 copy-start.3
  281.9 8.4 %collective-permute-start.3 = (f32[11,18,8,320]{3,2,1,0:T(8,128)}, f32[11,18,8,320]{3,2,1,0:T(8,128)}, u32[]{:S(2)}, u32[]{:S(2)}) collective-permute-start(f32[11,18,8,320]{3,2,1,0:T(8,128)} %constant_dynamic-slice_fusion), channel_id=1, source_target_pairs={{0,16},{16,0},{1,17},{17,1},{2,18},{18,2},{3,19},{19,3},{4,20},{20... | collective-permute-start | bytes 6082568 | tf_op jit(solution)/shard_map/ppermute | solution.py:845
  281.9 8.4 %collective-permute-start.2 = (f32[11,18,8,320]{3,2,1,0:T(8,128)S(1)}, f32[11,18,8,320]{3,2,1,0:T(8,128)}, u32[]{:S(2)}, u32[]{:S(2)}) collective-permute-start(f32[11,18,8,320]{3,2,1,0:T(8,128)S(1)} %constant_dynamic-slice_fusion.1), channel_id=1, source_target_pairs={{0,16},{16,0},{1,17},{17,1},{2,18},{18,2},{3,19},{19,3},{4,20},{20... | collective-permute-start | bytes 6082568 | tf_op jit(solution)/shard_map/ppermute | solution.py:845
  282.4 0.8 copy-start.7
  282.4 0.8 copy-start.10
  282.4 279.8 %all-reduce.7.cloned.1.call-start = ((), (), s32[]{:S(2)}) async-start(), calls=%async_computation.1 | async-start | bytes 9502720 | tf_op jit(solution)/shard_map/psum | solution.py:855
  562.2 7.1 %copy-start.6 = (f32[320,1280]{1,0:T(8,128)S(1)}, f32[320,1280]{1,0:T(8,128)}, u32[]{:S(2)}) copy-start(f32[320,1280]{1,0:T(8,128)} %get-tuple-element.103) | copy-start | bytes 4915204
  565.5 5.0 copy-start.5
  570.4 1.2 copy-start.11
  570.4 1.8 copy-start.8
  570.4 2.4 copy-start.9
Sparse Core Ops, SparseCore 0:
  282.5 124.1 all-reduce.4
  414.3 147.8 all-reduce.6

commit v2 on v1

--- a/solution.py
+++ b/solution.py
@@ -1,4 +1,5 @@
 import functools
+import math
 
 import jax
 import jax.numpy as jnp
@@ -125,11 +126,109 @@
     return mean, lax.rsqrt(b8(sums, i + 1) / count - mean * mean + epsilon)
 
 
+def stage_list(sizes):
+    stages = [("rows", 1, sizes["rows"])]
+    left, stride = sizes["imgs"], 1
+    while left > 1:
+        size = 4 if left % 4 == 0 else (2 if left % 2 == 0 else left)
+        stages.append(("imgs", stride, size))
+        left, stride = left // size, stride * size
+    return [s for s in stages if s[2] > 1]
+
+
+def stage_peers(stages):
+    core = lax.axis_index("rows")
+    chip = lax.axis_index("imgs")
+    found = []
+    for axis, stride, size in stages:
+        index = core if axis == "rows" else chip
+        place = lax.rem(index // stride, size)
+        peers = []
+        for step in range(1, size):
+            other = lax.rem(place + step, size)
+            at = index + (other - place) * stride
+            peers.append((step, other, (at, chip) if axis == "rows" else (core, at)))
+        found.append((place, peers))
+    return found
+
+
+def say_here(found):
+    barrier = pltpu.get_barrier_semaphore()
+    for _, peers in found:
+        for _, _, device in peers:
+            pl.semaphore_signal(barrier, inc=1, device_id=device, device_id_type=MESH)
+
+
+def wait_all_here(found):
+    pl.semaphore_wait(pltpu.get_barrier_semaphore(), sum(len(peers) for _, peers in found))
+
+
+def greet(found):
+    say_here(found)
+    wait_all_here(found)
+
+
+def remote(src, dst, send, recv, device):
+    return pltpu.make_async_remote_copy(
+        src_ref=src, dst_ref=dst, send_sem=send, recv_sem=recv,
+        device_id=device, device_id_type=MESH,
+    )
+
+
+def all_sum(mine, slots, sems, found):
+    for k, (_, peers) in enumerate(found):
+        slot, (send, recv) = slots[k], sems[2 * k : 2 * k + 2]
+        copies = []
+        for step, _, device in peers:
+            copies.append(
+                remote(mine, slot.at[step - 1], send.at[step - 1], recv.at[step - 1], device)
+            )
+            copies[-1].start()
+        for copy in copies:
+            copy.wait()
+        total = mine[...]
+        for step, _, _ in peers:
+            total = total + slot[step - 1]
+        mine[...] = total
+
+
+def sum_scratch(stages, table):
+    sems = []
+    for _, _, size in stages:
+        sems += [pltpu.SemaphoreType.DMA((size - 1,))] * 2
+    slots = [pltpu.VMEM((size - 1,) + table, f32) for _, _, size in stages]
+    return [pltpu.VMEM(table, f32)] + slots + sems
+
+
+def reduce_kernel(stages, v_ref, out_ref, mine, *rest):
+    found = stage_peers(stages)
+    greet(found)
+    mine[...] = jnp.sum(v_ref[...], axis=1)
+    all_sum(mine, rest[: len(stages)], rest[len(stages) :], found)
+    out_ref[...] = mine[...]
+
+
+def reduce_all(v, stages, collective_id):
+    k, _, channels = v.shape
+    table = (k, channels)
+    return pl.pallas_call(
+        functools.partial(reduce_kernel, stages),
+        name="reduce_all",
+        out_shape=jax.ShapeDtypeStruct(table, f32),
+        in_specs=[VMEM],
+        out_specs=VMEM,
+        scratch_shapes=sum_scratch(stages, table),
+        compiler_params=pltpu.CompilerParams(collective_id=collective_id, has_side_effects=True),
+    )(v)
+
+
 def mixer_kernel(
-    xw, cw, meta, count, sums1, scales, shifts, w_in, w_gate, w_out, kl, kd,
+    stages, xw, cw, meta, count, sums1, scales, shifts, w_in, w_gate, w_out, kl, kd,
     xa_o, ca_o, gl_o, sl_o, c1_o, c2_o, gp_o, bn_o, sums_o,
-    cm, klb, kdb, xa, ca, gl, sl, c1, c2, gp, bn, gf, c1f, sem,
+    cm, klb, kdb, xa, ca, gl, sl, c1, c2, gp, bn, gf, c1f, sem, mine, *rest,
 ):
+    found = stage_peers(stages)
+    say_here(found)
     rows, px, channels = xa.shape
     columns = px // SUB
     groups = groups_of(channels)
@@ -227,13 +326,16 @@
     copies[-1].start()
     copies.append(pltpu.make_async_copy(bn, bn_o, sem.at[7]))
     copies[-1].start()
-    sums_o[0] = sums[0]
-    sums_o[1] = sums[1]
+    for k in range(2):
+        mine[k : k + 1, :] = jnp.sum(sums[k], axis=0, keepdims=True)
+    wait_all_here(found)
+    all_sum(mine, rest[: len(stages)], rest[len(stages) :], found)
+    sums_o[...] = mine[...]
     for copy in copies:
         copy.wait()
 
 
-def mixer_forward(xw, cw, meta, count, sums1, scales, shifts, w_in, w_gate, w_out, kl, kd):
+def mixer_forward(stages, xw, cw, meta, count, sums1, scales, shifts, w_in, w_gate, w_out, kl, kd):
     band, px, channels = xw.shape
     columns = px // SUB
     rows = columns
@@ -241,10 +343,10 @@
     small = (rows, px, channels)
     kinds = (bf16, bf16, bf16, f32, bf16, bf16, f32, f32)
     return pl.pallas_call(
-        mixer_kernel,
+        functools.partial(mixer_kernel, stages),
         name="mixer_forward",
         out_shape=[jax.ShapeDtypeStruct(small, k) for k in kinds]
-        + [jax.ShapeDtypeStruct((2, SUB, channels), f32)],
+        + [jax.ShapeDtypeStruct((2, channels), f32)],
         in_specs=[VMEM] * 12,
         out_specs=[ANY] * 8 + [VMEM],
         scratch_shapes=[
@@ -257,21 +359,27 @@
             pltpu.VMEM((n, rows + 4, columns, SUB, LANE), f32),
             pltpu.VMEM((n, rows, columns, SUB, LANE), f32),
             pltpu.SemaphoreType.DMA((8,)),
-        ],
-        compiler_params=pltpu.CompilerParams(vmem_limit_bytes=56 * MIB),
+        ]
+        + sum_scratch(stages, (2, channels)),
+        compiler_params=pltpu.CompilerParams(
+            collective_id=2, has_side_effects=True, vmem_limit_bytes=56 * MIB
+        ),
     )(xw, cw, meta, count, sums1, scales, shifts, w_in, w_gate, w_out, kl, kd)
 
 
 def hidden_kernel(
-    xa, ca, bn, meta, count, sums2, scales, shifts, hshift, w_e, w_rt, kh,
+    stages, xa, ca, bn, meta, count, sums2, scales, shifts, hshift, w_e, w_rt, kh,
     res_o, gn_o, gwe_o, gwr_o, gk_o, gh_o, sums_o,
-    cm, khb, kfb, n2, gr, ha, ge, em, gc, kacc, wet, wr, sem,
+    cm, khb, kfb, n2, gr, ha, ge, em, gc, kacc, wet, wr, mine, *rest,
 ):
+    found = stage_peers(stages)
+    say_here(found)
     rows, px, channels = xa.shape
     columns = px // SUB
     hidden = w_e.shape[1]
     wide = em.shape[0] * LANE
     parts = em.shape[0]
+    wide_step = 6
     make_col_mask(meta, cm)
     spread_taps(kh, khb)
     spread_taps(kh, kfb, flip=True)
@@ -295,22 +403,26 @@
         return acc + fold(grad.astype(f32))
 
     zero = jnp.zeros((SUB, channels), f32)
-    sums_o[2] = lax.fori_loop(0, rows, prepare, zero)
+    grad_sum = lax.fori_loop(0, rows, prepare, zero)
 
     def chunk(f, _):
         base = pl.multiple_of(f * wide, wide)
         lanes = pl.ds(base, wide)
         group = f * parts
 
-        def expand(r, _):
-            mask = row_mask(meta, cm, r)[:, :, :LANE]
-            value = dot(n2[r], w_e[:, lanes])
-            value = low(value + jnp.broadcast_to(hshift[0:1, lanes], value.shape))
-            for g in range(parts):
-                em[g, r + 1] = mask * pixels3(value[:, g * LANE : (g + 1) * LANE])
+        def expand(b, _):
+            tall = n2[pl.ds(b * wide_step, wide_step)].reshape(wide_step * px, channels)
+            product = dot(tall, w_e[:, lanes])
+            for k in range(wide_step):
+                r = b * wide_step + k
+                mask = row_mask(meta, cm, r)[:, :, :LANE]
+                value = product[k * px : (k + 1) * px]
+                value = low(value + jnp.broadcast_to(hshift[0:1, lanes], value.shape))
+                for g in range(parts):
+                    em[g, r + 1] = mask * pixels3(value[:, g * LANE : (g + 1) * LANE])
             return 0
 
-        lax.fori_loop(0, rows, expand, 0)
+        lax.fori_loop(0, rows // wide_step, expand, 0)
 
         def forward(r, acc):
             grad = dot(gr[r], w_rt[:, lanes])
@@ -375,24 +487,38 @@
     gwe_o[...] = dot_tn(n2[...].reshape(whole, channels), ge[...].reshape(whole, hidden))
     gwr_o[...] = dot_tn(gr[...].reshape(whole, channels), ha[...].reshape(whole, hidden))
 
-    def finish(r, sums):
-        mask = row_mask(meta, cm, r)
-        reduced = pixels3(dot(ha[r], wr[...])) + b8(shifts, 7)
-        middle = middle_of(r)
-        res_o[r] = pixels2(mask * (middle + b8(scales, 3) * reduced))
-        gn = pixels3(dot(ge[r], wet[...]))
-        gn_o[r] = pixels2(gn)
-        hat = (middle - mean) * rstd
-        out = pixels3(ca[r].astype(f32))
-        return sums[0] + fold(gn), sums[1] + fold(gn * hat), sums[2] + fold(out * reduced)
-
-    sums = lax.fori_loop(0, rows, finish, (zero, zero, zero))
-    sums_o[0] = sums[0]
-    sums_o[1] = sums[1]
-    sums_o[3] = sums[2]
-
-
-def hidden_block(xa, ca, bn, meta, count, sums2, scales, shifts, hshift, w_e, w_rt, kh):
+    step = 3
+
+    def finish(b, sums):
+        sums = list(sums)
+        at = pl.ds(b * step, step)
+        tall = step * px
+        reduced_all = dot(ha[at].reshape(tall, hidden), wr[...])
+        gn_all = dot(ge[at].reshape(tall, hidden), wet[...])
+        for k in range(step):
+            r = b * step + k
+            mask = row_mask(meta, cm, r)
+            reduced = pixels3(reduced_all[k * px : (k + 1) * px]) + b8(shifts, 7)
+            middle = middle_of(r)
+            res_o[r] = pixels2(mask * (middle + b8(scales, 3) * reduced))
+            gn = pixels3(gn_all[k * px : (k + 1) * px])
+            gn_o[r] = pixels2(gn)
+            hat = (middle - mean) * rstd
+            out = pixels3(ca[r].astype(f32))
+            sums[0] = sums[0] + fold(gn)
+            sums[1] = sums[1] + fold(gn * hat)
+            sums[2] = sums[2] + fold(out * reduced)
+        return tuple(sums)
+
+    sums = lax.fori_loop(0, rows // step, finish, (zero, zero, zero))
+    for k, value in enumerate((sums[0], sums[1], grad_sum, sums[2])):
+        mine[k : k + 1, :] = jnp.sum(value, axis=0, keepdims=True)
+    wait_all_here(found)
+    all_sum(mine, rest[: len(stages)], rest[len(stages) :], found)
+    sums_o[...] = mine[...]
+
+
+def hidden_block(stages, xa, ca, bn, meta, count, sums2, scales, shifts, hshift, w_e, w_rt, kh):
     rows, px, channels = xa.shape
     columns = px // SUB
     hidden = w_e.shape[1]
@@ -400,7 +526,7 @@
     parts = 2
     shape = jax.ShapeDtypeStruct
     return pl.pallas_call(
-        hidden_kernel,
+        functools.partial(hidden_kernel, stages),
         name="hidden_block",
         out_shape=[
             shape((rows, px, channels), f32),
@@ -409,7 +535,7 @@
             shape((channels, hidden), f32),
             shape((9, hidden), f32),
             shape((2, hidden), f32),
-            shape((4, SUB, channels), f32),
+            shape((4, channels), f32),
         ],
         in_specs=[VMEM] * 12,
         out_specs=[VMEM] * 7,
@@ -426,18 +552,22 @@
             pltpu.VMEM((parts, 9, SUB, LANE), f32),
             pltpu.VMEM((hidden, channels), bf16),
             pltpu.VMEM((hidden, channels), bf16),
-            pltpu.SemaphoreType.DMA((1,)),
-        ],
-        compiler_params=pltpu.CompilerParams(vmem_limit_bytes=60 * MIB),
+        ]
+        + sum_scratch(stages, (4, channels)),
+        compiler_params=pltpu.CompilerParams(
+            collective_id=3, has_side_effects=True, vmem_limit_bytes=60 * MIB
+        ),
     )(xa, ca, bn, meta, count, sums2, scales, shifts, hshift, w_e, w_rt, kh)
 
 
 def back_kernel(
-    gn, bn, xa, ca, gl, sl, c1, c2, gp, meta, count, sums1, sums2, sums3, scales, shifts,
+    stages, gn, bn, xa, ca, gl, sl, c1, c2, gp, meta, count, sums1, sums2, sums3, scales, shifts,
     w_in, w_gate, w_out, kl, kd,
     mix_o, gwi_o, gwg_o, gwo_o, gkl_o, gkd_o, sums_o,
-    cm, klb, kdb, gb, gg, gt, gm, tt, g2, g1, src, sem,
+    cm, klb, kdb, gb, gg, gt, gm, tt, g2, g1, src, mine, *rest,
 ):
+    found = stage_peers(stages)
+    say_here(found)
     rows, px, channels = xa.shape
     columns = px // SUB
     groups = groups_of(channels)
@@ -485,7 +615,7 @@
 
     sums = lax.fori_loop(0, rows, first, (zero,) * 4)
     for k in range(4):
-        sums_o[2 + k] = sums[k]
+        mine[2 + k : 3 + k, :] = jnp.sum(sums[k], axis=0, keepdims=True)
     whole = rows * px
     flat = lambda ref: ref[...].reshape(whole, channels)
     gwo_o[...] = dot_tn(flat(gt), flat(gb))
@@ -527,7 +657,7 @@
     start = tuple(jnp.zeros((SUB, width), f32) for g, width in groups)
     sums = lax.fori_loop(0, rows, dilated, start)
     for g, width in groups:
-        sums_o[6, :, g * LANE : g * LANE + width] = sums[g]
+        mine[6:7, g * LANE : g * LANE + width] = jnp.sum(sums[g], axis=0, keepdims=True)
 
     def refill(r, _):
         for g, width in groups:
@@ -567,7 +697,7 @@
 
     sums = lax.fori_loop(0, rows, local, start)
     for g, width in groups:
-        sums_o[7, :, g * LANE : g * LANE + width] = sums[g]
+        mine[7:8, g * LANE : g * LANE + width] = jnp.sum(sums[g], axis=0, keepdims=True)
 
     def last(r, sums):
         x = pixels3(xa[r].astype(f32))
@@ -580,12 +710,15 @@
         return sums[0] + fold(gn1), sums[1] + fold(gn1 * hat)
 
     sums = lax.fori_loop(0, rows, last, (zero, zero))
-    sums_o[0] = sums[0]
-    sums_o[1] = sums[1]
+    for k in range(2):
+        mine[k : k + 1, :] = jnp.sum(sums[k], axis=0, keepdims=True)
+    wait_all_here(found)
+    all_sum(mine, rest[: len(stages)], rest[len(stages) :], found)
+    sums_o[...] = mine[...]
     gwi_o[...] = dot_tn(flat(gb), flat(gg))
 
 
-def mixer_back(gn, bn, xa, ca, gl, sl, c1, c2, gp, meta, count, sums1, sums2, sums3, scales,
+def mixer_back(stages, gn, bn, xa, ca, gl, sl, c1, c2, gp, meta, count, sums1, sums2, sums3, scales,
                shifts, w_in, w_gate, w_out, kl, kd):
     rows, px, channels = xa.shape
     columns = px // SUB
@@ -594,11 +727,11 @@
     shape = jax.ShapeDtypeStruct
     square = shape((channels, channels), f32)
     return pl.pallas_call(
-        back_kernel,
+        functools.partial(back_kernel, stages),
         name="mixer_back",
         out_shape=[
             shape(small, f32), square, square, square,
-            shape((25, channels), f32), shape((49, channels), f32), shape((8, SUB, channels), f32),
+            shape((25, channels), f32), shape((49, channels), f32), shape((8, channels), f32),
         ],
         in_specs=[VMEM] * 21,
         out_specs=[VMEM] * 7,
@@ -614,9 +747,11 @@
             pltpu.VMEM((n, rows, columns, SUB, LANE), f32),
             pltpu.VMEM((n, rows + 4, columns, SUB, LANE), f32),
             pltpu.VMEM((n, rows, columns, SUB, LANE), f32),
-            pltpu.SemaphoreType.DMA((1,)),
-        ],
-        compiler_params=pltpu.CompilerParams(vmem_limit_bytes=62 * MIB),
+        ]
+        + sum_scratch(stages, (8, channels)),
+        compiler_params=pltpu.CompilerParams(
+            collective_id=4, has_side_effects=True, vmem_limit_bytes=62 * MIB
+        ),
     )(gn, bn, xa, ca, gl, sl, c1, c2, gp, meta, count, sums1, sums2, sums3, scales, shifts,
       w_in, w_gate, w_out, kl, kd)
 
@@ -685,73 +820,127 @@
     )(res, meta)
 
 
-def reduce_kernel(stages, v_ref, out_ref, mine, *rest):
+def tile_plan(shapes):
+    plan, base = [], 0
+    for rows, width in shapes:
+        blocks = pl.cdiv(rows, SUB)
+        plan.append((base, rows, groups_of(width)))
+        base += blocks * pl.cdiv(width, LANE)
+    return plan, base
+
+
+def tiles_in(refs, plan, buf):
+    for ref, (base, rows, groups) in zip(refs, plan):
+        n, full = len(groups), rows // SUB
+
+        def block(b, _, ref=ref, base=base, groups=groups, n=n):
+            at = pl.ds(pl.multiple_of(b * SUB, SUB), SUB)
+            for g, width in groups:
+                buf[base + b * n + g, :, :width] = ref[at, g * LANE : g * LANE + width]
+            return 0
+
+        lax.fori_loop(0, full, block, 0)
+        if rows % SUB:
+            for g, width in groups:
+                buf[base + full * n + g, : rows % SUB, :width] = ref[
+                    full * SUB :, g * LANE : g * LANE + width
+                ]
+
+
+def tiles_out(refs, plan, buf):
+    for ref, (base, rows, groups) in zip(refs, plan):
+        n, full = len(groups), rows // SUB
+
+        def block(b, _, ref=ref, base=base, groups=groups, n=n):
+            at = pl.ds(pl.multiple_of(b * SUB, SUB), SUB)
+            for g, width in groups:
+                ref[at, g * LANE : g * LANE + width] = buf[base + b * n + g, :, :width]
+            return 0
+
+        lax.fori_loop(0, full, block, 0)
+        if rows % SUB:
+            for g, width in groups:
+                ref[full * SUB :, g * LANE : g * LANE + width] = buf[
+                    base + full * n + g, : rows % SUB, :width
+                ]
+
+
+def grads_kernel(stages, plan, *refs):
+    count = len(plan)
+    ins, outs, (buf, full, *rest) = refs[:count], refs[count : 2 * count], refs[2 * count :]
     slots, sems = rest[: len(stages)], rest[len(stages) :]
-    core = lax.axis_index("rows")
-    chip = lax.axis_index("imgs")
-    barrier = pltpu.get_barrier_semaphore()
-    peers = []
-    for axis, stride, size in stages:
-        place = lax.rem((core if axis == "rows" else chip) // stride, size)
-        stage = []
-        for step in range(1, size):
-            other = lax.rem(place + step, size)
-            index = (core if axis == "rows" else chip) + (other - place) * stride
-            stage.append((step, (index, chip) if axis == "rows" else (core, index)))
-        peers.append(stage)
-    for stage in peers:
-        for step, device in stage:
-            pl.semaphore_signal(barrier, inc=1, device_id=device, device_id_type=MESH)
-    pl.semaphore_wait(barrier, sum(len(stage) for stage in peers))
-    mine[...] = jnp.sum(v_ref[...], axis=1)
-    for k, stage in enumerate(peers):
-        slot, (send, recv) = slots[k], sems[2 * k : 2 * k + 2]
+    found = stage_peers(stages)
+
+    def clear(t, _):
+        buf[t] = jnp.zeros((SUB, LANE), f32)
+        return 0
+
+    lax.fori_loop(0, buf.shape[0], clear, 0)
+    tiles_in(ins, plan, buf)
+    greet(found)
+    start, length, steps = 0, buf.shape[0], []
+    for k, (place, peers) in enumerate(found):
+        share = length // stages[k][2]
+        send, recv = sems[4 * k : 4 * k + 2]
         copies = []
-        for step, device in stage:
+        for step, other, device in peers:
+            src = buf.at[pl.ds(start + other * share, share)]
             copies.append(
-                pltpu.make_async_remote_copy(
-                    src_ref=mine,
-                    dst_ref=slot.at[step - 1],
-                    send_sem=send.at[step - 1],
-                    recv_sem=recv.at[step - 1],
-                    device_id=device,
-                    device_id_type=MESH,
-                )
+                remote(src, slots[k].at[step - 1], send.at[step - 1], recv.at[step - 1], device)
             )
             copies[-1].start()
         for copy in copies:
             copy.wait()
-        total = mine[...]
-        for step, device in stage:
-            total = total + slot[step - 1]
-        mine[...] = total
-    out_ref[...] = mine[...]
-
-
-def reduce_all(v, sizes, collective_id):
-    k, _, channels = v.shape
-    stages = [("rows", 1, sizes["rows"])]
-    left, stride = sizes["imgs"], 1
-    while left > 1:
-        size = 4 if left % 4 == 0 else (2 if left % 2 == 0 else left)
-        stages.append(("imgs", stride, size))
-        left, stride = left // size, stride * size
-    stages = [s for s in stages if s[2] > 1]
-    table = (k, channels)
-    sems = []
+        start, length = start + place * share, share
+
+        def add(t, _, start=start, k=k, n=len(peers)):
+            total = buf[start + t]
+            for i in range(n):
+                total = total + slots[k][i, t]
+            buf[start + t] = total
+            return 0
+
+        lax.fori_loop(0, length, add, 0)
+        steps.append((start, length))
+
+    def settle(t, _):
+        full[start + t] = buf[start + t]
+        return 0
+
+    lax.fori_loop(0, length, settle, 0)
+    for k in reversed(range(len(stages))):
+        start, length = steps[k]
+        send, recv = sems[4 * k + 2 : 4 * k + 4]
+        copies = []
+        for step, other, device in found[k][1]:
+            here = full.at[pl.ds(start, length)]
+            copies.append(remote(here, here, send.at[step - 1], recv.at[step - 1], device))
+            copies[-1].start()
+        for copy in copies:
+            copy.wait()
+    tiles_out(outs, plan, full)
+
+
+def sum_grads(arrays, stages, collective_id):
+    devices = math.prod(size for _, _, size in stages)
+    plan, tiles = tile_plan([a.shape for a in arrays])
+    tiles = pl.cdiv(tiles, devices) * devices
+    slots, sems, length = [], [], tiles
     for _, _, size in stages:
-        sems += [pltpu.SemaphoreType.DMA((size - 1,))] * 2
+        length //= size
+        slots.append(pltpu.VMEM((size - 1, length, SUB, LANE), f32))
+        sems += [pltpu.SemaphoreType.DMA((size - 1,))] * 4
     return pl.pallas_call(
-        functools.partial(reduce_kernel, stages),
-        name="reduce_all",
-        out_shape=jax.ShapeDtypeStruct(table, f32),
-        in_specs=[VMEM],
-        out_specs=VMEM,
-        scratch_shapes=[pltpu.VMEM(table, f32)]
-        + [pltpu.VMEM((size - 1,) + table, f32) for _, _, size in stages]
-        + sems,
-        compiler_params=pltpu.CompilerParams(collective_id=collective_id, has_side_effects=True),
-    )(v)
+        functools.partial(grads_kernel, stages, plan),
+        name="sum_grads",
+        out_shape=[jax.ShapeDtypeStruct(a.shape, f32) for a in arrays],
+        in_specs=[VMEM] * len(arrays),
+        out_specs=[VMEM] * len(arrays),
+        scratch_shapes=[pltpu.VMEM((tiles, SUB, LANE), f32)] * 2 + slots + sems,
+        compiler_params=pltpu.CompilerParams(
+            collective_id=collective_id, has_side_effects=True, vmem_limit_bytes=48 * MIB
+        ),
+    )(*arrays)
 
 
 def halves(values, core, half, axis):
@@ -813,7 +1002,8 @@
 
     x = jnp.transpose(inputs, (1, 2, 0, 3))
     y = jnp.transpose(cotangent, (1, 2, 0, 3))
-    sums1 = reduce_all(first_sums(x, own_meta), sizes, 1)
+    stages = stage_list(sizes)
+    sums1 = reduce_all(first_sums(x, own_meta), stages, 1)
 
     def gather_rows(v):
         mine, theirs = halves(v, core, half, 2)
@@ -822,21 +1012,18 @@
         return jnp.concatenate([upper, lower], axis=0).reshape(2 * band, px, channels)
 
     xw, cw = gather_rows(x), gather_rows(y)
-    xa, ca, gl, sl, c1, c2, gp, bn, part2 = mixer_forward(
-        xw, cw, meta, count, sums1, scales, shifts, w_inward, w_gating, w_outward,
+    xa, ca, gl, sl, c1, c2, gp, bn, sums2 = mixer_forward(
+        stages, xw, cw, meta, count, sums1, scales, shifts, w_inward, w_gating, w_outward,
         kernel_local, kernel_dilated,
     )
-    sums2 = reduce_all(part2, sizes, 2)
-    res, gn, gwe, gwr, gk, gh, part3 = hidden_block(
-        xa, ca, bn, meta, count, sums2, scales, shifts, hidden_shift, w_expand, w_reduce.T,
+    res, gn, gwe, gwr, gk, gh, sums3 = hidden_block(
+        stages, xa, ca, bn, meta, count, sums2, scales, shifts, hidden_shift, w_expand, w_reduce.T,
         kernel_hidden,
     )
-    sums3 = reduce_all(part3, sizes, 3)
-    mix, gwi, gwg, gwo, gkl, gkd, part4 = mixer_back(
-        gn, bn, xa, ca, gl, sl, c1, c2, gp, meta, count, sums1, sums2, sums3, scales, shifts,
+    mix, gwi, gwg, gwo, gkl, gkd, sums4 = mixer_back(
+        stages, gn, bn, xa, ca, gl, sl, c1, c2, gp, meta, count, sums1, sums2, sums3, scales, shifts,
         w_inward, w_gating, w_outward, kernel_local, kernel_dilated,
     )
-    sums4 = reduce_all(part4, sizes, 4)
 
     def scatter_rows(v):
         v = v.reshape(2 * band, columns, half, channels)
@@ -852,8 +1039,8 @@
     input_grad = scatter_rows(
         input_grad_kernel(mix, xa, meta, count, sums1, sums4, scales, 2 * band)
     )
-    gwe, gwr, gk, gh, gwi, gwg, gwo, gkl, gkd = lax.psum(
-        (gwe, gwr, gk, gh, gwi, gwg, gwo, gkl, gkd), ("rows", "imgs")
+    gwe, gwr, gk, gh, gwi, gwg, gwo, gkl, gkd = sum_grads(
+        (gwe, gwr, gk, gh, gwi, gwg, gwo, gkl, gkd), stages, 5
     )
     scales_grad = jnp.stack([sums4[1], sums4[2], sums3[1], sums3[3]])
     shifts_grad = jnp.stack(

time: 581 us -> 390 us (0.67)
  waiting for transfers between devices: 268 us -> 0.01 us
  Pallas kernels: 254 us -> 341 us
  between operations: 14.9 us -> 1.49 us
    psum x2 -> x0, waiting for transfers between devices: 262 us -> none  [on_device(): lax.psum((gwe, gwr, gk, gh, gwi, gwg, gwo, gkl, gkd), ('rows', 'imgs'))]
    pallas_call x3 -> x4, Pallas kernels: 192 us -> 313 us  [the longest x1 114 us: sum_grads(): pl.pallas_call(functools.partial(grads_kernel, stages, plan), name='sum_g...]
    pallas_call x4 -> x1, Pallas kernels: 47.5 us -> 13.6 us  [reduce_all(): pl.pallas_call(functools.partial(reduce_kernel, stages), name='reduce_all...]
    ppermute x2, waiting for transfers between devices: 5.83 us -> 0.01 us  [scatter_rows(): theirs = lax.ppermute(other, 'rows', [(0, 1), (1, 0)])]
    unnamed x39 -> x49, local copies, waits for them, and re-layouts: 14.7 us -> 14.4 us
  transfers between devices with their start and end apart: 6 -> 4, of which waited for: 3 -> 0; matrix products, arithmetic and copies ran while one was open for 3% -> 2% of each run, Pallas kernels for 3% -> 33%
where the time goes in v2:
time: 390 us; the launch traced here: 388 us
  Pallas kernels  341 us (87%)
  local copies, waits for them, and re-layouts  25.4 us (7%)
  other arithmetic  19 us (5%)
    pallas_call x1, Pallas kernels, sum_grads(): pl.pallas_call(functools.partial(grads_kernel, stages, plan), name='sum_g...  114 us
    pallas_call x1, Pallas kernels, hidden_block(): pl.pallas_call(functools.partial(hidden_kernel, stages), name='hidden_blo...  84 us
    pallas_call x1, Pallas kernels, mixer_back(): pl.pallas_call(functools.partial(back_kernel, stages), name='mixer_back',...  69.2 us
    pallas_call x1, Pallas kernels, mixer_forward(): pl.pallas_call(functools.partial(mixer_kernel, stages), name='mixer_forwa...  45.9 us
    unnamed x49, local copies, waits for them, and re-layouts  14.4 us
    pallas_call x1, Pallas kernels, reduce_all(): pl.pallas_call(functools.partial(reduce_kernel, stages), name='reduce_all...  13.6 us
  transfers between devices with their start and end apart: 4, of which 0 were waited for; matrix products, arithmetic and copies ran while one was open for 2% of the time, Pallas kernels for 33%

profile of v2, /device:TPU:0, one launch (start us, length us, event | category | flops | bytes accessed | tf_op | source)
XLA Modules:
  0.0 387.9 jit_solution(16459280026249552503)
XLA Ops:
  0.7 2.6 dynamic-slice_bitcast_fusion.1
  3.3 0.5 collective-permute-start
  3.7 2.4 dynamic-slice_bitcast_fusion
  6.2 0.1 collective-permute-start.1
  6.2 0.2 select_reduce_fusion.1
  6.4 0.6 multiply_reduce_fusion
  7.7 0.1 broadcast_in_dim.8.meta
  7.8 1.5 first_sums.1.v_ref
  9.4 0.6 copy-done.4
  10.0 13.6 %reduce_all.1.sums1 = f32[2,320]{1,0:T(2,128)} custom-call(f32[2,8,320]{2,1,0:T(8,128)} %copy-done.4), custom_call_target="tpu_custom_call" | custom-call | tf_op jit(solution)/shard_map/reduce_all/pallas_call | solution.py:214
  23.5 0.1 constant_dynamic-slice_fusion.2
  23.6 1.7 bitcast_select_fusion.3
  25.4 1.9 maximum_bitcast_fusion.2.xw
  27.2 0.5 copy-done.13
  27.8 1.8 bitcast_select_fusion.1
  29.5 1.9 maximum_bitcast_fusion.3.cw
  31.4 0.6 broadcast_in_dim.7.count
  32.0 0.7 broadcast_in_dim.6.meta
  32.7 45.9 %mixer_forward.1 = (bf16[18,144,320]{2,1,0:T(8,128)(2,1)}, bf16[18,144,320]{2,1,0:T(8,128)(2,1)}, bf16[18,144,320]{2,1,0:T(8,128)(2,1)}, f32[18,144,320]{2,1,0:T...) custom-call(bf16[22,144,320]{2,1,0:T(8,128)(2,1)} %maximum_bitcast_f, ...), custom_call_target="tpu_custom_call" | custom-call | tf_op jit(solution)/shard_map/mixer_forward/pallas_call | solution.py:345
  78.6 84.0 %hidden_block.1 = (f32[18,144,320]{2,1,0:T(8,128)}, f32[18,144,320]{2,1,0:T(8,128)}, f32[320,1280]{1,0:T(8,128)}, f32[320,1280]{1,0:T(8,128)}, f32[9,1280]{1,0:T...) custom-call(bf16[18,144,320]{2,1,0:T(8,128)(2,1)} %get-tuple-element.45.xa, bf16[18,144,320]{2,1,0:T(8,128)(2,1)} %get-tuple-element.46.ca, ...), custom_call_target="tpu_custom_call" | custom-call | tf_op jit(solution)/shard_map/hidden_block/pallas_call | solution.py:528
  162.6 5.2 %unalign.1 = f32[22,144,320]{2,1,0:T(8,128)} custom-call(f32[18,144,320]{2,1,0:T(8,128)} %get-tuple-element.49.res, f32[3,8,320]{2,1,0:T(8,128)} %broadcast_in_dim.6.meta), custom_call_target="tpu_custom_call" | custom-call | tf_op jit(solution)/shard_map/unalign/pallas_call | solution.py:813
  167.8 69.2 %mixer_back.1 = (f32[18,144,320]{2,1,0:T(8,128)}, f32[320,320]{1,0:T(8,128)}, f32[320,320]{1,0:T(8,128)}, f32[320,320]{1,0:T(8,128)}, f32[25,320]{1,0:T(8,128)}, /*index=5*/f32[49,320]{1,0:T(8,128)}, f32[8,320]{1,0:T(8,128)}) custom-call(f32[18,144,320]{2,1,0:T(8,128)} %get-tuple-element.50.gn, f32[18,144,320]{2,1,0:T(8,128)} %get-tuple-element.47.bn, ...), custom_call_target="tpu_custom_call" | custom-call | tf_op jit(solution)/shard_map/mixer_back/pallas_call | solution.py:729
  237.1 7.4 %input_grad.1 = f32[22,144,320]{2,1,0:T(8,128)} custom-call(f32[18,144,320]{2,1,0:T(8,128)} %get-tuple-element.57.mix, bf16[18,144,320]{2,1,0:T(8,128)(2,1)} %get-tuple-element.45.xa, f32[3,8,320]{2,1,0:T(8,128)} %broadcast_in_dim.6.meta, f32[8,128]{1,0:T(8,128)} %broadcast_in_dim.7.count, f32[2,320]{1,0:T(2,128)} %reduce_all.1.sums1, ...), custom_call_target="tpu_custom_call" | custom-call | tf_op jit(solution)/shard_map/input_grad/pallas_call | solution.py:793
  244.5 1.6 constant_dynamic-slice_fusion.1
  246.1 1.7 copy-done.12
  247.8 1.6 constant_dynamic-slice_fusion
  249.4 0.5 collective-permute-start.2
  249.9 0.7 slice.35
  250.7 1.0 copy-done.1
  251.7 1.0 copy-done.2
  252.7 1.0 copy-done.3
  253.8 0.7 copy-done.8
  254.5 114.1 %sum_grads.1 = (f32[320,1280]{1,0:T(8,128)S(1)}, f32[320,1280]{1,0:T(8,128)}, f32[9,1280]{1,0:T(8,128)S(1)}, f32[2,1280]{1,0:T(2,128)S(1)}, f32[320,320]{1,0:T(8...) custom-call(f32[320,1280]{1,0:T(8,128)} %get-tuple-element.59.refs_0, ...), custom_call_target="tpu_custom_call" | custom-call | tf_op jit(solution)/shard_map/sum_grads/pallas_call | solution.py:933
  368.6 0.6 copy-done.9
  369.2 0.6 stack.25
  369.8 0.6 pad_maximum_fusion
  370.4 4.6 %dynamic-slice_select_fusion.1 = (f32[11,18,8,320]{3,2,1,0:T(8,128)S(1)}, f32[11,18,8,320]{3,2,1,0:T(8,128)S(1)}, f32[11,18,8,320]{3,2,1,0:T(8,128)S(1)}, f32[11,18,8,320]{3,2,1,0:T(8,128)S(1)}) fusion(f32[11,18,8,320]{3,2,1,0:T(8,128)} %collective-permute-done.3, f32[22,18,8,320]{3,2,1,0:T(8,128)} %bitcast.35, s32[]{:T(128)S(6)} %select_n.62, pred[]{:T(512)S(6)} %eq.8, ...), kind=kLoop, calls=%fused_computation.5 | loop fusion | flops 2027520 | bytes 16220165 | tf_op jit(solution)/shard_map/jit(_where)/select_n | solution.py:1033
  375.1 2.8 maximum_bitcast_fusion.1
  377.9 2.8 maximum_bitcast_fusion
  380.7 0.6 copy.38
  381.3 0.8 copy.39
  382.1 0.8 copy.40
  382.9 0.8 copy.41
  383.7 1.2 copy.42
  384.8 1.2 copy.43
  386.0 0.6 copy.44
  386.6 0.6 copy.45
  387.3 0.6 copy.46
  (41 shorter events, 0.1 us)
Async XLA Ops:
  0.7 5.6 %copy-start.17 = (s32[256]{0:T(256)S(1)}, s32[256]{0:T(256)}, u32[]{:S(2)}) copy-start(s32[256]{0:T(256)} %param.30) | copy-start | bytes 3076
  0.7 5.6 %copy-start.18 = (s32[256]{0:T(256)S(1)}, s32[256]{0:T(256)}, u32[]{:S(2)}) copy-start(s32[256]{0:T(256)} %param.29) | copy-start | bytes 3076
  0.7 5.6 %copy-start.19 = (s32[16]{0:T(128)S(1)}, s32[16]{0:T(128)}, u32[]{:S(2)}) copy-start(s32[16]{0:T(128)} %param.31) | copy-start | bytes 196
  0.7 7.1 %copy-start = (bf16[16,11,18,320]{3,0,2,1:T(8,128)(2,1)S(1)}, bf16[16,11,18,320]{3,0,2,1:T(8,128)(2,1)}, u32[]{:S(2)}) copy-start(bf16[16,11,18,320]{3,0,2,1:T(8,128)(2,1)} %param.16) | copy-start | bytes 6082564
  3.3 20.3 %collective-permute-start = (bf16[11,18,8,320]{3,2,1,0:T(8,128)(2,1)}, bf16[11,18,8,320]{3,2,1,0:T(8,128)(2,1)}, u32[]{:S(2)}, u32[]{:S(2)}) collective-permute-start(bf16[11,18,8,320]{3,2,1,0:T(8,128)(2,1)} %dynamic-slice_bitcast_fusion.1), channel_id=1, source_target_pairs={{0,16},{16,0},{1,17},{17,1},{2,18},{18,2},{3,19},{19,3},{4,20},{20... | collective-permute-start | bytes 3041288 | tf_op jit(solution)/shard_map/ppermute | solution.py:949
  6.2 21.1 %collective-permute-start.1 = (bf16[11,18,8,320]{3,2,1,0:T(8,128)(2,1)}, bf16[11,18,8,320]{3,2,1,0:T(8,128)(2,1)}, u32[]{:S(2)}, u32[]{:S(2)}) collective-permute-start(bf16[11,18,8,320]{3,2,1,0:T(8,128)(2,1)} %dynamic-slice_bitcast_fusion), channel_id=1, source_target_pairs={{0,16},{16,0},{1,17},{17,1},{2,18},{18,2},{3,19},{19,3},{4,20},{20... | collective-permute-start | bytes 3041288 | tf_op jit(solution)/shard_map/ppermute | solution.py:949
  9.4 0.6 copy-start.4
  25.4 2.4 copy-start.13
  237.1 7.4 %copy-start.11 = (f32[22,144,320]{2,1,0:T(8,128)S(1)}, f32[22,144,320]{2,1,0:T(8,128)}, u32[]{:S(2)}) copy-start(f32[22,144,320]{2,1,0:T(8,128)} %unalign.1) | copy-start | bytes 12165124
  244.5 3.3 copy-start.12
  247.8 2.9 copy-start.5
  247.8 2.9 copy-start.6
  247.8 2.9 copy-start.7
  249.4 121.0 %collective-permute-start.3 = (f32[11,18,8,320]{3,2,1,0:T(8,128)}, f32[11,18,8,320]{3,2,1,0:T(8,128)}, u32[]{:S(2)}, u32[]{:S(2)}) collective-permute-start(f32[11,18,8,320]{3,2,1,0:T(8,128)} %constant_dynamic-slice_fusion), channel_id=1, source_target_pairs={{0,16},{16,0},{1,17},{17,1},{2,18},{18,2},{3,19},{19,3},{4,20},{20... | collective-permute-start | bytes 6082568 | tf_op jit(solution)/shard_map/ppermute | solution.py:1032
  249.4 121.0 %collective-permute-start.2 = (f32[11,18,8,320]{3,2,1,0:T(8,128)}, f32[11,18,8,320]{3,2,1,0:T(8,128)}, u32[]{:S(2)}, u32[]{:S(2)}) collective-permute-start(f32[11,18,8,320]{3,2,1,0:T(8,128)} %constant_dynamic-slice_fusion.1), channel_id=1, source_target_pairs={{0,16},{16,0},{1,17},{17,1},{2,18},{18,2},{3,19},{19,3},{4,20},{20... | collective-permute-start | bytes 6082568 | tf_op jit(solution)/shard_map/ppermute | solution.py:1032
  250.7 1.0 copy-start.1
  251.7 1.0 copy-start.2
  252.7 1.0 copy-start.3
  253.8 0.7 copy-start.8
  254.5 114.7 %copy-start.15 = (f32[8,320]{1,0:T(8,128)S(1)}, f32[8,320]{1,0:T(8,128)}, u32[]{:S(2)}) copy-start(f32[8,320]{1,0:T(8,128)} %get-tuple-element.58.sums4) | copy-start | bytes 30724
  254.5 114.7 %copy-start.16 = (f32[4,320]{1,0:T(4,128)S(1)}, f32[4,320]{1,0:T(4,128)}, u32[]{:S(2)}) copy-start(f32[4,320]{1,0:T(4,128)} %get-tuple-element.56.sums3) | copy-start | bytes 15364
  368.6 0.6 copy-start.9
  377.9 2.8 copy-start.10
  382.1 2.7 copy-start.14

commit v3 on v2

--- a/solution.py
+++ b/solution.py
@@ -369,8 +369,8 @@
 
 def hidden_kernel(
     stages, xa, ca, bn, meta, count, sums2, scales, shifts, hshift, w_e, w_rt, kh,
-    res_o, gn_o, gwe_o, gwr_o, gk_o, gh_o, sums_o,
-    cm, khb, kfb, n2, gr, ha, ge, em, gc, kacc, wet, wr, mine, *rest,
+    nat_o, gn_o, tiles_o, sums_o,
+    cm, khb, kfb, n2, gr, ha, ge, em, gc, kacc, wet, wr, res, nat, gn_s, tiles, sem, mine, *rest,
 ):
     found = stage_peers(stages)
     say_here(found)
@@ -380,6 +380,10 @@
     wide = em.shape[0] * LANE
     parts = em.shape[0]
     wide_step = 6
+    groups = hidden // LANE
+    tap_tile, bias_tile, last_tile = hidden_tiles(channels, hidden)
+    for t in range(tap_tile, last_tile):
+        tiles[t] = jnp.zeros((SUB, LANE), f32)
     make_col_mask(meta, cm)
     spread_taps(kh, khb)
     spread_taps(kh, kfb, flip=True)
@@ -444,8 +448,7 @@
 
         bias = lax.fori_loop(0, rows, forward, tuple(zeros_list(parts)))
         for g in range(parts):
-            here = pl.ds(pl.multiple_of(base + g * LANE, LANE), LANE)
-            gh_o[1:2, here] = jnp.sum(bias[g], axis=0, keepdims=True)
+            tiles[bias_tile + group + g, 1:2, :] = jnp.sum(bias[g], axis=0, keepdims=True)
             for tap in range(9):
                 kacc[g, tap] = jnp.zeros((SUB, LANE), f32)
 
@@ -475,17 +478,24 @@
 
         bias = lax.fori_loop(0, rows, backward, tuple(zeros_list(parts)))
         for g in range(parts):
-            here = pl.ds(pl.multiple_of(base + g * LANE, LANE), LANE)
-            gh_o[0:1, here] = jnp.sum(bias[g], axis=0, keepdims=True)
+            tiles[bias_tile + group + g, 0:1, :] = jnp.sum(bias[g], axis=0, keepdims=True)
             for tap in range(9):
-                gk_o[8 - tap : 9 - tap, here] = jnp.sum(kacc[g, tap], axis=0, keepdims=True)
+                at = tap_tile + (8 - tap) // SUB * groups + group + g
+                row = (8 - tap) % SUB
+                tiles[at, row : row + 1, :] = jnp.sum(kacc[g, tap], axis=0, keepdims=True)
         return 0
 
     lax.fori_loop(0, hidden // wide, chunk, 0)
 
     whole = rows * px
-    gwe_o[...] = dot_tn(n2[...].reshape(whole, channels), ge[...].reshape(whole, hidden))
-    gwr_o[...] = dot_tn(gr[...].reshape(whole, channels), ha[...].reshape(whole, hidden))
+    blocks = channels // SUB
+    for k, (left, right) in enumerate(((n2, ge), (gr, ha))):
+        grad = dot_tn(left[...].reshape(whole, channels), right[...].reshape(whole, hidden))
+        for g in range(groups):
+            part = grad[:, g * LANE : (g + 1) * LANE].reshape(blocks, SUB, LANE)
+            tiles[pl.ds(k * blocks * groups + g, blocks, stride=groups)] = part
+    copies = [pltpu.make_async_copy(tiles, tiles_o, sem.at[0])]
+    copies[0].start()
 
     step = 3
 
@@ -500,9 +510,9 @@
             mask = row_mask(meta, cm, r)
             reduced = pixels3(reduced_all[k * px : (k + 1) * px]) + b8(shifts, 7)
             middle = middle_of(r)
-            res_o[r] = pixels2(mask * (middle + b8(scales, 3) * reduced))
+            res[r] = pixels2(mask * (middle + b8(scales, 3) * reduced))
             gn = pixels3(gn_all[k * px : (k + 1) * px])
-            gn_o[r] = pixels2(gn)
+            gn_s[r] = pixels2(gn)
             hat = (middle - mean) * rstd
             out = pixels3(ca[r].astype(f32))
             sums[0] = sums[0] + fold(gn)
@@ -511,14 +521,27 @@
         return tuple(sums)
 
     sums = lax.fori_loop(0, rows // step, finish, (zero, zero, zero))
+    copies.append(pltpu.make_async_copy(gn_s, gn_o, sem.at[1]))
+    copies[-1].start()
     for k, value in enumerate((sums[0], sums[1], grad_sum, sums[2])):
         mine[k : k + 1, :] = jnp.sum(value, axis=0, keepdims=True)
     wait_all_here(found)
+    unalign(res, meta, nat)
+    copies.append(pltpu.make_async_copy(nat, nat_o, sem.at[2]))
+    copies[-1].start()
     all_sum(mine, rest[: len(stages)], rest[len(stages) :], found)
     sums_o[...] = mine[...]
-
-
-def hidden_block(stages, xa, ca, bn, meta, count, sums2, scales, shifts, hshift, w_e, w_rt, kh):
+    for copy in copies:
+        copy.wait()
+
+
+def hidden_tiles(channels, hidden):
+    groups = hidden // LANE
+    tap_tile = 2 * (channels // SUB) * groups
+    return tap_tile, tap_tile + 2 * groups, tap_tile + 3 * groups
+
+
+def hidden_block(stages, tiles, band, xa, ca, bn, meta, count, sums2, scales, shifts, hshift, w_e, w_rt, kh):
     rows, px, channels = xa.shape
     columns = px // SUB
     hidden = w_e.shape[1]
@@ -529,16 +552,13 @@
         functools.partial(hidden_kernel, stages),
         name="hidden_block",
         out_shape=[
+            shape((2 * band, columns, SUB, channels), f32),
             shape((rows, px, channels), f32),
-            shape((rows, px, channels), f32),
-            shape((channels, hidden), f32),
-            shape((channels, hidden), f32),
-            shape((9, hidden), f32),
-            shape((2, hidden), f32),
+            shape((tiles, SUB, LANE), f32),
             shape((4, channels), f32),
         ],
         in_specs=[VMEM] * 12,
-        out_specs=[VMEM] * 7,
+        out_specs=[ANY] * 3 + [VMEM],
         scratch_shapes=[
             pltpu.VMEM((columns, SUB, channels), f32),
             pltpu.VMEM((9, groups, SUB, LANE), f32),
@@ -552,6 +572,11 @@
             pltpu.VMEM((parts, 9, SUB, LANE), f32),
             pltpu.VMEM((hidden, channels), bf16),
             pltpu.VMEM((hidden, channels), bf16),
+            pltpu.VMEM((rows, px, channels), f32),
+            pltpu.VMEM((2 * band, columns, SUB, channels), f32),
+            pltpu.VMEM((rows, px, channels), f32),
+            pltpu.VMEM((tiles, SUB, LANE), f32),
+            pltpu.SemaphoreType.DMA((3,)),
         ]
         + sum_scratch(stages, (4, channels)),
         compiler_params=pltpu.CompilerParams(
@@ -560,17 +585,172 @@
     )(xa, ca, bn, meta, count, sums2, scales, shifts, hshift, w_e, w_rt, kh)
 
 
+class Wave:
+    def __init__(self, order, buf, full, pair_base, slots, sems, staging, sem):
+        self.order, self.found = order, stage_peers(order)
+        self.buf, self.full, self.pair_base = buf, full, pair_base
+        self.slots, self.sems, self.staging, self.sem = slots, sems, staging, sem
+        self.start, self.length = 0, buf.shape[0]
+        self.shares, self.copies = [], []
+
+    @property
+    def steps(self):
+        return 2 * len(self.order) + 1
+
+    def wait(self):
+        for copy in self.copies:
+            copy.wait()
+        self.copies = []
+
+    def add(self, k):
+        place, peers = self.found[k]
+        share = self.length // self.order[k][2]
+        self.start, self.length = self.start + place * share, share
+        self.shares.append((self.start, self.length))
+        size = math.gcd(share, 16)
+        start, buf, slot, count = self.start, self.buf, self.slots[k], len(peers)
+
+        def some(t, _):
+            at = pl.ds(start + t * size, size)
+            total = buf[at]
+            for i in range(count):
+                total = total + slot[i, pl.ds(t * size, size)]
+            buf[at] = total
+            return 0
+
+        lax.fori_loop(0, share // size, some, 0)
+
+    def scatter(self, k):
+        share = self.length // self.order[k][2]
+        send, recv = self.sems[4 * k : 4 * k + 2]
+        for step, other, device in self.found[k][1]:
+            src = self.buf.at[pl.ds(self.start + other * share, share)]
+            at = step - 1
+            self.copies.append(remote(src, self.slots[k].at[at], send.at[at], recv.at[at], device))
+            self.copies[-1].start()
+
+    def round(self):
+        start, buf, staging = self.start, self.buf, self.staging
+        pairs = self.length // 2
+
+        def one(p, _):
+            both = jnp.concatenate([buf[start + 2 * p], buf[start + 2 * p + 1]], axis=0)
+            staging[p] = both.astype(bf16)
+            return 0
+
+        lax.fori_loop(0, pairs, one, 0)
+        copy = pltpu.make_async_copy(staging, self.part(len(self.order) - 1), self.sem.at[0])
+        copy.start()
+        copy.wait()
+
+    def part(self, k):
+        start, length = self.shares[k]
+        return self.full.at[pl.ds(self.pair_base + start // 2, length // 2)]
+
+    def gather(self, k):
+        send, recv = self.sems[4 * k + 2 : 4 * k + 4]
+        here = self.part(k)
+        for step, _, device in self.found[k][1]:
+            at = step - 1
+            self.copies.append(remote(here, here, send.at[at], recv.at[at], device))
+            self.copies[-1].start()
+
+    def step(self, i):
+        n = len(self.order)
+        if i > 0:
+            self.wait()
+        if 1 <= i <= n:
+            self.add(i - 1)
+        if i < n:
+            self.scatter(i)
+        elif i < 2 * n:
+            if i == n:
+                self.round()
+            self.gather(2 * n - 1 - i)
+
+
+def wave_scratch(order, tiles):
+    slots, sems, length = [], [], tiles
+    for _, _, size in order:
+        length //= size
+        slots.append(pltpu.VMEM((size - 1, length, SUB, LANE), f32))
+        sems += [pltpu.SemaphoreType.DMA((size - 1,))] * 4
+    own = [
+        pltpu.VMEM((tiles, SUB, LANE), f32),
+        pltpu.VMEM((length // 2, 2 * SUB, LANE), bf16),
+        pltpu.SemaphoreType.DMA((1,)),
+    ]
+    return own + slots + sems
+
+
+def make_wave(order, full, pair_base, refs):
+    buf, staging, sem, *rest = refs[: 3 + 5 * len(order)]
+    slots, sems = rest[: len(order)], rest[len(order) :]
+    return Wave(order, buf, full, pair_base, slots, sems, staging, sem), refs[3 + 5 * len(order) :]
+
+
+def wave_plan(sizes, channels, hidden):
+    chips = sizes["imgs"]
+    side = 2 if chips == 16 else 4
+    one, two = ("imgs", 1, side), ("imgs", side, side)
+    rest = ("imgs", side * side, chips // (side * side))
+    first = ("rows", 1, sizes["rows"])
+    first_order, second_order = [first, one, two, rest], [first, two, one, rest]
+    short_order = [first, ("imgs", 1, side * side), rest]
+    step = 2 * sizes["rows"] * chips
+    square = channels // SUB * pl.cdiv(channels, LANE)
+    small = pl.cdiv(25, SUB) + pl.cdiv(49, SUB)
+    half = pl.cdiv(hidden_tiles(channels, hidden)[2], 2 * step) * step
+    return [
+        (first_order, half),
+        (second_order, half),
+        (first_order, pl.cdiv(2 * square, step) * step),
+        (short_order, pl.cdiv(square + small * pl.cdiv(channels, LANE), step) * step),
+    ]
+
+
 def back_kernel(
-    stages, gn, bn, xa, ca, gl, sl, c1, c2, gp, meta, count, sums1, sums2, sums3, scales, shifts,
-    w_in, w_gate, w_out, kl, kd,
-    mix_o, gwi_o, gwg_o, gwo_o, gkl_o, gkd_o, sums_o,
-    cm, klb, kdb, gb, gg, gt, gm, tt, g2, g1, src, mine, *rest,
+    stages, plan, gn, bn_i, xa_i, ca_i, gl_i, sl_i, c1_i, c2_i, gp, tiles_i, nat_i,
+    meta, count, sums1, sums2, sums3, scales, shifts, w_in, w_gate, w_out, kl, kd,
+    mixq_o, resq_o, full_o, sums_o,
+    cm, klb, kdb, gm, tt, sl, xa, ca, gl, c1, c2, gb, gg, gt, g2, g1, src, gw,
+    in_sem, move_sem, mine, *rest,
 ):
     found = stage_peers(stages)
     say_here(found)
     rows, px, channels = xa.shape
     columns = px // SUB
     groups = groups_of(channels)
+    core, chip = lax.axis_index("rows"), lax.axis_index("imgs")
+    band = mixq_o.shape[0]
+    parts = 3
+    step = rows // parts
+    pairs = [
+        (gn, gm), (bn_i, gw), (xa_i, xa), (ca_i, ca), (gl_i, gl), (gp, tt), (c1_i, c1),
+    ]
+    loads = []
+    for p in range(parts):
+        at = pl.ds(p * step, step)
+        loads.append([])
+        for k, (a, b) in enumerate(pairs):
+            loads[p].append(pltpu.make_async_copy(a.at[at], b.at[at], in_sem.at[p, k]))
+            loads[p][-1].start()
+    tail, waves, pair_base = list(rest[len(stages) * 3 :]), [], 0
+    for order, tiles in plan:
+        wave, tail = make_wave(order, full_o, pair_base, tail)
+        waves.append(wave)
+        pair_base += tiles // 2
+    late = [
+        pltpu.make_async_copy(c2_i, c2, in_sem.at[0, 7]),
+        pltpu.make_async_copy(sl_i, sl, in_sem.at[1, 7]),
+    ]
+    half = plan[0][1]
+    tile_loads = [
+        pltpu.make_async_copy(tiles_i.at[pl.ds(k * half, half)], waves[k].buf, in_sem.at[k, 8])
+        for k in range(2)
+    ]
+    for copy in tile_loads + late:
+        copy.start()
     make_col_mask(meta, cm)
     spread_taps(kl, klb, flip=True)
     spread_taps(kd, kdb, flip=True)
@@ -585,42 +765,116 @@
     back1 = b8(sums3, 1) / total
     zero = jnp.zeros((SUB, channels), f32)
 
-    def first(r, sums):
-        mask = row_mask(meta, cm, r)
-        both = pixels3(bn[r])
-        middle = pixels3(xa[r].astype(f32)) + b8(scales, 1) * both
-        hat = (middle - mean2) * rstd2
-        grad = pixels3(ca[r].astype(f32)) + scale2 * (
-            pixels3(gn[r]) - mask * (back0 + hat * back1)
+    def to_rows(v, out, first_sem):
+        images = pl.ds(pl.multiple_of(core * SUB, SUB), SUB)
+        there = remote(
+            v.at[pl.ds((1 - core) * band, band)], out.at[:, :, images, :],
+            move_sem.at[first_sem], move_sem.at[first_sem + 1], (1 - core, chip),
         )
-        gm[r] = pixels2(grad)
-        branch = (b8(scales, 1) * grad).astype(bf16)
-        gb[r] = pixels2(branch)
-        gated_grad = dot_nt(pixels2(branch), w_out[...])
-        gelu = gl[r].astype(f32)
-        gate_grad = (gated_grad * gelu).astype(bf16)
-        gg[r] = gate_grad
-        gt[r] = (gelu * gp[r]).astype(bf16)
-        tt[r] = gated_grad * gp[r]
-        conv = low(dot_nt(gate_grad, w_gate[...]))
-        for g, width in groups:
-            g2[g, r, :, :, :width] = pixels3(conv[:, g * LANE : g * LANE + width])
-            src[g, r, :, :, :width] = pixels3(c1[r, :, g * LANE : g * LANE + width].astype(f32))
-        return (
-            sums[0] + fold(grad * both),
-            sums[1] + fold(branch.astype(f32)),
-            sums[2] + fold(pixels3(gate_grad.astype(f32))),
-            sums[3] + fold(pixels3(conv)),
+        here = pltpu.make_async_copy(
+            v.at[pl.ds(core * band, band)], out.at[:, :, images, :], move_sem.at[first_sem + 2]
         )
-
-    sums = lax.fori_loop(0, rows, first, (zero,) * 4)
+        return [there, here]
+
+    wait_all_here(found)
+    moves = to_rows(nat_i, resq_o, 0)
+    for copy in moves:
+        copy.start()
+    for copy in tile_loads:
+        copy.wait()
+    done = [0, 0, 0, 0]
+
+    def advance(*which):
+        for w in which:
+            if done[w] < waves[w].steps:
+                waves[w].step(done[w])
+                done[w] += 1
+
+    advance(0, 1)
+
+    def first(b, sums):
+        sums = list(sums)
+        gated_parts = []
+        for k in range(step // 2):
+            r = b * (step // 2) + k
+            mask = row_mask(meta, cm, r)
+            both = gw[r]
+            middle = pixels3(xa[r].astype(f32)) + b8(scales, 1) * both
+            hat = (middle - mean2) * rstd2
+            grad = pixels3(ca[r].astype(f32)) + scale2 * (
+                pixels3(gm[r]) - mask * (back0 + hat * back1)
+            )
+            gm[r] = pixels2(grad)
+            branch = (b8(scales, 1) * grad).astype(bf16)
+            gb[r] = pixels2(branch)
+            sums[0] = sums[0] + fold(grad * both)
+            sums[1] = sums[1] + fold(branch.astype(f32))
+            gated_parts.append(pixels2(branch))
+        gated_grad = dot_nt(jnp.concatenate(gated_parts, axis=0), w_out[...])
+        gate_parts = []
+        for k in range(step // 2):
+            r = b * (step // 2) + k
+            mine_grad = gated_grad[k * px : (k + 1) * px]
+            gelu = gl[r].astype(f32)
+            gate_grad = (mine_grad * gelu).astype(bf16)
+            gg[r] = gate_grad
+            gate = tt[r]
+            gt[r] = (gelu * gate).astype(bf16)
+            tt[r] = mine_grad * gate
+            sums[2] = sums[2] + fold(pixels3(gate_grad.astype(f32)))
+            gate_parts.append(gate_grad)
+        conv_all = low(dot_nt(jnp.concatenate(gate_parts, axis=0), w_gate[...]))
+        for k in range(step // 2):
+            r = b * (step // 2) + k
+            conv = conv_all[k * px : (k + 1) * px]
+            for g, width in groups:
+                at = slice(g * LANE, g * LANE + width)
+                g2[g, r, :, :, :width] = pixels3(conv[:, at])
+                src[g, r, :, :, :width] = pixels3(c1[r, :, at].astype(f32))
+            sums[3] = sums[3] + fold(pixels3(conv))
+        return tuple(sums)
+
+    sums = (zero,) * 4
+    for p in range(parts):
+        for copy in loads[p]:
+            copy.wait()
+        sums = lax.fori_loop(2 * p, 2 * p + 2, first, sums)
+        if p == 1:
+            advance(0, 1)
     for k in range(4):
         mine[2 + k : 3 + k, :] = jnp.sum(sums[k], axis=0, keepdims=True)
     whole = rows * px
     flat = lambda ref: ref[...].reshape(whole, channels)
-    gwo_o[...] = dot_tn(flat(gt), flat(gb))
-    gwg_o[...] = dot_tn(flat(c2), flat(gg))
-
+    blocks, n = channels // SUB, len(groups)
+
+    def square(left, right, wave, base):
+        grad = dot_tn(flat(left), flat(right))
+        for g, width in groups:
+            part = grad[:, g * LANE : g * LANE + width].reshape(blocks, SUB, width)
+            wave.buf[pl.ds(base + g, blocks, stride=n), :, :width] = part
+
+    def clear(buf):
+        def one(t, _):
+            buf[t] = jnp.zeros((SUB, LANE), f32)
+            return 0
+
+        lax.fori_loop(0, buf.shape[0], one, 0)
+
+    clear(waves[2].buf)
+    clear(waves[3].buf)
+    square(gt, gb, waves[2], 0)
+    for copy in late:
+        copy.wait()
+    square(c2, gg, waves[2], blocks * n)
+    advance(2)
+
+    def put_tap(tap, g, acc, base):
+        row = jnp.sum(acc, axis=0, keepdims=True)
+        at = base + tap // SUB * n + g
+        waves[3].buf[at, tap % SUB : tap % SUB + 1, :] = row
+
+    near_base = blocks * n
+    far_base = near_base + pl.cdiv(kl.shape[0], SUB) * n
     for g, width in groups:
         for i in range(7):
             first_row = max(0, 3 * (3 - i))
@@ -634,8 +888,11 @@
 
             acc = lax.fori_loop(first_row, last_row, taps_row, zeros_list(7))
             for j in range(7):
-                row = jnp.sum(acc[j], axis=0, keepdims=True)
-                gkd_o[7 * i + j : 7 * i + j + 1, g * LANE : g * LANE + width] = row[:, :width]
+                put_tap(7 * i + j, g, acc[j], far_base)
+        if g == 1:
+            advance(0, 1, 2)
+
+    advance(0, 1)
 
     def dilated(r, sums):
         mask = row_mask(meta, cm, r)
@@ -655,9 +912,13 @@
         return tuple(out)
 
     start = tuple(jnp.zeros((SUB, width), f32) for g, width in groups)
-    sums = lax.fori_loop(0, rows, dilated, start)
+    sums = lax.fori_loop(0, rows // 2, dilated, start)
+    advance(2)
+    sums = lax.fori_loop(rows // 2, rows, dilated, sums)
     for g, width in groups:
-        mine[6:7, g * LANE : g * LANE + width] = jnp.sum(sums[g], axis=0, keepdims=True)
+        at = slice(g * LANE, g * LANE + width)
+        mine[6:7, at] = jnp.sum(sums[g], axis=0, keepdims=True)
+    advance(0, 1, 2)
 
     def refill(r, _):
         for g, width in groups:
@@ -676,13 +937,12 @@
 
             acc = lax.fori_loop(0, rows, taps_row, zeros_list(5))
             for j in range(5):
-                tap = 24 - (5 * i + j)
-                row = jnp.sum(acc[j], axis=0, keepdims=True)
-                gkl_o[tap : tap + 1, g * LANE : g * LANE + width] = row[:, :width]
+                put_tap(24 - (5 * i + j), g, acc[j], near_base)
+        advance(0, 1, 2)
 
     def local(r, sums):
         mask = row_mask(meta, cm, r)
-        parts = []
+        out = []
         for g, width in groups:
             acc = zeros_list(columns)
             for i in range(5):
@@ -692,88 +952,96 @@
             at = slice(g * LANE, g * LANE + width)
             grad = (tt[r, :, at] + pixels2(value)) * sl[r, :, at]
             gg[r, :, at] = grad.astype(bf16)
-            parts.append(sums[g] + fold(pixels3(low(grad))))
-        return tuple(parts)
-
-    sums = lax.fori_loop(0, rows, local, start)
+            out.append(sums[g] + fold(pixels3(low(grad))))
+        x = pixels3(xa[r].astype(f32))
+        gb[r] = pixels2((x - mean1) * scale1 + b8(shifts, 0)).astype(bf16)
+        return tuple(out)
+
+    sums = start
+    for p in range(2):
+        sums = lax.fori_loop(p * (rows // 2), (p + 1) * (rows // 2), local, sums)
+        advance(0, 1, 2)
     for g, width in groups:
-        mine[7:8, g * LANE : g * LANE + width] = jnp.sum(sums[g], axis=0, keepdims=True)
-
-    def last(r, sums):
-        x = pixels3(xa[r].astype(f32))
-        grad = pixels3(gm[r])
-        gn1 = pixels3(dot_nt(gg[r], w_in[...])) + b8(scales, 1) * grad
-        mix_o[r] = pixels2(grad + scale1 * gn1)
-        hat = (x - mean1) * rstd1
-        normed = (x - mean1) * scale1 + b8(shifts, 0)
-        gb[r] = pixels2(normed).astype(bf16)
-        return sums[0] + fold(gn1), sums[1] + fold(gn1 * hat)
-
-    sums = lax.fori_loop(0, rows, last, (zero, zero))
+        at = slice(g * LANE, g * LANE + width)
+        mine[7:8, at] = jnp.sum(sums[g], axis=0, keepdims=True)
+    square(gb, gg, waves[3], 0)
+    advance(3)
+
+    def last(b, sums):
+        sums = list(sums)
+        tall = gg[pl.ds(b * (step // 2), step // 2)].reshape(step // 2 * px, channels)
+        product = dot_nt(tall, w_in[...])
+        for k in range(step // 2):
+            r = b * (step // 2) + k
+            x = pixels3(xa[r].astype(f32))
+            grad = pixels3(gm[r])
+            gn1 = pixels3(product[k * px : (k + 1) * px]) + b8(scales, 1) * grad
+            gm[r] = pixels2(grad + scale1 * gn1)
+            hat = (x - mean1) * rstd1
+            sums[0] = sums[0] + fold(gn1)
+            sums[1] = sums[1] + fold(gn1 * hat)
+        return tuple(sums)
+
+    sums = lax.fori_loop(0, 2 * parts, last, (zero, zero))
     for k in range(2):
         mine[k : k + 1, :] = jnp.sum(sums[k], axis=0, keepdims=True)
-    wait_all_here(found)
-    all_sum(mine, rest[: len(stages)], rest[len(stages) :], found)
+    advance(3)
+    unalign(gm, meta, gw)
+    moves += to_rows(gw, mixq_o, 3)
+    for copy in moves[2:]:
+        copy.start()
+    all_sum(mine, rest[: len(stages)], rest[len(stages) : len(stages) * 3], found)
     sums_o[...] = mine[...]
-    gwi_o[...] = dot_tn(flat(gb), flat(gg))
-
-
-def mixer_back(stages, gn, bn, xa, ca, gl, sl, c1, c2, gp, meta, count, sums1, sums2, sums3, scales,
-               shifts, w_in, w_gate, w_out, kl, kd):
+    while any(d < w.steps for d, w in zip(done, waves)):
+        advance(0, 1, 2, 3)
+    for copy in moves:
+        copy.wait()
+
+
+def mixer_back(stages, plan, band, gn, bn, xa, ca, gl, sl, c1, c2, gp, tiles, nat, meta, count,
+               sums1, sums2, sums3, scales, shifts, w_in, w_gate, w_out, kl, kd):
     rows, px, channels = xa.shape
     columns = px // SUB
     n = len(groups_of(channels))
     small = (rows, px, channels)
     shape = jax.ShapeDtypeStruct
-    square = shape((channels, channels), f32)
+    pairs = sum(tiles // 2 for _, tiles in plan)
+    waves = []
+    for order, tiles_there in plan:
+        waves += wave_scratch(order, tiles_there)
     return pl.pallas_call(
-        functools.partial(back_kernel, stages),
+        functools.partial(back_kernel, stages, plan),
         name="mixer_back",
         out_shape=[
-            shape(small, f32), square, square, square,
-            shape((25, channels), f32), shape((49, channels), f32), shape((8, channels), f32),
+            shape((band, columns, 2 * SUB, channels), f32),
+            shape((band, columns, 2 * SUB, channels), f32),
+            shape((pairs, 2 * SUB, LANE), bf16),
+            shape((8, channels), f32),
         ],
-        in_specs=[VMEM] * 21,
-        out_specs=[VMEM] * 7,
+        in_specs=[ANY] * 11 + [VMEM] * 12,
+        out_specs=[ANY] * 3 + [VMEM],
         scratch_shapes=[
             pltpu.VMEM((columns, SUB, channels), f32),
             pltpu.VMEM((25, n, SUB, LANE), f32),
             pltpu.VMEM((49, n, SUB, LANE), f32),
-            pltpu.VMEM(small, bf16),
-            pltpu.VMEM(small, bf16),
-            pltpu.VMEM(small, bf16),
-            pltpu.VMEM(small, f32),
-            pltpu.VMEM(small, f32),
+        ]
+        + [pltpu.VMEM(small, k) for k in (f32,) * 3 + (bf16,) * 8]
+        + [
             pltpu.VMEM((n, rows, columns, SUB, LANE), f32),
             pltpu.VMEM((n, rows + 4, columns, SUB, LANE), f32),
             pltpu.VMEM((n, rows, columns, SUB, LANE), f32),
+            pltpu.VMEM((2 * band, columns, SUB, channels), f32),
+            pltpu.SemaphoreType.DMA((3, 9)),
+            pltpu.SemaphoreType.DMA((6,)),
         ]
-        + sum_scratch(stages, (8, channels)),
+        + sum_scratch(stages, (8, channels))
+        + waves,
         compiler_params=pltpu.CompilerParams(
-            collective_id=4, has_side_effects=True, vmem_limit_bytes=62 * MIB
+            collective_id=4, has_side_effects=True, vmem_limit_bytes=63 * MIB
         ),
-    )(gn, bn, xa, ca, gl, sl, c1, c2, gp, meta, count, sums1, sums2, sums3, scales, shifts,
-      w_in, w_gate, w_out, kl, kd)
-
-
-def input_kernel(mix, xa, meta, count, sums1, sums4, scales, out, cm, al):
-    rows, px, channels = xa.shape
-    make_col_mask(meta, cm)
-    total = count[0:1, 0:1]
-    mean1, rstd1 = statistics(sums1, total, 0)
-    scale1 = rstd1 * b8(scales, 0)
-    back0 = b8(sums4, 0) / total
-    back1 = b8(sums4, 1) / total
-
-    def one(r, _):
-        mask = row_mask(meta, cm, r)
-        hat = (pixels3(xa[r].astype(f32)) - mean1) * rstd1
-        grad = mask * (pixels3(mix[r]) - scale1 * (back0 + hat * back1))
-        al[r] = pixels2(grad)
-        return 0
-
-    lax.fori_loop(0, rows, one, 0)
-    unalign(al, meta, out)
+    )(gn, bn.reshape(rows, columns, SUB, channels), xa, ca, gl, sl, c1, c2, gp, tiles, nat, meta,
+      count, sums1, sums2, sums3, scales,
+      shifts, w_in, w_gate, w_out, kl, kd)
 
 
 def unalign(al, meta, out):
@@ -785,162 +1053,77 @@
             if 0 <= at - t < rows:
                 chosen = (meta[0] == float(t))[None]
                 value = jnp.where(chosen, pixels3(al[at - t]), value)
-        out[at] = pixels2(value)
-
-
-def input_grad_kernel(mix, xa, meta, count, sums1, sums4, scales, band):
-    rows, px, channels = xa.shape
+        out[at] = value
+
+
+def tiles_out(full, base, ref):
+    rows, width = ref.shape
+    groups = groups_of(width)
+    n, blocks = len(groups), rows // SUB
+    period = 1 if n % 2 == 0 else 2
+
+    def block(b, _):
+        for k in range(period):
+            for g, wide in groups:
+                tile = k * n + g
+                pair = base // 2 + b * (period * n // 2) + tile // 2
+                value = full[pair].astype(f32)[tile % 2 * SUB : (tile % 2 + 1) * SUB]
+                at = pl.ds(pl.multiple_of((b * period + k) * SUB, SUB), SUB)
+                ref[at, g * LANE : g * LANE + wide] = value[:, :wide]
+        return 0
+
+    lax.fori_loop(0, blocks // period, block, 0)
+    for b in range(blocks // period * period, pl.cdiv(rows, SUB)):
+        count = min(SUB, rows - b * SUB)
+        for g, wide in groups:
+            tile = base + b * n + g
+            value = full[tile // 2].astype(f32)[tile % 2 * SUB : tile % 2 * SUB + count]
+            ref[b * SUB : b * SUB + count, g * LANE : g * LANE + wide] = value[:, :wide]
+
+
+def finish_kernel(
+    bases, x, mixq, resq, meta, count, sums1, sums4, scales, full, in_o, res_o, *rest,
+):
+    grads, cm = rest[:-1], rest[-1]
+    row = pl.program_id(0)
+    size, top = meta[2], meta[0]
+
+    @pl.when(row == 0)
+    def _():
+        for c in range(cm.shape[0]):
+            cm[c] = (size > c).astype(f32)
+        for ref, base in zip(grads, bases):
+            tiles_out(full, base, ref)
+
+    total = count[0:1, 0:1]
+    mean = sums1[0:1, :] / total
+    rstd = lax.rsqrt(sums1[1:2, :] / total - mean * mean + epsilon)
+    scale = rstd * scales[0:1, :]
+    back0, back1 = sums4[0:1, :] / total, sums4[1:2, :] / total
+    spread = lambda v: jnp.broadcast_to(v, size.shape)
+    mean, rstd, scale, back0, back1 = (spread(v) for v in (mean, rstd, scale, back0, back1))
+    at = row.astype(f32)
+    inside = ((at >= top) & (at < top + size)).astype(f32)
+    mask = cm[...] * inside[None]
+    hat = (mask * x[0].astype(f32) - mean) * rstd
+    in_o[0] = mask * (mixq[0] - scale * (back0 + hat * back1))
+    res_o[0] = resq[0]
+
+
+def finish(x, mixq, resq, meta, count, sums1, sums4, scales, full, shapes, bases):
+    band, columns, images, channels = x.shape
+    block = pl.BlockSpec((1, columns, images, channels), lambda r: (r, 0, 0, 0))
+    shape = jax.ShapeDtypeStruct
     return pl.pallas_call(
-        input_kernel,
-        name="input_grad",
-        out_shape=jax.ShapeDtypeStruct((band, px, channels), f32),
-        in_specs=[VMEM] * 7,
-        out_specs=VMEM,
-        scratch_shapes=[
-            pltpu.VMEM((px // SUB, SUB, channels), f32),
-            pltpu.VMEM((rows, px, channels), f32),
-        ],
-        compiler_params=pltpu.CompilerParams(vmem_limit_bytes=56 * MIB),
-    )(mix, xa, meta, count, sums1, sums4, scales)
-
-
-def unalign_kernel(res, meta, out):
-    unalign(res, meta, out)
-
-
-def unaligned(res, meta, band):
-    rows, px, channels = res.shape
-    return pl.pallas_call(
-        unalign_kernel,
-        name="unalign",
-        out_shape=jax.ShapeDtypeStruct((band, px, channels), f32),
-        in_specs=[VMEM] * 2,
-        out_specs=VMEM,
-        compiler_params=pltpu.CompilerParams(vmem_limit_bytes=56 * MIB),
-    )(res, meta)
-
-
-def tile_plan(shapes):
-    plan, base = [], 0
-    for rows, width in shapes:
-        blocks = pl.cdiv(rows, SUB)
-        plan.append((base, rows, groups_of(width)))
-        base += blocks * pl.cdiv(width, LANE)
-    return plan, base
-
-
-def tiles_in(refs, plan, buf):
-    for ref, (base, rows, groups) in zip(refs, plan):
-        n, full = len(groups), rows // SUB
-
-        def block(b, _, ref=ref, base=base, groups=groups, n=n):
-            at = pl.ds(pl.multiple_of(b * SUB, SUB), SUB)
-            for g, width in groups:
-                buf[base + b * n + g, :, :width] = ref[at, g * LANE : g * LANE + width]
-            return 0
-
-        lax.fori_loop(0, full, block, 0)
-        if rows % SUB:
-            for g, width in groups:
-                buf[base + full * n + g, : rows % SUB, :width] = ref[
-                    full * SUB :, g * LANE : g * LANE + width
-                ]
-
-
-def tiles_out(refs, plan, buf):
-    for ref, (base, rows, groups) in zip(refs, plan):
-        n, full = len(groups), rows // SUB
-
-        def block(b, _, ref=ref, base=base, groups=groups, n=n):
-            at = pl.ds(pl.multiple_of(b * SUB, SUB), SUB)
-            for g, width in groups:
-                ref[at, g * LANE : g * LANE + width] = buf[base + b * n + g, :, :width]
-            return 0
-
-        lax.fori_loop(0, full, block, 0)
-        if rows % SUB:
-            for g, width in groups:
-                ref[full * SUB :, g * LANE : g * LANE + width] = buf[
-                    base + full * n + g, : rows % SUB, :width
-                ]
-
-
-def grads_kernel(stages, plan, *refs):
-    count = len(plan)
-    ins, outs, (buf, full, *rest) = refs[:count], refs[count : 2 * count], refs[2 * count :]
-    slots, sems = rest[: len(stages)], rest[len(stages) :]
-    found = stage_peers(stages)
-
-    def clear(t, _):
-        buf[t] = jnp.zeros((SUB, LANE), f32)
-        return 0
-
-    lax.fori_loop(0, buf.shape[0], clear, 0)
-    tiles_in(ins, plan, buf)
-    greet(found)
-    start, length, steps = 0, buf.shape[0], []
-    for k, (place, peers) in enumerate(found):
-        share = length // stages[k][2]
-        send, recv = sems[4 * k : 4 * k + 2]
-        copies = []
-        for step, other, device in peers:
-            src = buf.at[pl.ds(start + other * share, share)]
-            copies.append(
-                remote(src, slots[k].at[step - 1], send.at[step - 1], recv.at[step - 1], device)
-            )
-            copies[-1].start()
-        for copy in copies:
-            copy.wait()
-        start, length = start + place * share, share
-
-        def add(t, _, start=start, k=k, n=len(peers)):
-            total = buf[start + t]
-            for i in range(n):
-                total = total + slots[k][i, t]
-            buf[start + t] = total
-            return 0
-
-        lax.fori_loop(0, length, add, 0)
-        steps.append((start, length))
-
-    def settle(t, _):
-        full[start + t] = buf[start + t]
-        return 0
-
-    lax.fori_loop(0, length, settle, 0)
-    for k in reversed(range(len(stages))):
-        start, length = steps[k]
-        send, recv = sems[4 * k + 2 : 4 * k + 4]
-        copies = []
-        for step, other, device in found[k][1]:
-            here = full.at[pl.ds(start, length)]
-            copies.append(remote(here, here, send.at[step - 1], recv.at[step - 1], device))
-            copies[-1].start()
-        for copy in copies:
-            copy.wait()
-    tiles_out(outs, plan, full)
-
-
-def sum_grads(arrays, stages, collective_id):
-    devices = math.prod(size for _, _, size in stages)
-    plan, tiles = tile_plan([a.shape for a in arrays])
-    tiles = pl.cdiv(tiles, devices) * devices
-    slots, sems, length = [], [], tiles
-    for _, _, size in stages:
-        length //= size
-        slots.append(pltpu.VMEM((size - 1, length, SUB, LANE), f32))
-        sems += [pltpu.SemaphoreType.DMA((size - 1,))] * 4
-    return pl.pallas_call(
-        functools.partial(grads_kernel, stages, plan),
-        name="sum_grads",
-        out_shape=[jax.ShapeDtypeStruct(a.shape, f32) for a in arrays],
-        in_specs=[VMEM] * len(arrays),
-        out_specs=[VMEM] * len(arrays),
-        scratch_shapes=[pltpu.VMEM((tiles, SUB, LANE), f32)] * 2 + slots + sems,
-        compiler_params=pltpu.CompilerParams(
-            collective_id=collective_id, has_side_effects=True, vmem_limit_bytes=48 * MIB
-        ),
-    )(*arrays)
+        functools.partial(finish_kernel, bases),
+        name="finish",
+        grid=(band,),
+        out_shape=[shape(x.shape, f32)] * 2 + [shape(s, f32) for s in shapes],
+        in_specs=[block] * 3 + [VMEM] * 6,
+        out_specs=[block] * 2 + [VMEM] * len(shapes),
+        scratch_shapes=[pltpu.VMEM((columns, images, channels), f32)],
+        compiler_params=pltpu.CompilerParams(vmem_limit_bytes=48 * MIB),
+    )(x, mixq, resq, meta, count, sums1, sums4, scales, full)
 
 
 def halves(values, core, half, axis):
@@ -1016,38 +1199,47 @@
         stages, xw, cw, meta, count, sums1, scales, shifts, w_inward, w_gating, w_outward,
         kernel_local, kernel_dilated,
     )
-    res, gn, gwe, gwr, gk, gh, sums3 = hidden_block(
-        stages, xa, ca, bn, meta, count, sums2, scales, shifts, hidden_shift, w_expand, w_reduce.T,
-        kernel_hidden,
+    hidden = w_expand.shape[1]
+    plan = wave_plan(sizes, channels, hidden)
+    half_tiles = plan[0][1]
+    nat, gn, tiles, sums3 = hidden_block(
+        stages, 2 * half_tiles, band, xa, ca, bn, meta, count, sums2, scales, shifts,
+        hidden_shift, w_expand, w_reduce.T, kernel_hidden,
     )
-    mix, gwi, gwg, gwo, gkl, gkd, sums4 = mixer_back(
-        stages, gn, bn, xa, ca, gl, sl, c1, c2, gp, meta, count, sums1, sums2, sums3, scales, shifts,
-        w_inward, w_gating, w_outward, kernel_local, kernel_dilated,
+    mixq, resq, full, sums4 = mixer_back(
+        stages, plan, band, gn, bn, xa, ca, gl, sl, c1, c2, gp, tiles, nat, meta, count,
+        sums1, sums2, sums3, scales, shifts, w_inward, w_gating, w_outward, kernel_local,
+        kernel_dilated,
     )
-
-    def scatter_rows(v):
-        v = v.reshape(2 * band, columns, half, channels)
-        mine = lax.dynamic_slice_in_dim(v, core * band, band, axis=0)
-        other = lax.dynamic_slice_in_dim(v, (1 - core) * band, band, axis=0)
-        theirs = lax.ppermute(other, "rows", [(0, 1), (1, 0)])
-        lower = jnp.where(core == 0, mine, theirs)
-        upper = jnp.where(core == 0, theirs, mine)
-        both = jnp.concatenate([lower, upper], axis=2)
-        return jnp.transpose(both, (2, 0, 1, 3))
-
-    result = scatter_rows(unaligned(res, meta, 2 * band))
-    input_grad = scatter_rows(
-        input_grad_kernel(mix, xa, meta, count, sums1, sums4, scales, 2 * band)
-    )
-    gwe, gwr, gk, gh, gwi, gwg, gwo, gkl, gkd = sum_grads(
-        (gwe, gwr, gk, gh, gwi, gwg, gwo, gkl, gkd), stages, 5
+    square, wide = (channels, channels), (channels, hidden)
+    blocks, n = channels // SUB, len(groups_of(channels))
+    tap_tile, bias_tile, _ = hidden_tiles(channels, hidden)
+    second = 2 * half_tiles
+    third = second + plan[2][1]
+    near = third + blocks * n
+    far = near + pl.cdiv(kernel_local.shape[0], SUB) * n
+    targets = [
+        (wide, 0),
+        (wide, tap_tile // 2),
+        (kernel_hidden.shape, tap_tile),
+        (hidden_shift.shape, bias_tile),
+        (square, second),
+        (square, second + blocks * n),
+        (square, third),
+        (kernel_local.shape, near),
+        (kernel_dilated.shape, far),
+    ]
+    input_grad, result, gwe, gwr, gk, gh, gwo, gwg, gwi, gkl, gkd = finish(
+        x, mixq, resq, own_meta, count, sums1, sums4, scales, full,
+        [t[0] for t in targets], [t[1] for t in targets],
     )
     scales_grad = jnp.stack([sums4[1], sums4[2], sums3[1], sums3[3]])
     shifts_grad = jnp.stack(
         [sums4[0], sums4[7], sums4[6], sums4[5], sums4[4], sums4[3], sums3[0], sums3[2]]
     )
+    back = lambda v: jnp.transpose(v, (2, 0, 1, 3))
     return (
-        result, input_grad, scales_grad, shifts_grad, gh, gwi, gwg, gwo, gwe, gwr.T,
+        back(result), back(input_grad), scales_grad, shifts_grad, gh, gwi, gwg, gwo, gwe, gwr.T,
         gkl, gkd, gk,
     )
 

time: 390 us -> 284 us (0.73)
  Pallas kernels: 341 us -> 259 us
  local copies, waits for them, and re-layouts: 25.4 us -> 14.4 us
  other arithmetic: 19 us -> 8.05 us
    pallas_call x4 -> x2, Pallas kernels: 196 us -> 117 us  [the longest x1 102 us: mixer_back(): pl.pallas_call(functools.partial(back_kernel, stages, plan), name='mixer_...]
    unnamed x49 -> x22, local copies, waits for them, and re-layouts: 14.4 us -> 4.8 us
    transpose x2 -> x0, other arithmetic: 5.66 us -> none  [scatter_rows(): return jnp.transpose(both, (2, 0, 1, 3))]
    select_n x1 -> x0, other arithmetic: 4.64 us -> none  [scatter_rows(): lower = jnp.where(core == 0, mine, theirs)]
  transfers between devices with their start and end apart: 4 -> 2, of which waited for: 0 -> 0; matrix products, arithmetic and copies ran while one was open for 2% -> 1% of each run, Pallas kernels for 33% -> 5%
where the time goes in v3:
time: 284 us; the launch traced here: 283 us
  Pallas kernels  259 us (91%)
  local copies, waits for them, and re-layouts  14.4 us (5%)
  other arithmetic  8.05 us (3%)
    pallas_call x1, Pallas kernels, mixer_back(): pl.pallas_call(functools.partial(back_kernel, stages, plan), name='mixer_...  102 us
    pallas_call x1, Pallas kernels, hidden_block(): pl.pallas_call(functools.partial(hidden_kernel, stages), name='hidden_blo...  81.5 us
    pallas_call x1, Pallas kernels, mixer_forward(): pl.pallas_call(functools.partial(mixer_kernel, stages), name='mixer_forwa...  45.9 us
    pallas_call x1, Pallas kernels, finish(): pl.pallas_call(functools.partial(finish_kernel, bases), name='finish', gr...  15 us
    pallas_call x1, Pallas kernels, reduce_all(): pl.pallas_call(functools.partial(reduce_kernel, stages), name='reduce_all...  13.6 us
  transfers between devices with their start and end apart: 2, of which 0 were waited for; matrix products, arithmetic and copies ran while one was open for 1% of the time, Pallas kernels for 5%

profile of v3, /device:TPU:0, one launch (start us, length us, event | category | flops | bytes accessed | tf_op | source)
XLA Modules:
  0.0 283.5 jit_solution(16088075019344160526)
XLA Ops:
  0.7 0.0 copy-start.9
  0.7 0.0 copy-start.8
  0.7 0.0 copy-start.10
  0.7 0.0 copy-start
  0.7 2.6 dynamic-slice_bitcast_fusion.1
  3.3 0.5 collective-permute-start
  3.7 2.4 dynamic-slice_bitcast_fusion
  6.2 0.1 collective-permute-start.1
  6.2 0.0 copy-done.9
  6.2 0.6 multiply_reduce_fusion
  7.5 0.0 copy-done.8
  7.5 0.0 copy-done.10
  7.5 0.2 select_reduce_fusion.1
  7.7 0.1 broadcast_in_dim.8.meta
  7.8 0.0 copy-done
  7.8 1.5 first_sums.1.v_ref
  9.4 0.0 copy-start.4
  9.4 0.6 copy-done.4
  10.0 13.6 %reduce_all.1.sums1 = f32[2,320]{1,0:T(2,128)} custom-call(f32[2,8,320]{2,1,0:T(8,128)} %copy-done.4), custom_call_target="tpu_custom_call" | custom-call | tf_op jit(solution)/shard_map/reduce_all/pallas_call | solution.py:214
  23.6 0.1 constant_dynamic-slice_fusion
  23.7 0.0 collective-permute-done
  23.7 0.0 collective-permute-done.1
  23.7 2.9 %bitcast_select_fusion.1 = (bf16[11,18,8,320]{3,2,1,0:T(8,128)(2,1)S(1)}, bf16[11,18,8,320]{3,2,1,0:T(8,128)(2,1)S(1)}, bf16[11,18,8,320]{3,2,1,0:T(8,128)(2,1)S(1)}, bf16[11,18,8,320]{3,2,1,0:T(8,128)(2,1)S(1)}) fusion(bf16[11,18,8,320]{3,2,1,0:T(8,128)(2,1)} %collective-permute-done.1, pred[]{:T(512)S(6)} %eq.8, bf16[16,11,18,320]{3,0,2,1:T(8,128)(2,1)} %param.17, ...), kind=kLoop, calls=%fused_computation.3 | loop fusion | flops 2027520 | bytes 8110085 | tf_op jit(solution)/shard_map/jit(_where)/select_n | solution.py:1193
  26.6 1.9 maximum_bitcast_fusion.1.cw
  28.4 1.9 maximum_bitcast_fusion.xw
  30.3 0.6 broadcast_in_dim.7.count
  30.9 0.7 broadcast_in_dim.6.meta
  31.6 45.9 %mixer_forward.1 = (bf16[18,144,320]{2,1,0:T(8,128)(2,1)}, bf16[18,144,320]{2,1,0:T(8,128)(2,1)}, bf16[18,144,320]{2,1,0:T(8,128)(2,1)}, f32[18,144,320]{2,1,0:T...) custom-call(bf16[22,144,320]{2,1,0:T(8,128)(2,1)} %maximum_bitcast_f, ...), custom_call_target="tpu_custom_call" | custom-call | tf_op jit(solution)/shard_map/mixer_forward/pallas_call | solution.py:345
  77.5 81.5 %hidden_block.1 = (f32[22,18,8,320]{3,2,1,0:T(8,128)}, f32[18,144,320]{2,1,0:T(8,128)}, f32[896,8,128]{2,1,0:T(8,128)}, f32[4,320]{1,0:T(4,128)}) custom-call(bf16[18,144,320]{2,1,0:T(8,128)(2,1)} %get-tuple-element.41.xa.xa_i, bf16[18,144,320]{2,1,0:T(8,128)(2,1)} %get-tuple-element.42.ca.ca_i, f32[18,144,320]{2,1,0:T(8,128)} %get-tuple-element.43.bn, ...), custom_call_target="tpu_custom_call" | custom-call | tf_op jit(solution)/shard_map/hidden_block/pallas_call | solution.py:551
  159.0 0.8 fusion.4
  159.9 0.0 copy-start.3
  159.9 0.0 copy-start.5
  159.9 0.0 copy-start.6
  159.9 101.5 %mixer_back.1 = (f32[11,18,16,320]{3,2,1,0:T(8,128)}, f32[11,18,16,320]{3,2,1,0:T(8,128)}, bf16[672,16,128]{2,1,0:T(8,128)(2,1)}, f32[8,320]{1,0:T(8,128)}) custom-call(f32[18,144,320]{2,1,0:T(8,128)} %get-tuple-element.45.gn, f32[18,18,8,320]{3,2,1,0:T(8,128)} %bitcast.31, bf16[18,144,320]{2,1,0:T(8,128)(2,1)} %get-tuple-element.41.xa.xa_i, ...), custom_call_target="tpu_custom_call" | custom-call | tf_op jit(solution)/shard_map/mixer_back/pallas_call | solution.py:1012
  261.4 0.7 slice.35
  262.1 0.9 fusion.3
  263.1 0.6 pad_maximum_fusion
  263.7 0.0 copy-done.3
  263.7 0.0 copy-done.5
  263.7 0.0 copy-done.6
  263.7 0.0 copy-start.1
  263.7 1.7 copy-done.1
  265.4 0.0 copy-start.2
  265.4 1.8 copy-done.2
  267.2 0.0 copy-start.7
  267.2 0.7 copy-done.7
  267.9 15.0 %finish.1 = (f32[11,18,16,320]{3,2,1,0:T(8,128)}, f32[11,18,16,320]{3,2,1,0:T(8,128)}, f32[320,1280]{1,0:T(8,128)}, f32[320,1280]{1,0:T(8,128)}, f32[9,1280]{1,0...) custom-call(bf16[11,18,16,320]{3,2,1,0:T(8,128)(2,1)S(1)} %bitcast.3, ...), custom_call_target="tpu_custom_call" | custom-call | tf_op jit(solution)/shard_map/finish/pallas_call | solution.py:1117
  282.9 0.6 stack.25
  (3 shorter events, 0.0 us)
Async XLA Ops:
  0.7 5.6 %copy-start.9 = (s32[256]{0:T(256)S(1)}, s32[256]{0:T(256)}, u32[]{:S(2)}) copy-start(s32[256]{0:T(256)} %param.29) | copy-start | bytes 3076
  0.7 6.8 %copy-start.8 = (s32[256]{0:T(256)S(1)}, s32[256]{0:T(256)}, u32[]{:S(2)}) copy-start(s32[256]{0:T(256)} %param.30) | copy-start | bytes 3076
  0.7 6.8 %copy-start.10 = (s32[16]{0:T(128)S(1)}, s32[16]{0:T(128)}, u32[]{:S(2)}) copy-start(s32[16]{0:T(128)} %param.31) | copy-start | bytes 196
  0.7 7.1 %copy-start = (bf16[16,11,18,320]{3,0,2,1:T(8,128)(2,1)S(1)}, bf16[16,11,18,320]{3,0,2,1:T(8,128)(2,1)}, u32[]{:S(2)}) copy-start(bf16[16,11,18,320]{3,0,2,1:T(8,128)(2,1)} %param.16) | copy-start | bytes 6082564
  3.3 20.4 %collective-permute-start = (bf16[11,18,8,320]{3,2,1,0:T(8,128)(2,1)}, bf16[11,18,8,320]{3,2,1,0:T(8,128)(2,1)}, u32[]{:S(2)}, u32[]{:S(2)}) collective-permute-start(bf16[11,18,8,320]{3,2,1,0:T(8,128)(2,1)} %dynamic-slice_bitcast_fusion.1), channel_id=1, source_target_pairs={{0,16},{16,0},{1,17},{17,1},{2,18},{18,2},{3,19},{19,3},{4,20},{20... | collective-permute-start | bytes 3041288 | tf_op jit(solution)/shard_map/ppermute | solution.py:1132
  6.2 17.5 %collective-permute-start.1 = (bf16[11,18,8,320]{3,2,1,0:T(8,128)(2,1)}, bf16[11,18,8,320]{3,2,1,0:T(8,128)(2,1)}, u32[]{:S(2)}, u32[]{:S(2)}) collective-permute-start(bf16[11,18,8,320]{3,2,1,0:T(8,128)(2,1)} %dynamic-slice_bitcast_fusion), channel_id=1, source_target_pairs={{0,16},{16,0},{1,17},{17,1},{2,18},{18,2},{3,19},{19,3},{4,20},{20... | collective-permute-start | bytes 3041288 | tf_op jit(solution)/shard_map/ppermute | solution.py:1132
  9.4 0.6 copy-start.4
  159.9 103.8 %copy-start.3 = (f32[8,128]{1,0:T(8,128)S(1)}, f32[8,128]{1,0:T(8,128)}, u32[]{:S(2)}) copy-start(f32[8,128]{1,0:T(8,128)} %broadcast_in_dim.7.count) | copy-start | bytes 12292
  159.9 103.8 %copy-start.5 = (f32[4,320]{1,0:T(4,128)S(1)}, f32[4,320]{1,0:T(4,128)}, u32[]{:S(2)}) copy-start(f32[4,320]{1,0:T(4,128)} %scales.7) | copy-start | bytes 15364
  159.9 103.8 %copy-start.6 = (f32[2,320]{1,0:T(2,128)S(1)}, f32[2,320]{1,0:T(2,128)}, u32[]{:S(2)}) copy-start(f32[2,320]{1,0:T(2,128)} %reduce_all.1.sums1) | copy-start | bytes 7684
  263.7 1.7 copy-start.1
  265.4 1.8 copy-start.2
  267.2 0.7 copy-start.7

commit v4 on v3

--- a/solution.py
+++ b/solution.py
@@ -24,15 +24,8 @@
 
 
 def normal_parts(v):
-    bell = jnp.exp(-0.5 * (v * v))
-    base = 1.0 + (0.3275911 * 0.7071067811865476) * jnp.abs(v)
-    t = pl.reciprocal(base, approx=True)
-    t = t * (2.0 - base * t)
-    poly = 0.5 * 1.061405429
-    for coef in (-1.453152027, 1.421413741, -0.284496736, 0.254829592):
-        poly = poly * t + 0.5 * coef
-    tail = poly * t * bell
-    return jnp.where(v >= 0, 1.0 - tail, tail), bell * 0.3989422804014327
+    bell = jnp.exp2((-0.5 * 1.4426950408889634) * (v * v))
+    return 0.5 + 0.5 * lax.erf(v * 0.7071067811865476), bell * 0.3989422804014327
 
 
 def dot(a, b):
@@ -134,6 +127,10 @@
         stages.append(("imgs", stride, size))
         left, stride = left // size, stride * size
     return [s for s in stages if s[2] > 1]
+
+
+def reach_list(sizes):
+    return [("rows", 1, sizes["rows"]), ("imgs", 1, sizes["imgs"])]
 
 
 def stage_peers(stages):
@@ -175,21 +172,34 @@
     )
 
 
-def all_sum(mine, slots, sems, found):
-    for k, (_, peers) in enumerate(found):
-        slot, (send, recv) = slots[k], sems[2 * k : 2 * k + 2]
-        copies = []
-        for step, _, device in peers:
-            copies.append(
-                remote(mine, slot.at[step - 1], send.at[step - 1], recv.at[step - 1], device)
-            )
-            copies[-1].start()
-        for copy in copies:
+class AllSum:
+    def __init__(self, stages, mine, rest):
+        self.found, self.mine = stage_peers(stages), mine
+        n = len(stages)
+        self.slots, self.sems = rest[:n], rest[n : 3 * n]
+
+    def start(self, k):
+        slot, (send, recv) = self.slots[k], self.sems[2 * k : 2 * k + 2]
+        self.copies = []
+        for step, _, device in self.found[k][1]:
+            at = step - 1
+            self.copies.append(remote(self.mine, slot.at[at], send.at[at], recv.at[at], device))
+            self.copies[-1].start()
+
+    def end(self, k):
+        for copy in self.copies:
             copy.wait()
-        total = mine[...]
-        for step, _, _ in peers:
-            total = total + slot[step - 1]
-        mine[...] = total
+        total = self.mine[...]
+        for step, _, _ in self.found[k][1]:
+            total = total + self.slots[k][step - 1]
+        self.mine[...] = total
+
+
+def all_sum(stages, mine, rest):
+    total = AllSum(stages, mine, rest)
+    for k in range(len(stages)):
+        total.start(k)
+        total.end(k)
 
 
 def sum_scratch(stages, table):
@@ -200,32 +210,11 @@
     return [pltpu.VMEM(table, f32)] + slots + sems
 
 
-def reduce_kernel(stages, v_ref, out_ref, mine, *rest):
-    found = stage_peers(stages)
-    greet(found)
-    mine[...] = jnp.sum(v_ref[...], axis=1)
-    all_sum(mine, rest[: len(stages)], rest[len(stages) :], found)
-    out_ref[...] = mine[...]
-
-
-def reduce_all(v, stages, collective_id):
-    k, _, channels = v.shape
-    table = (k, channels)
-    return pl.pallas_call(
-        functools.partial(reduce_kernel, stages),
-        name="reduce_all",
-        out_shape=jax.ShapeDtypeStruct(table, f32),
-        in_specs=[VMEM],
-        out_specs=VMEM,
-        scratch_shapes=sum_scratch(stages, table),
-        compiler_params=pltpu.CompilerParams(collective_id=collective_id, has_side_effects=True),
-    )(v)
-
-
 def mixer_kernel(
-    stages, xw, cw, meta, count, sums1, scales, shifts, w_in, w_gate, w_out, kl, kd,
-    xa_o, ca_o, gl_o, sl_o, c1_o, c2_o, gp_o, bn_o, sums_o,
-    cm, klb, kdb, xa, ca, gl, sl, c1, c2, gp, bn, gf, c1f, sem, mine, *rest,
+    stages, x_i, y_i, own_meta, meta, count, scales, shifts, w_in, w_gate, w_out, kl, kd,
+    xa_o, ca_o, gl_o, sl_o, c1_o, c2_o, gp_o, bn_o, sums1_o, sums_o,
+    cm, klb, kdb, xa, ca, gl, sl, c1, c2, gp, bn, gf, c1f, sem,
+    own_cm, xs, ys, xw, cw, move_sem, mine, *rest,
 ):
     found = stage_peers(stages)
     say_here(found)
@@ -233,13 +222,61 @@
     columns = px // SUB
     groups = groups_of(channels)
     offsets = xw.shape[0] - rows + 1
+    core, chip = lax.axis_index("rows"), lax.axis_index("imgs")
+    band = x_i.shape[0]
+    upper = core == 0
+    size, top = own_meta[1], own_meta[0]
+    for c in range(columns):
+        own_cm[c] = (size > c).astype(f32)
+
+    def split(value, full, out, r):
+        a, b = value[:, :SUB], value[:, SUB:]
+        full[core * band + r] = pixels2(jnp.where(upper, a, b)).astype(bf16)
+        out[r] = pixels2(jnp.where(upper, b, a)).astype(bf16)
+
+    def split_x(r, sums):
+        at = (r * 1).astype(f32)
+        inside = ((at >= top) & (at < top + size)).astype(f32)
+        value = x_i[r].astype(f32)
+        split(value, xw, xs, r)
+        value = own_cm[...] * inside[None] * value
+        return sums[0] + fold(value), sums[1] + fold(value * value)
+
+    def split_y(r, _):
+        split(y_i[r].astype(f32), cw, ys, r)
+        return 0
+
+    def to_other(out, full, k):
+        at = pl.ds(core * band, band)
+        return remote(out, full.at[at], move_sem.at[k], move_sem.at[k + 1], (1 - core, chip))
+
+    zero = jnp.zeros((2 * SUB, channels), f32)
+    sums = lax.fori_loop(0, band, split_x, (zero, zero))
+    for k in range(2):
+        mine[k : k + 1, :] = jnp.sum(sums[k], axis=0, keepdims=True)
+    wait_all_here(found)
+    moves = [to_other(xs, xw, 0), to_other(ys, cw, 2)]
+    first_sum = AllSum(stages, mine, rest)
+    first_sum.start(0)
+    moves[0].start()
+    lax.fori_loop(0, band, split_y, 0)
+    moves[1].start()
+    first_sum.end(0)
+    first_sum.start(1)
     make_col_mask(meta, cm)
     spread_taps(kl, klb)
     spread_taps(kd, kdb)
     for edge in (0, 1, rows + 2, rows + 3):
         gf[:, edge] = jnp.zeros(gf.shape[:1] + gf.shape[2:], f32)
+    first_sum.end(1)
+    for k in range(2, len(stages)):
+        first_sum.start(k)
+        first_sum.end(k)
+    sums1_o[...] = mine[...]
+    for copy in moves:
+        copy.wait()
     total = count[0:1, 0:1]
-    mean, rstd = statistics(sums1, total, 0)
+    mean, rstd = statistics(sums1_o, total, 0)
     scale = rstd * b8(scales, 0)
     starts = [meta[0] == float(t) for t in range(offsets)]
 
@@ -328,16 +365,17 @@
     copies[-1].start()
     for k in range(2):
         mine[k : k + 1, :] = jnp.sum(sums[k], axis=0, keepdims=True)
-    wait_all_here(found)
-    all_sum(mine, rest[: len(stages)], rest[len(stages) :], found)
+    all_sum(stages, mine, rest[3 * len(stages) :])
     sums_o[...] = mine[...]
     for copy in copies:
         copy.wait()
 
 
-def mixer_forward(stages, xw, cw, meta, count, sums1, scales, shifts, w_in, w_gate, w_out, kl, kd):
-    band, px, channels = xw.shape
-    columns = px // SUB
+def mixer_forward(
+    stages, x, y, own_meta, meta, count, scales, shifts, w_in, w_gate, w_out, kl, kd
+):
+    band, columns, images, channels = x.shape
+    px = columns * SUB
     rows = columns
     n = len(groups_of(channels))
     small = (rows, px, channels)
@@ -346,9 +384,9 @@
         functools.partial(mixer_kernel, stages),
         name="mixer_forward",
         out_shape=[jax.ShapeDtypeStruct(small, k) for k in kinds]
-        + [jax.ShapeDtypeStruct((2, channels), f32)],
+        + [jax.ShapeDtypeStruct((2, channels), f32)] * 2,
         in_specs=[VMEM] * 12,
-        out_specs=[ANY] * 8 + [VMEM],
+        out_specs=[ANY] * 8 + [VMEM] * 2,
         scratch_shapes=[
             pltpu.VMEM((columns, SUB, channels), f32),
             pltpu.VMEM((25, n, SUB, LANE), f32),
@@ -359,21 +397,158 @@
             pltpu.VMEM((n, rows + 4, columns, SUB, LANE), f32),
             pltpu.VMEM((n, rows, columns, SUB, LANE), f32),
             pltpu.SemaphoreType.DMA((8,)),
+            pltpu.VMEM((columns, images, channels), f32),
+            pltpu.VMEM((band, px, channels), bf16),
+            pltpu.VMEM((band, px, channels), bf16),
+            pltpu.VMEM((2 * band, px, channels), bf16),
+            pltpu.VMEM((2 * band, px, channels), bf16),
+            pltpu.SemaphoreType.DMA((4,)),
         ]
-        + sum_scratch(stages, (2, channels)),
+        + sum_scratch(stages, (2, channels))
+        + sum_scratch(stages, (2, channels))[1:],
         compiler_params=pltpu.CompilerParams(
-            collective_id=2, has_side_effects=True, vmem_limit_bytes=56 * MIB
+            collective_id=2, has_side_effects=True, vmem_limit_bytes=62 * MIB
         ),
-    )(xw, cw, meta, count, sums1, scales, shifts, w_in, w_gate, w_out, kl, kd)
+    )(x, y, own_meta, meta, count, scales, shifts, w_in, w_gate, w_out, kl, kd)
+
+
+class Wave:
+    def __init__(self, order, tiles, refs, buf, base=0, full=None, pair_base=0, done=0):
+        self.order, self.found = order, stage_peers(order)
+        self.buf, self.base, self.full, self.pair_base = buf, base, full, pair_base
+        n = len(order)
+        self.slots, self.sems = refs[:n], refs[n:]
+        self.start, self.length, self.origin = 0, tiles, 0
+        self.shares, self.copies, self.done = [], [], done
+        for k in range(done):
+            self.take(k)
+        self.origin = self.start
+
+    @property
+    def steps(self):
+        return 2 * len(self.order) + 1
+
+    def take(self, k):
+        self.length //= self.order[k][2]
+        self.start = self.start + self.found[k][0] * self.length
+        self.shares.append((self.start, self.length))
+
+    def wait(self):
+        for copy in self.copies:
+            copy.wait()
+        self.copies = []
+
+    def at(self, tile):
+        return self.base + tile - self.origin
+
+    def add(self, k):
+        self.wait()
+        self.take(k)
+        size = math.gcd(self.length, 16)
+        start, buf, slot = self.at(self.start), self.buf, self.slots[k]
+        count = len(self.found[k][1])
+
+        def some(t, _):
+            at = pl.ds(start + t * size, size)
+            total = buf[at]
+            for i in range(count):
+                total = total + slot[i, pl.ds(t * size, size)]
+            buf[at] = total
+            return 0
+
+        lax.fori_loop(0, self.length // size, some, 0)
+
+    def scatter(self, k):
+        share = self.length // self.order[k][2]
+        send, recv = self.sems[4 * k : 4 * k + 2]
+        for step, other, device in self.found[k][1]:
+            src = self.buf.at[pl.ds(self.at(self.start + other * share), share)]
+            at = step - 1
+            self.copies.append(remote(src, self.slots[k].at[at], send.at[at], recv.at[at], device))
+            self.copies[-1].start()
+
+    def round(self):
+        start, buf, full = self.at(self.start), self.buf, self.full
+        first = self.pair_base + self.start // 2
+
+        def one(p, _):
+            both = jnp.concatenate([buf[start + 2 * p], buf[start + 2 * p + 1]], axis=0)
+            full[first + p] = both.astype(bf16)
+            return 0
+
+        lax.fori_loop(0, self.length // 2, one, 0)
+
+    def part(self, k):
+        start, length = self.shares[k]
+        return self.full.at[pl.ds(self.pair_base + start // 2, length // 2)]
+
+    def gather(self, k):
+        send, recv = self.sems[4 * k + 2 : 4 * k + 4]
+        here = self.part(k)
+        for step, _, device in self.found[k][1]:
+            at = step - 1
+            self.copies.append(remote(here, here, send.at[at], recv.at[at], device))
+            self.copies[-1].start()
+
+    def guess(self, i):
+        n = len(self.order)
+        if i >= 2 * n:
+            return 0.0
+        k = i if i < n else 2 * n - 1 - i
+        axis, _, size = self.order[k]
+        share = self.length // size if i < n else self.shares[k][1] / 2
+        if axis == "rows":
+            return 1.5 + share * 0.008
+        links = {2: 2, 4: 8}.get(size, 16)
+        return LATENCY + links * share * PER_TILE
+
+    def step(self, i):
+        n = len(self.order)
+        self.wait()
+        if self.done < i <= n:
+            self.add(i - 1)
+        if i < n:
+            self.scatter(i)
+        elif i < 2 * n:
+            if i == n:
+                self.round()
+            self.gather(2 * n - 1 - i)
+
+
+def wave_scratch(order, tiles, first=0, last=None):
+    last = len(order) if last is None else last
+    slots, sems, length = [], [], tiles
+    for k, (_, _, size) in enumerate(order):
+        length //= size
+        used = first <= k < last
+        slots.append(pltpu.VMEM((size - 1, length if used else 1, SUB, LANE), f32))
+        sems += [pltpu.SemaphoreType.DMA((size - 1,))] * 4
+    return slots + sems
+
+
+def wave_refs(order):
+    return 5 * len(order)
+
+
+LATENCY, PER_TILE = 3.0, 0.065
+EARLY = 2
+
+
+def early_tiles(order, tiles):
+    return tiles // math.prod(size for _, _, size in order[:EARLY])
 
 
 def hidden_kernel(
-    stages, xa, ca, bn, meta, count, sums2, scales, shifts, hshift, w_e, w_rt, kh,
+    stages, plan, xa, ca, bn, meta, count, sums2, scales, shifts, hshift, w_e, w_rt, kh,
     nat_o, gn_o, tiles_o, sums_o,
     cm, khb, kfb, n2, gr, ha, ge, em, gc, kacc, wet, wr, res, nat, gn_s, tiles, sem, mine, *rest,
 ):
     found = stage_peers(stages)
     say_here(found)
+    tail, waves = list(rest[3 * len(stages) :]), []
+    for k, (order, count_tiles) in enumerate(plan[:2]):
+        refs, tail = tail[: wave_refs(order)], tail[wave_refs(order) :]
+        waves.append(Wave(order, count_tiles, refs, tiles, base=k * count_tiles))
     rows, px, channels = xa.shape
     columns = px // SUB
     hidden = w_e.shape[1]
@@ -494,8 +669,9 @@
         for g in range(groups):
             part = grad[:, g * LANE : (g + 1) * LANE].reshape(blocks, SUB, LANE)
             tiles[pl.ds(k * blocks * groups + g, blocks, stride=groups)] = part
-    copies = [pltpu.make_async_copy(tiles, tiles_o, sem.at[0])]
-    copies[0].start()
+    wait_all_here(found)
+    for wave in waves:
+        wave.step(0)
 
     step = 3
 
@@ -520,17 +696,25 @@
             sums[2] = sums[2] + fold(out * reduced)
         return tuple(sums)
 
-    sums = lax.fori_loop(0, rows // step, finish, (zero, zero, zero))
-    copies.append(pltpu.make_async_copy(gn_s, gn_o, sem.at[1]))
+    sums = lax.fori_loop(0, 2, finish, (zero, zero, zero))
+    for wave in waves:
+        wave.step(1)
+    sums = lax.fori_loop(2, rows // step, finish, sums)
+    copies = [pltpu.make_async_copy(gn_s, gn_o, sem.at[1])]
     copies[-1].start()
     for k, value in enumerate((sums[0], sums[1], grad_sum, sums[2])):
         mine[k : k + 1, :] = jnp.sum(value, axis=0, keepdims=True)
-    wait_all_here(found)
     unalign(res, meta, nat)
     copies.append(pltpu.make_async_copy(nat, nat_o, sem.at[2]))
     copies[-1].start()
-    all_sum(mine, rest[: len(stages)], rest[len(stages) :], found)
+    all_sum(stages, mine, rest)
     sums_o[...] = mine[...]
+    for k, wave in enumerate(waves):
+        wave.add(EARLY - 1)
+        at = pl.ds(wave.at(wave.start), wave.length)
+        here = pl.ds(k * wave.length, wave.length)
+        copies.append(pltpu.make_async_copy(tiles.at[at], tiles_o.at[here], sem.at[k and 3]))
+        copies[-1].start()
     for copy in copies:
         copy.wait()
 
@@ -541,20 +725,25 @@
     return tap_tile, tap_tile + 2 * groups, tap_tile + 3 * groups
 
 
-def hidden_block(stages, tiles, band, xa, ca, bn, meta, count, sums2, scales, shifts, hshift, w_e, w_rt, kh):
+def hidden_block(stages, plan, band, xa, ca, bn, meta, count, sums2, scales, shifts, hshift, w_e, w_rt, kh):
     rows, px, channels = xa.shape
     columns = px // SUB
     hidden = w_e.shape[1]
     groups = hidden // LANE
     parts = 2
     shape = jax.ShapeDtypeStruct
+    tiles = sum(count_tiles for _, count_tiles in plan[:2])
+    early = sum(early_tiles(*wave) for wave in plan[:2])
+    waves = []
+    for wave in plan[:2]:
+        waves += wave_scratch(*wave, 0, EARLY)
     return pl.pallas_call(
-        functools.partial(hidden_kernel, stages),
+        functools.partial(hidden_kernel, stages, plan),
         name="hidden_block",
         out_shape=[
             shape((2 * band, columns, SUB, channels), f32),
             shape((rows, px, channels), f32),
-            shape((tiles, SUB, LANE), f32),
+            shape((early, SUB, LANE), f32),
             shape((4, channels), f32),
         ],
         in_specs=[VMEM] * 12,
@@ -576,117 +765,14 @@
             pltpu.VMEM((2 * band, columns, SUB, channels), f32),
             pltpu.VMEM((rows, px, channels), f32),
             pltpu.VMEM((tiles, SUB, LANE), f32),
-            pltpu.SemaphoreType.DMA((3,)),
+            pltpu.SemaphoreType.DMA((4,)),
         ]
-        + sum_scratch(stages, (4, channels)),
+        + sum_scratch(stages, (4, channels))
+        + waves,
         compiler_params=pltpu.CompilerParams(
-            collective_id=3, has_side_effects=True, vmem_limit_bytes=60 * MIB
+            collective_id=3, has_side_effects=True, vmem_limit_bytes=63 * MIB
         ),
     )(xa, ca, bn, meta, count, sums2, scales, shifts, hshift, w_e, w_rt, kh)
-
-
-class Wave:
-    def __init__(self, order, buf, full, pair_base, slots, sems, staging, sem):
-        self.order, self.found = order, stage_peers(order)
-        self.buf, self.full, self.pair_base = buf, full, pair_base
-        self.slots, self.sems, self.staging, self.sem = slots, sems, staging, sem
-        self.start, self.length = 0, buf.shape[0]
-        self.shares, self.copies = [], []
-
-    @property
-    def steps(self):
-        return 2 * len(self.order) + 1
-
-    def wait(self):
-        for copy in self.copies:
-            copy.wait()
-        self.copies = []
-
-    def add(self, k):
-        place, peers = self.found[k]
-        share = self.length // self.order[k][2]
-        self.start, self.length = self.start + place * share, share
-        self.shares.append((self.start, self.length))
-        size = math.gcd(share, 16)
-        start, buf, slot, count = self.start, self.buf, self.slots[k], len(peers)
-
-        def some(t, _):
-            at = pl.ds(start + t * size, size)
-            total = buf[at]
-            for i in range(count):
-                total = total + slot[i, pl.ds(t * size, size)]
-            buf[at] = total
-            return 0
-
-        lax.fori_loop(0, share // size, some, 0)
-
-    def scatter(self, k):
-        share = self.length // self.order[k][2]
-        send, recv = self.sems[4 * k : 4 * k + 2]
-        for step, other, device in self.found[k][1]:
-            src = self.buf.at[pl.ds(self.start + other * share, share)]
-            at = step - 1
-            self.copies.append(remote(src, self.slots[k].at[at], send.at[at], recv.at[at], device))
-            self.copies[-1].start()
-
-    def round(self):
-        start, buf, staging = self.start, self.buf, self.staging
-        pairs = self.length // 2
-
-        def one(p, _):
-            both = jnp.concatenate([buf[start + 2 * p], buf[start + 2 * p + 1]], axis=0)
-            staging[p] = both.astype(bf16)
-            return 0
-
-        lax.fori_loop(0, pairs, one, 0)
-        copy = pltpu.make_async_copy(staging, self.part(len(self.order) - 1), self.sem.at[0])
-        copy.start()
-        copy.wait()
-
-    def part(self, k):
-        start, length = self.shares[k]
-        return self.full.at[pl.ds(self.pair_base + start // 2, length // 2)]
-
-    def gather(self, k):
-        send, recv = self.sems[4 * k + 2 : 4 * k + 4]
-        here = self.part(k)
-        for step, _, device in self.found[k][1]:
-            at = step - 1
-            self.copies.append(remote(here, here, send.at[at], recv.at[at], device))
-            self.copies[-1].start()
-
-    def step(self, i):
-        n = len(self.order)
-        if i > 0:
-            self.wait()
-        if 1 <= i <= n:
-            self.add(i - 1)
-        if i < n:
-            self.scatter(i)
-        elif i < 2 * n:
-            if i == n:
-                self.round()
-            self.gather(2 * n - 1 - i)
-
-
-def wave_scratch(order, tiles):
-    slots, sems, length = [], [], tiles
-    for _, _, size in order:
-        length //= size
-        slots.append(pltpu.VMEM((size - 1, length, SUB, LANE), f32))
-        sems += [pltpu.SemaphoreType.DMA((size - 1,))] * 4
-    own = [
-        pltpu.VMEM((tiles, SUB, LANE), f32),
-        pltpu.VMEM((length // 2, 2 * SUB, LANE), bf16),
-        pltpu.SemaphoreType.DMA((1,)),
-    ]
-    return own + slots + sems
-
-
-def make_wave(order, full, pair_base, refs):
-    buf, staging, sem, *rest = refs[: 3 + 5 * len(order)]
-    slots, sems = rest[: len(order)], rest[len(order) :]
-    return Wave(order, buf, full, pair_base, slots, sems, staging, sem), refs[3 + 5 * len(order) :]
 
 
 def wave_plan(sizes, channels, hidden):
@@ -696,7 +782,7 @@
     rest = ("imgs", side * side, chips // (side * side))
     first = ("rows", 1, sizes["rows"])
     first_order, second_order = [first, one, two, rest], [first, two, one, rest]
-    short_order = [first, ("imgs", 1, side * side), rest]
+    short_order = [first, ("imgs", 1, chips)]
     step = 2 * sizes["rows"] * chips
     square = channels // SUB * pl.cdiv(channels, LANE)
     small = pl.cdiv(25, SUB) + pl.cdiv(49, SUB)
@@ -710,14 +796,14 @@
 
 
 def back_kernel(
-    stages, plan, gn, bn_i, xa_i, ca_i, gl_i, sl_i, c1_i, c2_i, gp, tiles_i, nat_i,
+    reach, stages, plan, gn, bn_i, xa_i, ca_i, gl_i, sl_i, c1_i, c2_i, gp, tiles_i, nat_i,
     meta, count, sums1, sums2, sums3, scales, shifts, w_in, w_gate, w_out, kl, kd,
-    mixq_o, resq_o, full_o, sums_o,
-    cm, klb, kdb, gm, tt, sl, xa, ca, gl, c1, c2, gb, gg, gt, g2, g1, src, gw,
+    mixo_o, mixq_o, resq_o, full_o, sums_o,
+    cm, klb, kdb, gm, tt, sl, xa, ca, gl, c1, c2, gb, gg, gt, g2, g1, src, gw, full,
     in_sem, move_sem, mine, *rest,
 ):
     found = stage_peers(stages)
-    say_here(found)
+    say_here(stage_peers(reach))
     rows, px, channels = xa.shape
     columns = px // SUB
     groups = groups_of(channels)
@@ -736,15 +822,16 @@
             loads[p].append(pltpu.make_async_copy(a.at[at], b.at[at], in_sem.at[p, k]))
             loads[p][-1].start()
     tail, waves, pair_base = list(rest[len(stages) * 3 :]), [], 0
-    for order, tiles in plan:
-        wave, tail = make_wave(order, full_o, pair_base, tail)
-        waves.append(wave)
+    for k, (order, tiles) in enumerate(plan):
+        (buf, *refs), tail = tail[: 1 + wave_refs(order)], tail[1 + wave_refs(order) :]
+        early = EARLY if k < 2 else 0
+        waves.append(Wave(order, tiles, refs, buf, 0, full, pair_base, early))
         pair_base += tiles // 2
     late = [
         pltpu.make_async_copy(c2_i, c2, in_sem.at[0, 7]),
         pltpu.make_async_copy(sl_i, sl, in_sem.at[1, 7]),
     ]
-    half = plan[0][1]
+    half = early_tiles(*plan[0])
     tile_loads = [
         pltpu.make_async_copy(tiles_i.at[pl.ds(k * half, half)], waves[k].buf, in_sem.at[k, 8])
         for k in range(2)
@@ -765,32 +852,33 @@
     back1 = b8(sums3, 1) / total
     zero = jnp.zeros((SUB, channels), f32)
 
-    def to_rows(v, out, first_sem):
-        images = pl.ds(pl.multiple_of(core * SUB, SUB), SUB)
-        there = remote(
-            v.at[pl.ds((1 - core) * band, band)], out.at[:, :, images, :],
+    def to_other(v, out, first_sem):
+        return remote(
+            v.at[pl.ds((1 - core) * band, band)], out,
             move_sem.at[first_sem], move_sem.at[first_sem + 1], (1 - core, chip),
         )
-        here = pltpu.make_async_copy(
-            v.at[pl.ds(core * band, band)], out.at[:, :, images, :], move_sem.at[first_sem + 2]
-        )
-        return [there, here]
-
-    wait_all_here(found)
-    moves = to_rows(nat_i, resq_o, 0)
-    for copy in moves:
-        copy.start()
+
+    all_found = stage_peers(reach)
+    wait_all_here(all_found)
     for copy in tile_loads:
         copy.wait()
-    done = [0, 0, 0, 0]
-
-    def advance(*which):
-        for w in which:
-            if done[w] < waves[w].steps:
-                waves[w].step(done[w])
-                done[w] += 1
-
-    advance(0, 1)
+    done, ready, clock = [EARLY, EARLY, 0, 0], [0.0, 0.0, None, None], [0.0]
+
+    def take(w):
+        wave = waves[w]
+        wave.step(done[w])
+        ready[w] = clock[0] + wave.guess(done[w])
+        done[w] += 1
+
+    def stop(spent):
+        clock[0] += spent
+        for w, wave in enumerate(waves):
+            if ready[w] is not None and done[w] < wave.steps and ready[w] <= clock[0]:
+                take(w)
+
+    stop(0.0)
+    moves = [to_other(nat_i, resq_o, 0)]
+    moves[0].start()
 
     def first(b, sums):
         sums = list(sums)
@@ -839,8 +927,7 @@
         for copy in loads[p]:
             copy.wait()
         sums = lax.fori_loop(2 * p, 2 * p + 2, first, sums)
-        if p == 1:
-            advance(0, 1)
+        stop(3.0)
     for k in range(4):
         mine[2 + k : 3 + k, :] = jnp.sum(sums[k], axis=0, keepdims=True)
     whole = rows * px
@@ -866,7 +953,8 @@
     for copy in late:
         copy.wait()
     square(c2, gg, waves[2], blocks * n)
-    advance(2)
+    ready[2] = 0.0
+    stop(1.7)
 
     def put_tap(tap, g, acc, base):
         row = jnp.sum(acc, axis=0, keepdims=True)
@@ -889,10 +977,8 @@
             acc = lax.fori_loop(first_row, last_row, taps_row, zeros_list(7))
             for j in range(7):
                 put_tap(7 * i + j, g, acc[j], far_base)
-        if g == 1:
-            advance(0, 1, 2)
-
-    advance(0, 1)
+            stop(0.39)
+
 
     def dilated(r, sums):
         mask = row_mask(meta, cm, r)
@@ -912,13 +998,13 @@
         return tuple(out)
 
     start = tuple(jnp.zeros((SUB, width), f32) for g, width in groups)
-    sums = lax.fori_loop(0, rows // 2, dilated, start)
-    advance(2)
-    sums = lax.fori_loop(rows // 2, rows, dilated, sums)
+    sums = start
+    for p in range(parts * 2):
+        sums = lax.fori_loop(p * (step // 2), (p + 1) * (step // 2), dilated, sums)
+        stop(1.5)
     for g, width in groups:
         at = slice(g * LANE, g * LANE + width)
         mine[6:7, at] = jnp.sum(sums[g], axis=0, keepdims=True)
-    advance(0, 1, 2)
 
     def refill(r, _):
         for g, width in groups:
@@ -938,7 +1024,7 @@
             acc = lax.fori_loop(0, rows, taps_row, zeros_list(5))
             for j in range(5):
                 put_tap(24 - (5 * i + j), g, acc[j], near_base)
-        advance(0, 1, 2)
+            stop(0.48)
 
     def local(r, sums):
         mask = row_mask(meta, cm, r)
@@ -958,14 +1044,15 @@
         return tuple(out)
 
     sums = start
-    for p in range(2):
-        sums = lax.fori_loop(p * (rows // 2), (p + 1) * (rows // 2), local, sums)
-        advance(0, 1, 2)
+    for p in range(parts * 2):
+        sums = lax.fori_loop(p * (step // 2), (p + 1) * (step // 2), local, sums)
+        stop(1.25)
     for g, width in groups:
         at = slice(g * LANE, g * LANE + width)
         mine[7:8, at] = jnp.sum(sums[g], axis=0, keepdims=True)
     square(gb, gg, waves[3], 0)
-    advance(3)
+    ready[3] = 0.0
+    stop(1.0)
 
     def last(b, sums):
         sums = list(sums)
@@ -982,23 +1069,41 @@
             sums[1] = sums[1] + fold(gn1 * hat)
         return tuple(sums)
 
-    sums = lax.fori_loop(0, 2 * parts, last, (zero, zero))
+    sums = (zero, zero)
+    for p in range(parts * 2):
+        sums = lax.fori_loop(p, p + 1, last, sums)
+        stop(0.8)
     for k in range(2):
         mine[k : k + 1, :] = jnp.sum(sums[k], axis=0, keepdims=True)
-    advance(3)
-    unalign(gm, meta, gw)
-    moves += to_rows(gw, mixq_o, 3)
-    for copy in moves[2:]:
-        copy.start()
-    all_sum(mine, rest[: len(stages)], rest[len(stages) : len(stages) * 3], found)
+    total_sum = AllSum(stages, mine, rest)
+    total_sum.start(0)
+    total_sum.end(0)
+    stop(1.3)
+    for k in range(1, len(stages)):
+        total_sum.start(k)
+        if k == 1:
+            unalign(gm, meta, gw)
+            moves.append(to_other(gw, mixq_o, 2))
+            own_rows = gw.at[pl.ds(core * band, band)]
+            moves.append(pltpu.make_async_copy(own_rows, mixo_o, move_sem.at[4]))
+            for copy in moves[1:]:
+                copy.start()
+        total_sum.end(k)
+        stop(3.0)
     sums_o[...] = mine[...]
-    while any(d < w.steps for d, w in zip(done, waves)):
-        advance(0, 1, 2, 3)
+    pair_base = 0
+    for w, (_, tiles) in enumerate(plan):
+        while done[w] < waves[w].steps:
+            take(w)
+        at = pl.ds(pair_base, tiles // 2)
+        moves.append(pltpu.make_async_copy(full.at[at], full_o.at[at], move_sem.at[5 + w]))
+        moves[-1].start()
+        pair_base += tiles // 2
     for copy in moves:
         copy.wait()
 
 
-def mixer_back(stages, plan, band, gn, bn, xa, ca, gl, sl, c1, c2, gp, tiles, nat, meta, count,
+def mixer_back(reach, stages, plan, band, gn, bn, xa, ca, gl, sl, c1, c2, gp, tiles, nat, meta, count,
                sums1, sums2, sums3, scales, shifts, w_in, w_gate, w_out, kl, kd):
     rows, px, channels = xa.shape
     columns = px // SUB
@@ -1007,19 +1112,23 @@
     shape = jax.ShapeDtypeStruct
     pairs = sum(tiles // 2 for _, tiles in plan)
     waves = []
-    for order, tiles_there in plan:
-        waves += wave_scratch(order, tiles_there)
+    for k, (order, count_tiles) in enumerate(plan):
+        early = early_tiles(order, count_tiles) if k < 2 else count_tiles
+        waves.append(pltpu.VMEM((early, SUB, LANE), f32))
+        waves += wave_scratch(order, count_tiles, EARLY if k < 2 else 0)
+    half = shape((band, columns, SUB, channels), f32)
     return pl.pallas_call(
-        functools.partial(back_kernel, stages, plan),
+        functools.partial(back_kernel, reach, stages, plan),
         name="mixer_back",
         out_shape=[
-            shape((band, columns, 2 * SUB, channels), f32),
-            shape((band, columns, 2 * SUB, channels), f32),
+            half,
+            half,
+            half,
             shape((pairs, 2 * SUB, LANE), bf16),
             shape((8, channels), f32),
         ],
         in_specs=[ANY] * 11 + [VMEM] * 12,
-        out_specs=[ANY] * 3 + [VMEM],
+        out_specs=[ANY] * 4 + [VMEM],
         scratch_shapes=[
             pltpu.VMEM((columns, SUB, channels), f32),
             pltpu.VMEM((25, n, SUB, LANE), f32),
@@ -1031,8 +1140,9 @@
             pltpu.VMEM((n, rows + 4, columns, SUB, LANE), f32),
             pltpu.VMEM((n, rows, columns, SUB, LANE), f32),
             pltpu.VMEM((2 * band, columns, SUB, channels), f32),
+            pltpu.VMEM((pairs, 2 * SUB, LANE), bf16),
             pltpu.SemaphoreType.DMA((3, 9)),
-            pltpu.SemaphoreType.DMA((6,)),
+            pltpu.SemaphoreType.DMA((5 + len(plan),)),
         ]
         + sum_scratch(stages, (8, channels))
         + waves,
@@ -1082,19 +1192,45 @@
 
 
 def finish_kernel(
-    bases, x, mixq, resq, meta, count, sums1, sums4, scales, full, in_o, res_o, *rest,
+    bases, x_i, mixo, mixq, nat, resq, meta, count, sums1, sums4, scales, full,
+    in_o, res_o, *rest,
 ):
-    grads, cm = rest[:-1], rest[-1]
-    row = pl.program_id(0)
-    size, top = meta[2], meta[0]
-
-    @pl.when(row == 0)
-    def _():
-        for c in range(cm.shape[0]):
-            cm[c] = (size > c).astype(f32)
-        for ref, base in zip(grads, bases):
-            tiles_out(full, base, ref)
-
+    n = len(bases)
+    grads, (x, mix, res, cm), grad_s = rest[:n], rest[n : n + 4], rest[n + 4 : -3]
+    in_sem, out_sem, grad_sem = rest[-3:]
+    band, columns = x.shape[:2]
+    core = lax.axis_index("rows")
+    mine = pl.ds(pl.multiple_of(core * SUB, SUB), SUB)
+    other = pl.ds(pl.multiple_of((1 - core) * SUB, SUB), SUB)
+
+    def loads(r):
+        pairs = [
+            (x_i.at[r], x.at[r]),
+            (mixo.at[r], mix.at[r, :, mine]),
+            (mixq.at[r], mix.at[r, :, other]),
+            (nat.at[core * band + r], res.at[r, :, mine]),
+            (resq.at[r], res.at[r, :, other]),
+        ]
+        return [pltpu.make_async_copy(a, b, in_sem.at[r, k]) for k, (a, b) in enumerate(pairs)]
+
+    def stores(r):
+        pairs = [(mix.at[r], in_o.at[r]), (res.at[r], res_o.at[r])]
+        return [pltpu.make_async_copy(a, b, out_sem.at[r, k]) for k, (a, b) in enumerate(pairs)]
+
+    def begin(r, _):
+        for copy in loads(r):
+            copy.start()
+        return 0
+
+    lax.fori_loop(0, band, begin, 0)
+    size, top = meta[1], meta[0]
+    for c in range(columns):
+        cm[c] = (size > c).astype(f32)
+    copies = []
+    for k, (ref, base) in enumerate(zip(grad_s, bases)):
+        tiles_out(full, base, ref)
+        copies.append(pltpu.make_async_copy(ref, grads[k], grad_sem.at[k]))
+        copies[-1].start()
     total = count[0:1, 0:1]
     mean = sums1[0:1, :] / total
     rstd = lax.rsqrt(sums1[1:2, :] / total - mean * mean + epsilon)
@@ -1102,65 +1238,54 @@
     back0, back1 = sums4[0:1, :] / total, sums4[1:2, :] / total
     spread = lambda v: jnp.broadcast_to(v, size.shape)
     mean, rstd, scale, back0, back1 = (spread(v) for v in (mean, rstd, scale, back0, back1))
-    at = row.astype(f32)
-    inside = ((at >= top) & (at < top + size)).astype(f32)
-    mask = cm[...] * inside[None]
-    hat = (mask * x[0].astype(f32) - mean) * rstd
-    in_o[0] = mask * (mixq[0] - scale * (back0 + hat * back1))
-    res_o[0] = resq[0]
-
-
-def finish(x, mixq, resq, meta, count, sums1, sums4, scales, full, shapes, bases):
+
+    def row(r, _):
+        for copy in loads(r):
+            copy.wait()
+        at = (r * 1).astype(f32)
+        inside = ((at >= top) & (at < top + size)).astype(f32)
+        mask = cm[...] * inside[None]
+        hat = (mask * x[r].astype(f32) - mean) * rstd
+        mix[r] = mask * (mix[r] - scale * (back0 + hat * back1))
+        for copy in stores(r):
+            copy.start()
+        return 0
+
+    lax.fori_loop(0, band, row, 0)
+
+    def end(r, _):
+        for copy in stores(r):
+            copy.wait()
+        return 0
+
+    lax.fori_loop(0, band, end, 0)
+    for copy in copies:
+        copy.wait()
+
+
+def finish(x, mixo, mixq, nat, resq, meta, count, sums1, sums4, scales, full, shapes, bases):
     band, columns, images, channels = x.shape
-    block = pl.BlockSpec((1, columns, images, channels), lambda r: (r, 0, 0, 0))
     shape = jax.ShapeDtypeStruct
     return pl.pallas_call(
         functools.partial(finish_kernel, bases),
         name="finish",
-        grid=(band,),
+        in_specs=[ANY] * 5 + [VMEM] * 6,
+        out_specs=[ANY] * (2 + len(shapes)),
+        scratch_shapes=[
+            pltpu.VMEM(x.shape, bf16),
+            pltpu.VMEM(x.shape, f32),
+            pltpu.VMEM(x.shape, f32),
+            pltpu.VMEM((columns, images, channels), f32),
+        ]
+        + [pltpu.VMEM(s, f32) for s in shapes]
+        + [
+            pltpu.SemaphoreType.DMA((band, 5)),
+            pltpu.SemaphoreType.DMA((band, 2)),
+            pltpu.SemaphoreType.DMA((len(shapes),)),
+        ],
         out_shape=[shape(x.shape, f32)] * 2 + [shape(s, f32) for s in shapes],
-        in_specs=[block] * 3 + [VMEM] * 6,
-        out_specs=[block] * 2 + [VMEM] * len(shapes),
-        scratch_shapes=[pltpu.VMEM((columns, images, channels), f32)],
-        compiler_params=pltpu.CompilerParams(vmem_limit_bytes=48 * MIB),
-    )(x, mixq, resq, meta, count, sums1, sums4, scales, full)
-
-
-def halves(values, core, half, axis):
-    mine = lax.dynamic_slice_in_dim(values, core * half, half, axis=axis)
-    other = lax.dynamic_slice_in_dim(values, (1 - core) * half, half, axis=axis)
-    return mine, lax.ppermute(other, "rows", [(0, 1), (1, 0)])
-
-
-def first_sums_kernel(x, meta, out, cm):
-    rows, columns, images, channels = x.shape
-    size, top = meta[2], meta[0]
-    for c in range(columns):
-        cm[c] = (size > c).astype(f32)
-
-    def one(r, sums):
-        at = (r * 1).astype(f32)
-        inside = ((at >= top) & (at < top + size)).astype(f32)
-        value = cm[...] * inside[None] * x[r].astype(f32)
-        return sums[0] + fold(value), sums[1] + fold(value * value)
-
-    zero = jnp.zeros((images, channels), f32)
-    sums = lax.fori_loop(0, rows, one, (zero, zero))
-    for k in range(2):
-        out[k] = sums[k][:SUB] + sums[k][SUB:]
-
-
-def first_sums(x, meta):
-    rows, columns, images, channels = x.shape
-    return pl.pallas_call(
-        first_sums_kernel,
-        name="first_sums",
-        out_shape=jax.ShapeDtypeStruct((2, SUB, channels), f32),
-        in_specs=[VMEM] * 2,
-        out_specs=VMEM,
-        scratch_shapes=[pltpu.VMEM((columns, images, channels), f32)],
-        compiler_params=pltpu.CompilerParams(vmem_limit_bytes=32 * MIB),
-    )(x, meta)
+        compiler_params=pltpu.CompilerParams(vmem_limit_bytes=62 * MIB),
+    )(x, mixo, mixq, nat, resq, meta, count, sums1, sums4, scales, full)
 
 
 def on_device(sizes, inputs, cotangent, scales, shifts, hidden_shift, w_inward, w_gating,
@@ -1177,8 +1302,8 @@
     extent = jnp.sum(chosen * image_size[None, :], axis=1)
     top = band - jnp.sum(chosen * band_split[None, :], axis=1)
     start = jnp.clip(top, 0, 2 * band - columns)
-    own_meta = jnp.stack([top - core * band, top, extent]).astype(f32)
-    own_meta = jnp.broadcast_to(own_meta[:, :, None], (3, images, channels))
+    own_meta = jnp.stack([top - core * band, extent]).astype(f32)
+    own_meta = jnp.broadcast_to(own_meta[:, :, None], (2, images, channels))
     meta = jnp.stack([start, top - start, extent]).astype(f32)
     meta = lax.dynamic_slice_in_dim(meta, core * half, half, axis=1)
     meta = jnp.broadcast_to(meta[:, :, None], (3, half, channels))
@@ -1186,28 +1311,19 @@
     x = jnp.transpose(inputs, (1, 2, 0, 3))
     y = jnp.transpose(cotangent, (1, 2, 0, 3))
     stages = stage_list(sizes)
-    sums1 = reduce_all(first_sums(x, own_meta), stages, 1)
-
-    def gather_rows(v):
-        mine, theirs = halves(v, core, half, 2)
-        upper = jnp.where(core == 0, mine, theirs)
-        lower = jnp.where(core == 0, theirs, mine)
-        return jnp.concatenate([upper, lower], axis=0).reshape(2 * band, px, channels)
-
-    xw, cw = gather_rows(x), gather_rows(y)
-    xa, ca, gl, sl, c1, c2, gp, bn, sums2 = mixer_forward(
-        stages, xw, cw, meta, count, sums1, scales, shifts, w_inward, w_gating, w_outward,
+    xa, ca, gl, sl, c1, c2, gp, bn, sums1, sums2 = mixer_forward(
+        stages, x, y, own_meta, meta, count, scales, shifts, w_inward, w_gating, w_outward,
         kernel_local, kernel_dilated,
     )
     hidden = w_expand.shape[1]
     plan = wave_plan(sizes, channels, hidden)
     half_tiles = plan[0][1]
     nat, gn, tiles, sums3 = hidden_block(
-        stages, 2 * half_tiles, band, xa, ca, bn, meta, count, sums2, scales, shifts,
+        stages, plan, band, xa, ca, bn, meta, count, sums2, scales, shifts,
         hidden_shift, w_expand, w_reduce.T, kernel_hidden,
     )
-    mixq, resq, full, sums4 = mixer_back(
-        stages, plan, band, gn, bn, xa, ca, gl, sl, c1, c2, gp, tiles, nat, meta, count,
+    mixo, mixq, resq, full, sums4 = mixer_back(
+        reach_list(sizes), stages, plan, band, gn, bn, xa, ca, gl, sl, c1, c2, gp, tiles, nat, meta, count,
         sums1, sums2, sums3, scales, shifts, w_inward, w_gating, w_outward, kernel_local,
         kernel_dilated,
     )
@@ -1230,7 +1346,7 @@
         (kernel_dilated.shape, far),
     ]
     input_grad, result, gwe, gwr, gk, gh, gwo, gwg, gwi, gkl, gkd = finish(
-        x, mixq, resq, own_meta, count, sums1, sums4, scales, full,
+        x, mixo, mixq, nat, resq, own_meta, count, sums1, sums4, scales, full,
         [t[0] for t in targets], [t[1] for t in targets],
     )
     scales_grad = jnp.stack([sums4[1], sums4[2], sums3[1], sums3[3]])

time: 284 us -> 233 us (0.82)
  Pallas kernels: 259 us -> 225 us
  local copies, waits for them, and re-layouts: 14.4 us -> 2.69 us
  other arithmetic: 8.05 us -> 2.85 us
    pallas_call x5 -> x3, Pallas kernels: 213 us -> 170 us  [the longest x1 79 us: hidden_block(): pl.pallas_call(functools.partial(hidden_kernel, stages, plan), name='hidd...]
    pallas_call x1, Pallas kernels: 45.9 us -> 55.8 us  [mixer_forward(): pl.pallas_call(functools.partial(mixer_kernel, stages), name='mixer_forwa...]
    dynamic_slice x2 -> x0, local copies, waits for them, and re-layouts: 5.01 us -> none  [halves(): other = lax.dynamic_slice_in_dim(values, (1 - core) * half, half, axis=axis)]
    unnamed x22 -> x4, local copies, waits for them, and re-layouts: 4.8 us -> 0.01 us
    reshape x2 -> x0, other arithmetic: 3.7 us -> none  [gather_rows(): jnp.concatenate([upper, lower], axis=0).reshape(2 * band, px, channels)]
    select_n x1 -> x0, other arithmetic: 2.9 us -> none  [gather_rows(): upper = jnp.where(core == 0, mine, theirs)]
  transfers between devices with their start and end apart: 2 -> 0, of which waited for: 0 -> 0; matrix products, arithmetic and copies ran while one was open for 1% -> 0% of each run, Pallas kernels for 5% -> 0%
where the time goes in v4:
time: 233 us; the launch traced here: 232 us
  Pallas kernels  225 us (97%)
  other arithmetic  2.85 us (1%)
  local copies, waits for them, and re-layouts  2.69 us (1%)
    pallas_call x1, Pallas kernels, hidden_block(): pl.pallas_call(functools.partial(hidden_kernel, stages, plan), name='hidd...  79 us
    pallas_call x1, Pallas kernels, mixer_back(): pl.pallas_call(functools.partial(back_kernel, reach, stages, plan), name=...  78.1 us
    pallas_call x1, Pallas kernels, mixer_forward(): pl.pallas_call(functools.partial(mixer_kernel, stages), name='mixer_forwa...  55.8 us
    pallas_call x1, Pallas kernels, finish(): pl.pallas_call(functools.partial(finish_kernel, bases), name='finish', in...  12.5 us

profile of v4, /device:TPU:0, one launch (start us, length us, event | category | flops | bytes accessed | tf_op | source)
XLA Modules:
  0.0 232.4 jit_solution(10617224519774360228)
XLA Ops:
  0.6 1.3 multiply_reduce_fusion
  2.6 0.9 select_reduce_fusion.1
  3.5 0.1 constant_dynamic-slice_fusion
  3.6 0.6 broadcast_in_dim.8.count
  4.2 0.7 broadcast_in_dim.7.meta
  4.9 0.7 broadcast_in_dim.6.own_meta.meta
  5.6 55.8 %mixer_forward.1 = (bf16[18,144,320]{2,1,0:T(8,128)(2,1)}, bf16[18,144,320]{2,1,0:T(8,128)(2,1)}, bf16[18,144,320]{2,1,0:T(8,128)(2,1)}, f32[18,144,320]{2,1,0:T...) custom-call(bf16[11,18,16,320]{3,2,1,0:T(8,128)(2,1)} %bitcast.15, ...), custom_call_target="tpu_custom_call" | custom-call | tf_op jit(solution)/shard_map/mixer_forward/pallas_call | solution.py:383
  61.4 79.0 %hidden_block.1 = (f32[22,18,8,320]{3,2,1,0:T(8,128)}, f32[18,144,320]{2,1,0:T(8,128)}, f32[224,8,128]{2,1,0:T(8,128)}, f32[4,320]{1,0:T(4,128)}) custom-call(bf16[18,144,320]{2,1,0:T(8,128)(2,1)} %get-tuple-element.43.xa.xa_i, bf16[18,144,320]{2,1,0:T(8,128)(2,1)} %get-tuple-element.44.ca.ca_i, f32[18,144,320]{2,1,0:T(8,128)} %get-tuple-element.45.bn, ...), custom_call_target="tpu_custom_call" | custom-call | tf_op jit(solution)/shard_map/hidden_block/pallas_call | solution.py:740
  140.4 78.1 %mixer_back.1 = (f32[11,18,8,320]{3,2,1,0:T(8,128)}, f32[11,18,8,320]{3,2,1,0:T(8,128)}, f32[11,18,8,320]{3,2,1,0:T(8,128)}, bf16[672,16,128]{2,1,0:T(8,128)(2,1)}, f32[8,320]{1,0:T(8,128)}) custom-call(f32[18,144,320]{2,1,0:T(8,128)} %get-tuple-element.47.gn, f32[18,18,8,320]{3,2,1,0:T(8,128)} %bitcast.14, bf16[18,144,320]{2,1,0:T(8,128)(2,1)} %get-tuple-element.43.xa.xa_i, ...), custom_call_target="tpu_custom_call" | custom-call | tf_op jit(solution)/shard_map/mixer_back/pallas_call | solution.py:1120
  218.5 0.0 copy-start
  218.5 0.0 copy-start.1
  218.6 12.5 %finish.1 = (f32[11,18,16,320]{3,2,1,0:T(8,128)}, f32[11,18,16,320]{3,2,1,0:T(8,128)}, f32[320,1280]{1,0:T(8,128)}, f32[320,1280]{1,0:T(8,128)}, f32[9,1280]{1,0...) custom-call(bf16[11,18,16,320]{3,2,1,0:T(8,128)(2,1)} %bitcast.16, ...), custom_call_target="tpu_custom_call" | custom-call | tf_op jit(solution)/shard_map/finish/pallas_call | solution.py:1269
  231.1 0.0 copy-done
  231.1 0.0 copy-done.1
  231.2 0.6 stack.24
  231.8 0.6 pad_maximum_fusion
  (5 shorter events, 0.1 us)
Async XLA Ops:
  218.5 12.6 %copy-start = (f32[8,320]{1,0:T(8,128)S(1)}, f32[8,320]{1,0:T(8,128)}, u32[]{:S(2)}) copy-start(f32[8,320]{1,0:T(8,128)} %get-tuple-element.60.sums4) | copy-start | bytes 30724
  218.5 12.6 %copy-start.1 = (f32[4,320]{1,0:T(4,128)S(1)}, f32[4,320]{1,0:T(4,128)}, u32[]{:S(2)}) copy-start(f32[4,320]{1,0:T(4,128)} %get-tuple-element.56.sums3) | copy-start | bytes 15364

commit v5 on v4

--- a/solution.py
+++ b/solution.py
@@ -211,8 +211,8 @@
 
 
 def mixer_kernel(
-    stages, x_i, y_i, own_meta, meta, count, scales, shifts, w_in, w_gate, w_out, kl, kd,
-    xa_o, ca_o, gl_o, sl_o, c1_o, c2_o, gp_o, bn_o, sums1_o, sums_o,
+    stages, x_i, y_i, sizes, splits, slots, scales, shifts, w_in, w_gate, w_out, kl, kd,
+    xa_o, ca_o, gl_o, sl_o, c1_o, c2_o, gp_o, bn_o, sums1_o, sums_o, own_meta, meta, count,
     cm, klb, kdb, xa, ca, gl, sl, c1, c2, gp, bn, gf, c1f, sem,
     own_cm, xs, ys, xw, cw, move_sem, mine, *rest,
 ):
@@ -225,6 +225,7 @@
     core, chip = lax.axis_index("rows"), lax.axis_index("imgs")
     band = x_i.shape[0]
     upper = core == 0
+    place_images(sizes, splits, slots, core, band, columns, own_meta, meta, count)
     size, top = own_meta[1], own_meta[0]
     for c in range(columns):
         own_cm[c] = (size > c).astype(f32)
@@ -286,22 +287,31 @@
             value = jnp.where(starts[t][None], pixels3(ref[r + t].astype(f32)), value)
         return value
 
-    def first(r, _):
-        mask = row_mask(meta, cm, r)
-        x = mask * aligned(xw, r)
-        xa[r] = pixels2(x).astype(bf16)
-        ca[r] = pixels2(mask * aligned(cw, r)).astype(bf16)
-        normed = pixels2((x - mean) * scale + b8(shifts, 0)).astype(bf16)
-        pre = pixels3(dot(normed, w_in[...])) + b8(shifts, 1)
-        phi_sum, bell = normal_parts(pre)
-        gelu = mask * low(pre * phi_sum)
-        sl[r] = pixels2(phi_sum + pre * bell)
-        gl[r] = pixels2(gelu).astype(bf16)
-        for g, width in groups:
-            gf[g, r + 2, :, :, :width] = gelu[:, :, g * LANE : g * LANE + width]
+    tall_rows = 3
+
+    def first(b, _):
+        parts, masks = [], []
+        for k in range(tall_rows):
+            r = b * tall_rows + k
+            mask = row_mask(meta, cm, r)
+            x = mask * aligned(xw, r)
+            xa[r] = pixels2(x).astype(bf16)
+            ca[r] = pixels2(mask * aligned(cw, r)).astype(bf16)
+            parts.append(pixels2((x - mean) * scale + b8(shifts, 0)).astype(bf16))
+        product = dot(jnp.concatenate(parts, axis=0), w_in[...])
+        for k in range(tall_rows):
+            r = b * tall_rows + k
+            mask = row_mask(meta, cm, r)
+            pre = pixels3(product[k * px : (k + 1) * px]) + b8(shifts, 1)
+            phi_sum, bell = normal_parts(pre)
+            gelu = mask * low(pre * phi_sum)
+            sl[r] = pixels2(phi_sum + pre * bell)
+            gl[r] = pixels2(gelu).astype(bf16)
+            for g, width in groups:
+                gf[g, r + 2, :, :, :width] = gelu[:, :, g * LANE : g * LANE + width]
         return 0
 
-    lax.fori_loop(0, rows, first, 0)
+    lax.fori_loop(0, rows // tall_rows, first, 0)
     early = [(xa, xa_o), (ca, ca_o), (gl, gl_o), (sl, sl_o)]
     copies = [pltpu.make_async_copy(a, b, sem.at[k]) for k, (a, b) in enumerate(early)]
     for copy in copies:
@@ -344,21 +354,32 @@
     copies.append(pltpu.make_async_copy(c2, c2_o, sem.at[5]))
     copies[-1].start()
 
-    def last(r, sums):
-        mask = row_mask(meta, cm, r)
-        gate = dot(c2[r], w_gate[...]) + jnp.broadcast_to(shifts[4:5, :], (px, channels))
-        gp[r] = gate
-        gated = (gl[r].astype(f32) * gate).astype(bf16)
-        branch = dot(gated, w_out[...])
-        x = pixels3(xa[r].astype(f32))
-        normed = low((x - mean) * scale + b8(shifts, 0))
-        both = pixels3(branch) + b8(shifts, 5) + normed
-        bn[r] = pixels2(both)
-        middle = mask * (x + b8(scales, 1) * both)
-        return sums[0] + fold(middle), sums[1] + fold(middle * middle)
+    def last(b, sums):
+        sums = list(sums)
+        tall = c2[pl.ds(b * tall_rows, tall_rows)].reshape(tall_rows * px, channels)
+        gates = dot(tall, w_gate[...])
+        parts = []
+        for k in range(tall_rows):
+            r = b * tall_rows + k
+            gate = pixels3(gates[k * px : (k + 1) * px]) + b8(shifts, 4)
+            gate = pixels2(gate)
+            gp[r] = gate
+            parts.append((gl[r].astype(f32) * gate).astype(bf16))
+        branches = dot(jnp.concatenate(parts, axis=0), w_out[...])
+        for k in range(tall_rows):
+            r = b * tall_rows + k
+            mask = row_mask(meta, cm, r)
+            x = pixels3(xa[r].astype(f32))
+            normed = low((x - mean) * scale + b8(shifts, 0))
+            both = pixels3(branches[k * px : (k + 1) * px]) + b8(shifts, 5) + normed
+            bn[r] = pixels2(both)
+            middle = mask * (x + b8(scales, 1) * both)
+            sums[0] = sums[0] + fold(middle)
+            sums[1] = sums[1] + fold(middle * middle)
+        return tuple(sums)
 
     zero = jnp.zeros((SUB, channels), f32)
-    sums = lax.fori_loop(0, rows, last, (zero, zero))
+    sums = lax.fori_loop(0, rows // tall_rows, last, (zero, zero))
     copies.append(pltpu.make_async_copy(gp, gp_o, sem.at[6]))
     copies[-1].start()
     copies.append(pltpu.make_async_copy(bn, bn_o, sem.at[7]))
@@ -372,7 +393,7 @@
 
 
 def mixer_forward(
-    stages, x, y, own_meta, meta, count, scales, shifts, w_in, w_gate, w_out, kl, kd
+    stages, x, y, sizes, splits, slots, scales, shifts, w_in, w_gate, w_out, kl, kd
 ):
     band, columns, images, channels = x.shape
     px = columns * SUB
@@ -384,9 +405,14 @@
         functools.partial(mixer_kernel, stages),
         name="mixer_forward",
         out_shape=[jax.ShapeDtypeStruct(small, k) for k in kinds]
-        + [jax.ShapeDtypeStruct((2, channels), f32)] * 2,
+        + [jax.ShapeDtypeStruct((2, channels), f32)] * 2
+        + [
+            jax.ShapeDtypeStruct((2, images, channels), f32),
+            jax.ShapeDtypeStruct((3, SUB, channels), f32),
+            jax.ShapeDtypeStruct((SUB, LANE), f32),
+        ],
         in_specs=[VMEM] * 12,
-        out_specs=[ANY] * 8 + [VMEM] * 2,
+        out_specs=[ANY] * 8 + [VMEM] * 5,
         scratch_shapes=[
             pltpu.VMEM((columns, SUB, channels), f32),
             pltpu.VMEM((25, n, SUB, LANE), f32),
@@ -409,7 +435,37 @@
         compiler_params=pltpu.CompilerParams(
             collective_id=2, has_side_effects=True, vmem_limit_bytes=62 * MIB
         ),
-    )(x, y, own_meta, meta, count, scales, shifts, w_in, w_gate, w_out, kl, kd)
+    )(x, y, sizes, splits, slots, scales, shifts, w_in, w_gate, w_out, kl, kd)
+
+
+def place_images(sizes, splits, slots, core, band, columns, own_meta, meta, count):
+    images, channels = own_meta.shape[1:]
+    size = sizes[...].astype(f32)
+    total = jnp.sum(size * size, axis=1, keepdims=True)
+    count[...] = jnp.broadcast_to(total, count.shape)
+    shape = (images, images)
+    rows, cols = (lax.broadcasted_iota(jnp.int32, shape, k) for k in range(2))
+    spread = jnp.broadcast_to(slots[...].astype(f32), shape)
+    column = jnp.sum(jnp.where(rows == cols, spread, 0.0), axis=1, keepdims=True)
+    shape = (images, size.shape[1])
+    image = lax.broadcasted_iota(jnp.int32, shape, 1).astype(f32)
+    chosen = image == jnp.broadcast_to(column, shape)
+
+    def pick(row):
+        value = jnp.where(chosen, jnp.broadcast_to(row, shape), 0.0)
+        value = jnp.sum(value, axis=1, keepdims=True)
+        return jnp.broadcast_to(value, (images, channels))
+
+    extent = pick(size)
+    top = float(band) - pick(splits[...].astype(f32))
+    own_meta[0] = top - (core * band).astype(f32)
+    own_meta[1] = extent
+    half = lambda v: jnp.where(core == 0, v[:SUB], v[SUB:])
+    top, extent = half(top), half(extent)
+    start = jnp.clip(top, 0.0, float(2 * band - columns))
+    meta[0] = start
+    meta[1] = top - start
+    meta[2] = extent
 
 
 class Wave:
@@ -592,8 +648,13 @@
         def expand(b, _):
             tall = n2[pl.ds(b * wide_step, wide_step)].reshape(wide_step * px, channels)
             product = dot(tall, w_e[:, lanes])
+            grads = gr[pl.ds(b * wide_step, wide_step)].reshape(wide_step * px, channels)
+            grads = dot(grads, w_rt[:, lanes])
             for k in range(wide_step):
                 r = b * wide_step + k
+                for g in range(parts):
+                    at = slice(g * LANE, (g + 1) * LANE)
+                    gc[g, r + 1] = pixels3(grads[k * px : (k + 1) * px, at])
                 mask = row_mask(meta, cm, r)[:, :, :LANE]
                 value = product[k * px : (k + 1) * px]
                 value = low(value + jnp.broadcast_to(hshift[0:1, lanes], value.shape))
@@ -604,7 +665,6 @@
         lax.fori_loop(0, rows // wide_step, expand, 0)
 
         def forward(r, acc):
-            grad = dot(gr[r], w_rt[:, lanes])
             out = []
             for g in range(parts):
                 conv = zeros_list(columns)
@@ -615,8 +675,7 @@
                 v = jnp.stack(conv) + jnp.broadcast_to(hshift[1:2, here], (SUB, LANE))
                 phi_sum, bell = normal_parts(v)
                 ha[r, :, here] = pixels2(v * phi_sum).astype(bf16)
-                part = pixels3(grad[:, g * LANE : (g + 1) * LANE])
-                back = low(part * (phi_sum + v * bell))
+                back = low(gc[g, r + 1] * (phi_sum + v * bell))
                 gc[g, r + 1] = back
                 out.append(acc[g] + fold(back))
             return tuple(out)
@@ -791,7 +850,8 @@
         (first_order, half),
         (second_order, half),
         (first_order, pl.cdiv(2 * square, step) * step),
-        (short_order, pl.cdiv(square + small * pl.cdiv(channels, LANE), step) * step),
+        (short_order, pl.cdiv(square, step) * step),
+        (short_order, pl.cdiv(small * pl.cdiv(channels, LANE), step) * step),
     ]
 
 
@@ -799,7 +859,7 @@
     reach, stages, plan, gn, bn_i, xa_i, ca_i, gl_i, sl_i, c1_i, c2_i, gp, tiles_i, nat_i,
     meta, count, sums1, sums2, sums3, scales, shifts, w_in, w_gate, w_out, kl, kd,
     mixo_o, mixq_o, resq_o, full_o, sums_o,
-    cm, klb, kdb, gm, tt, sl, xa, ca, gl, c1, c2, gb, gg, gt, g2, g1, src, gw, full,
+    cm, klb, kdb, gm, tt, sl, xa, ca, gl, c2, gb, gg, gt, g2, g1, src, gw, full,
     in_sem, move_sem, mine, *rest,
 ):
     found = stage_peers(stages)
@@ -812,7 +872,7 @@
     parts = 3
     step = rows // parts
     pairs = [
-        (gn, gm), (bn_i, gw), (xa_i, xa), (ca_i, ca), (gl_i, gl), (gp, tt), (c1_i, c1),
+        (gn, gm), (bn_i, gw), (xa_i, xa), (ca_i, ca), (gl_i, gl), (gp, tt), (c1_i, gg),
     ]
     loads = []
     for p in range(parts):
@@ -862,7 +922,7 @@
     wait_all_here(all_found)
     for copy in tile_loads:
         copy.wait()
-    done, ready, clock = [EARLY, EARLY, 0, 0], [0.0, 0.0, None, None], [0.0]
+    done, ready, clock = [EARLY, EARLY, 0, 0, 0], [0.0, 0.0, None, None, None], [0.0]
 
     def take(w):
         wave = waves[w]
@@ -885,6 +945,9 @@
         gated_parts = []
         for k in range(step // 2):
             r = b * (step // 2) + k
+            for g, width in groups:
+                conv = gg[r, :, g * LANE : g * LANE + width].astype(f32)
+                src[g, r, :, :, :width] = pixels3(conv)
             mask = row_mask(meta, cm, r)
             both = gw[r]
             middle = pixels3(xa[r].astype(f32)) + b8(scales, 1) * both
@@ -918,7 +981,6 @@
             for g, width in groups:
                 at = slice(g * LANE, g * LANE + width)
                 g2[g, r, :, :, :width] = pixels3(conv[:, at])
-                src[g, r, :, :, :width] = pixels3(c1[r, :, at].astype(f32))
             sums[3] = sums[3] + fold(pixels3(conv))
         return tuple(sums)
 
@@ -947,8 +1009,8 @@
 
         lax.fori_loop(0, buf.shape[0], one, 0)
 
-    clear(waves[2].buf)
-    clear(waves[3].buf)
+    for wave in waves[2:]:
+        clear(wave.buf)
     square(gt, gb, waves[2], 0)
     for copy in late:
         copy.wait()
@@ -959,10 +1021,9 @@
     def put_tap(tap, g, acc, base):
         row = jnp.sum(acc, axis=0, keepdims=True)
         at = base + tap // SUB * n + g
-        waves[3].buf[at, tap % SUB : tap % SUB + 1, :] = row
-
-    near_base = blocks * n
-    far_base = near_base + pl.cdiv(kl.shape[0], SUB) * n
+        waves[4].buf[at, tap % SUB : tap % SUB + 1, :] = row
+
+    near_base, far_base = 0, pl.cdiv(kl.shape[0], SUB) * n
     for g, width in groups:
         for i in range(7):
             first_row = max(0, 3 * (3 - i))
@@ -1025,6 +1086,9 @@
             for j in range(5):
                 put_tap(24 - (5 * i + j), g, acc[j], near_base)
             stop(0.48)
+
+    ready[4] = 0.0
+    stop(0.0)
 
     def local(r, sums):
         mask = row_mask(meta, cm, r)
@@ -1134,7 +1198,7 @@
             pltpu.VMEM((25, n, SUB, LANE), f32),
             pltpu.VMEM((49, n, SUB, LANE), f32),
         ]
-        + [pltpu.VMEM(small, k) for k in (f32,) * 3 + (bf16,) * 8]
+        + [pltpu.VMEM(small, k) for k in (f32,) * 3 + (bf16,) * 7]
         + [
             pltpu.VMEM((n, rows, columns, SUB, LANE), f32),
             pltpu.VMEM((n, rows + 4, columns, SUB, LANE), f32),
@@ -1192,9 +1256,15 @@
 
 
 def finish_kernel(
-    bases, x_i, mixo, mixq, nat, resq, meta, count, sums1, sums4, scales, full,
-    in_o, res_o, *rest,
+    bases, x_i, mixo, mixq, nat, resq, meta, count, sums1, sums3, sums4, scales, full,
+    in_o, res_o, sg_o, bg_o, *rest,
 ):
+    for ref, order in (
+        (sg_o, ((sums4, 1), (sums4, 2), (sums3, 1), (sums3, 3))),
+        (bg_o, tuple((sums4, k) for k in (0, 7, 6, 5, 4, 3)) + ((sums3, 0), (sums3, 2))),
+    ):
+        for k, (table, row) in enumerate(order):
+            ref[k : k + 1, :] = table[row : row + 1, :]
     n = len(bases)
     grads, (x, mix, res, cm), grad_s = rest[:n], rest[n : n + 4], rest[n + 4 : -3]
     in_sem, out_sem, grad_sem = rest[-3:]
@@ -1263,14 +1333,16 @@
         copy.wait()
 
 
-def finish(x, mixo, mixq, nat, resq, meta, count, sums1, sums4, scales, full, shapes, bases):
+def finish(
+    x, mixo, mixq, nat, resq, meta, count, sums1, sums3, sums4, scales, full, shapes, bases
+):
     band, columns, images, channels = x.shape
     shape = jax.ShapeDtypeStruct
     return pl.pallas_call(
         functools.partial(finish_kernel, bases),
         name="finish",
-        in_specs=[ANY] * 5 + [VMEM] * 6,
-        out_specs=[ANY] * (2 + len(shapes)),
+        in_specs=[ANY] * 5 + [VMEM] * 7,
+        out_specs=[ANY] * 2 + [VMEM] * 2 + [ANY] * len(shapes),
         scratch_shapes=[
             pltpu.VMEM(x.shape, bf16),
             pltpu.VMEM(x.shape, f32),
@@ -1283,37 +1355,23 @@
             pltpu.SemaphoreType.DMA((band, 2)),
             pltpu.SemaphoreType.DMA((len(shapes),)),
         ],
-        out_shape=[shape(x.shape, f32)] * 2 + [shape(s, f32) for s in shapes],
+        out_shape=[shape(x.shape, f32)] * 2
+        + [shape((k, channels), f32) for k in (4, 8)]
+        + [shape(s, f32) for s in shapes],
         compiler_params=pltpu.CompilerParams(vmem_limit_bytes=62 * MIB),
-    )(x, mixo, mixq, nat, resq, meta, count, sums1, sums4, scales, full)
+    )(x, mixo, mixq, nat, resq, meta, count, sums1, sums3, sums4, scales, full)
 
 
 def on_device(sizes, inputs, cotangent, scales, shifts, hidden_shift, w_inward, w_gating,
               w_outward, w_expand, w_reduce, kernel_local, kernel_dilated, kernel_hidden,
               image_size, band_split, slot_image):
     images, band, columns, channels = inputs.shape
-    half = images // 2
-    px = columns * half
-    core = lax.axis_index("rows")
-    counted = jnp.sum(image_size * image_size).astype(f32)
-    count = jnp.full((SUB, LANE), counted)
-    everyone = jnp.arange(image_size.shape[0], dtype=jnp.int32)
-    chosen = (slot_image[:, None] == everyone[None, :]).astype(jnp.int32)
-    extent = jnp.sum(chosen * image_size[None, :], axis=1)
-    top = band - jnp.sum(chosen * band_split[None, :], axis=1)
-    start = jnp.clip(top, 0, 2 * band - columns)
-    own_meta = jnp.stack([top - core * band, extent]).astype(f32)
-    own_meta = jnp.broadcast_to(own_meta[:, :, None], (2, images, channels))
-    meta = jnp.stack([start, top - start, extent]).astype(f32)
-    meta = lax.dynamic_slice_in_dim(meta, core * half, half, axis=1)
-    meta = jnp.broadcast_to(meta[:, :, None], (3, half, channels))
-
     x = jnp.transpose(inputs, (1, 2, 0, 3))
     y = jnp.transpose(cotangent, (1, 2, 0, 3))
     stages = stage_list(sizes)
-    xa, ca, gl, sl, c1, c2, gp, bn, sums1, sums2 = mixer_forward(
-        stages, x, y, own_meta, meta, count, scales, shifts, w_inward, w_gating, w_outward,
-        kernel_local, kernel_dilated,
+    xa, ca, gl, sl, c1, c2, gp, bn, sums1, sums2, own_meta, meta, count = mixer_forward(
+        stages, x, y, image_size[None], band_split[None], slot_image[None], scales, shifts,
+        w_inward, w_gating, w_outward, kernel_local, kernel_dilated,
     )
     hidden = w_expand.shape[1]
     plan = wave_plan(sizes, channels, hidden)
@@ -1332,7 +1390,7 @@
     tap_tile, bias_tile, _ = hidden_tiles(channels, hidden)
     second = 2 * half_tiles
     third = second + plan[2][1]
-    near = third + blocks * n
+    near = third + plan[3][1]
     far = near + pl.cdiv(kernel_local.shape[0], SUB) * n
     targets = [
         (wide, 0),
@@ -1345,13 +1403,10 @@
         (kernel_local.shape, near),
         (kernel_dilated.shape, far),
     ]
-    input_grad, result, gwe, gwr, gk, gh, gwo, gwg, gwi, gkl, gkd = finish(
-        x, mixo, mixq, nat, resq, own_meta, count, sums1, sums4, scales, full,
+    (input_grad, result, scales_grad, shifts_grad, gwe, gwr, gk, gh, gwo, gwg, gwi, gkl,
+     gkd) = finish(
+        x, mixo, mixq, nat, resq, own_meta, count, sums1, sums3, sums4, scales, full,
         [t[0] for t in targets], [t[1] for t in targets],
-    )
-    scales_grad = jnp.stack([sums4[1], sums4[2], sums3[1], sums3[3]])
-    shifts_grad = jnp.stack(
-        [sums4[0], sums4[7], sums4[6], sums4[5], sums4[4], sums4[3], sums3[0], sums3[2]]
     )
     back = lambda v: jnp.transpose(v, (2, 0, 1, 3))
     return (

time: 233 us -> 220 us (0.944)
  Pallas kernels: 225 us -> 219 us
  other arithmetic: 2.85 us -> 0 us
  local copies, waits for them, and re-layouts: 2.69 us -> 0 us
    pallas_call x1, Pallas kernels: 55.8 us -> 51.5 us  [mixer_forward(): pl.pallas_call(functools.partial(mixer_kernel, stages), name='mixer_forwa...]
    pallas_call x1, Pallas kernels: 79 us -> 76.1 us  [hidden_block(): pl.pallas_call(functools.partial(hidden_kernel, stages, plan), name='hidd...]
where the time goes in v5:
time: 220 us
  Pallas kernels  219 us (100%)
    pallas_call x1, Pallas kernels, mixer_back(): pl.pallas_call(functools.partial(back_kernel, reach, stages, plan), name=...  78.3 us
    pallas_call x1, Pallas kernels, hidden_block(): pl.pallas_call(functools.partial(hidden_kernel, stages, plan), name='hidd...  76.1 us
    pallas_call x1, Pallas kernels, mixer_forward(): pl.pallas_call(functools.partial(mixer_kernel, stages), name='mixer_forwa...  51.5 us
    pallas_call x1, Pallas kernels, finish(): pl.pallas_call(functools.partial(finish_kernel, bases), name='finish', in...  13.2 us

profile of v5, /device:TPU:0, one launch (start us, length us, event | category | flops | bytes accessed | tf_op | source)
XLA Modules:
  0.0 219.9 jit_solution(11990691032621833346)
XLA Ops:
  0.6 51.5 %mixer_forward.1 = (bf16[18,144,320]{2,1,0:T(8,128)(2,1)}, bf16[18,144,320]{2,1,0:T(8,128)(2,1)}, bf16[18,144,320]{2,1,0:T(8,128)(2,1)}, f32[18,144,320]{2,1,0:T...) custom-call(bf16[11,18,16,320]{3,2,1,0:T(8,128)(2,1)} %bitcast.11, ...), custom_call_target="tpu_custom_call" | custom-call | tf_op jit(solution)/shard_map/mixer_forward/pallas_call | solution.py:404
  52.2 76.1 %hidden_block.1 = (f32[22,18,8,320]{3,2,1,0:T(8,128)}, f32[18,144,320]{2,1,0:T(8,128)}, f32[224,8,128]{2,1,0:T(8,128)}, f32[4,320]{1,0:T(4,128)}) custom-call(bf16[18,144,320]{2,1,0:T(8,128)(2,1)} %get-tuple-element.48.xa.xa_i, bf16[18,144,320]{2,1,0:T(8,128)(2,1)} %get-tuple-element.49.ca.ca_i, f32[18,144,320]{2,1,0:T(8,128)} %get-tuple-element.50.bn, ...), custom_call_target="tpu_custom_call" | custom-call | tf_op jit(solution)/shard_map/hidden_block/pallas_call | solution.py:799
  128.2 78.3 %mixer_back.1 = (f32[11,18,8,320]{3,2,1,0:T(8,128)}, f32[11,18,8,320]{3,2,1,0:T(8,128)}, f32[11,18,8,320]{3,2,1,0:T(8,128)}, bf16[672,16,128]{2,1,0:T(8,128)(2,1)}, f32[8,320]{1,0:T(8,128)}) custom-call(f32[18,144,320]{2,1,0:T(8,128)} %get-tuple-element.54.gn, f32[18,18,8,320]{3,2,1,0:T(8,128)} %bitcast.10, bf16[18,144,320]{2,1,0:T(8,128)(2,1)} %get-tuple-element.48.xa.xa_i, ...), custom_call_target="tpu_custom_call" | custom-call | tf_op jit(solution)/shard_map/mixer_back/pallas_call | solution.py:1184
  206.6 13.2 %finish.1 = (f32[11,18,16,320]{3,2,1,0:T(8,128)}, f32[11,18,16,320]{3,2,1,0:T(8,128)}, f32[4,320]{1,0:T(4,128)}, f32[8,320]{1,0:T(8,128)}, f32[320,1280]{1,0:T(8...) custom-call(bf16[11,18,16,320]{3,2,1,0:T(8,128)(2,1)} %bitcast.12, ...), custom_call_target="tpu_custom_call" | custom-call | tf_op jit(solution)/shard_map/finish/pallas_call | solution.py:1341

commit v6 on v5

--- a/solution.py
+++ b/solution.py
@@ -287,7 +287,7 @@
             value = jnp.where(starts[t][None], pixels3(ref[r + t].astype(f32)), value)
         return value
 
-    tall_rows = 3
+    tall_rows = 6
 
     def first(b, _):
         parts, masks = [], []
@@ -586,7 +586,7 @@
     return 5 * len(order)
 
 
-LATENCY, PER_TILE = 3.0, 0.065
+LATENCY, PER_TILE = 2.5, 0.055
 EARLY = 2
 
 
@@ -610,7 +610,7 @@
     hidden = w_e.shape[1]
     wide = em.shape[0] * LANE
     parts = em.shape[0]
-    wide_step = 6
+    wide_step = 9
     groups = hidden // LANE
     tap_tile, bias_tile, last_tile = hidden_tiles(channels, hidden)
     for t in range(tap_tile, last_tile):

time: 220 us -> 215 us (0.977)
  Pallas kernels: 219 us -> 214 us
    pallas_call x1, Pallas kernels: 78.3 us -> 75.1 us  [mixer_back(): pl.pallas_call(functools.partial(back_kernel, reach, stages, plan), name=...]
where the time goes in v6:
time: 215 us
  Pallas kernels  214 us (100%)
    pallas_call x1, Pallas kernels, hidden_block(): pl.pallas_call(functools.partial(hidden_kernel, stages, plan), name='hidd...  75.3 us
    pallas_call x1, Pallas kernels, mixer_back(): pl.pallas_call(functools.partial(back_kernel, reach, stages, plan), name=...  75.1 us
    pallas_call x1, Pallas kernels, mixer_forward(): pl.pallas_call(functools.partial(mixer_kernel, stages), name='mixer_forwa...  50.7 us
    pallas_call x1, Pallas kernels, finish(): pl.pallas_call(functools.partial(finish_kernel, bases), name='finish', in...  13.2 us

profile of v6, /device:TPU:0, one launch (start us, length us, event | category | flops | bytes accessed | tf_op | source)
XLA Modules:
  0.0 215.2 jit_solution(10375985001369292937)
XLA Ops:
  0.6 50.7 %mixer_forward.1 = (bf16[18,144,320]{2,1,0:T(8,128)(2,1)}, bf16[18,144,320]{2,1,0:T(8,128)(2,1)}, bf16[18,144,320]{2,1,0:T(8,128)(2,1)}, f32[18,144,320]{2,1,0:T...) custom-call(bf16[11,18,16,320]{3,2,1,0:T(8,128)(2,1)} %bitcast.11, ...), custom_call_target="tpu_custom_call" | custom-call | tf_op jit(solution)/shard_map/mixer_forward/pallas_call | solution.py:404
  51.4 75.3 %hidden_block.1 = (f32[22,18,8,320]{3,2,1,0:T(8,128)}, f32[18,144,320]{2,1,0:T(8,128)}, f32[224,8,128]{2,1,0:T(8,128)}, f32[4,320]{1,0:T(4,128)}) custom-call(bf16[18,144,320]{2,1,0:T(8,128)(2,1)} %get-tuple-element.48.xa.xa_i, bf16[18,144,320]{2,1,0:T(8,128)(2,1)} %get-tuple-element.49.ca.ca_i, f32[18,144,320]{2,1,0:T(8,128)} %get-tuple-element.50.bn, ...), custom_call_target="tpu_custom_call" | custom-call | tf_op jit(solution)/shard_map/hidden_block/pallas_call | solution.py:799
  126.7 75.1 %mixer_back.1 = (f32[11,18,8,320]{3,2,1,0:T(8,128)}, f32[11,18,8,320]{3,2,1,0:T(8,128)}, f32[11,18,8,320]{3,2,1,0:T(8,128)}, bf16[672,16,128]{2,1,0:T(8,128)(2,1)}, f32[8,320]{1,0:T(8,128)}) custom-call(f32[18,144,320]{2,1,0:T(8,128)} %get-tuple-element.54.gn, f32[18,18,8,320]{3,2,1,0:T(8,128)} %bitcast.10, bf16[18,144,320]{2,1,0:T(8,128)(2,1)} %get-tuple-element.48.xa.xa_i, ...), custom_call_target="tpu_custom_call" | custom-call | tf_op jit(solution)/shard_map/mixer_back/pallas_call | solution.py:1184
  201.9 13.2 %finish.1 = (f32[11,18,16,320]{3,2,1,0:T(8,128)}, f32[11,18,16,320]{3,2,1,0:T(8,128)}, f32[4,320]{1,0:T(4,128)}, f32[8,320]{1,0:T(8,128)}, f32[320,1280]{1,0:T(8...) custom-call(bf16[11,18,16,320]{3,2,1,0:T(8,128)(2,1)} %bitcast.12, ...), custom_call_target="tpu_custom_call" | custom-call | tf_op jit(solution)/shard_map/finish/pallas_call | solution.py:1341
